TPU v7x, 32 devices: a whole 2x2x4 slice. The times are simulated.
32 devices in a mesh: row: 8 (over z, y), col: 4 (over x, core).
Axes of the slice: x: 2, y: 2, z: 4, core: 2. Of those that a mesh axis runs over, the one named last changes fastest.
Arguments:
- lesser: bfloat16 [4096, 4096], P('row', 'col'), may hold values from -6 to 6
- greater: bfloat16 [4096, 4096], P('row', 'col'), may hold values from -6 to 6
- screened_lesser: bfloat16 [4096, 4096], P('row', 'col'), may hold values from -6 to 6
- screened_greater: bfloat16 [4096, 4096], P('row', 'col'), may hold values from -6 to 6
Outputs:
- collision: float32 [4096, 1024], P('row', 'col')
All inputs are finite; a program needn't handle non-finite values.
Results may differ from a plain program's by a relative error of at most 0.0051.
Values may be sent and summed in bfloat16 or wider, within the bound.
No kernel may reach another device: no remote copies, remote signals or barrier semaphores. Data moves between devices by JAX's collectives and lax.ppermute only.
A program may use at most 64 MiB of HBM per device.

v0:
```python
import jax
import jax.numpy as jnp
from jax import lax
from jax.sharding import PartitionSpec as P

WINDOW = 256


def carried_in(part, axis, combine, identity):
    place = lax.axis_index(axis)
    gathered = lax.all_gather(part, axis)
    state = jnp.zeros_like(part) + jnp.asarray(identity, part.dtype)

    def one(hop, state):
        return combine(state, lax.dynamic_index_in_dim(gathered, hop, 0, False))

    return lax.fori_loop(0, place, one, state)


def add_terms(first, second):
    return first + second


def local(lesser, greater, screened_lesser, screened_greater):
    row_count, tile_width = lesser.shape
    row_devices = lax.axis_size("row")
    col_devices = lax.axis_size("col")
    ratio = row_devices // col_devices
    my_row = lax.axis_index("row")
    my_col = lax.axis_index("col")
    scale = float(tile_width * col_devices) ** (-0.5)
    green_part = lesser.reshape(row_count, ratio, row_count)[:, :, :WINDOW]
    great_part = greater.reshape(row_count, ratio, row_count)[:, :, :WINDOW]
    diff_part = (green_part.astype(jnp.float32) - great_part.astype(jnp.float32)).astype(
        jnp.bfloat16
    )
    piece_rows = row_count // col_devices
    first_green = green_part.reshape(col_devices, piece_rows, ratio, WINDOW)
    first_diff = diff_part.reshape(col_devices, piece_rows, ratio, WINDOW)
    spread = (
        lax.all_to_all(first_green, "col", split_axis=0, concat_axis=0, tiled=True),
        lax.all_to_all(first_diff, "col", split_axis=0, concat_axis=0, tiled=True),
    )

    def to_rows(block):
        return jnp.transpose(block, (0, 2, 1, 3)).reshape(1, row_devices, piece_rows, WINDOW)

    crossed = (
        lax.all_to_all(to_rows(spread[0]), "row", split_axis=1, concat_axis=0, tiled=True),
        lax.all_to_all(to_rows(spread[1]), "row", split_axis=1, concat_axis=0, tiled=True),
    )

    def to_cols(block):
        shaped = block.reshape(col_devices, ratio, piece_rows, WINDOW)
        return jnp.transpose(shaped, (1, 0, 2, 3))

    settled = (
        lax.all_to_all(to_cols(crossed[0]), "col", split_axis=1, concat_axis=1, tiled=True),
        lax.all_to_all(to_cols(crossed[1]), "col", split_axis=1, concat_axis=1, tiled=True),
    )
    green_win = settled[0].reshape(tile_width, WINDOW)
    diff_win = settled[1].reshape(tile_width, WINDOW)
    inner_times = my_col * tile_width + jnp.arange(tile_width, dtype=jnp.int32)
    window_times = my_row * row_count + jnp.arange(WINDOW, dtype=jnp.int32)
    diff_win = jnp.where(
        inner_times[:, None] <= window_times[None, :], diff_win, jnp.zeros((), jnp.bfloat16)
    )
    later_times = my_row * row_count + jnp.arange(row_count, dtype=jnp.int32)
    prod_less = lesser.astype(jnp.float32) * screened_lesser.astype(jnp.float32)
    prod_great = greater.astype(jnp.float32) * screened_greater.astype(jnp.float32)
    sigma_less = prod_less.astype(jnp.bfloat16)
    sigma_ret = jnp.where(
        inner_times[None, :] <= later_times[:, None], prod_great - prod_less, 0.0
    ).astype(jnp.bfloat16)
    partial_value = jnp.dot(sigma_ret, green_win, preferred_element_type=jnp.float32)
    partial_value = partial_value + jnp.dot(
        sigma_less, diff_win, preferred_element_type=jnp.float32
    )
    partial_value = scale * partial_value
    earlier = carried_in(partial_value, "col", add_terms, jnp.zeros_like(partial_value))
    collision = earlier + partial_value
    return collision


def solution(mesh):
    in_specs = (P("row", "col"), P("row", "col"), P("row", "col"), P("row", "col"))
    out_specs = P("row", "col")
    return jax.shard_map(local, mesh=mesh, in_specs=in_specs, out_specs=out_specs, check_vma=False)
```

profile of v0, /device:TPU:25, one launch (start us, length us, event | category | flops | bytes accessed | tf_op | source)
XLA Modules:
  0.0 128.2 jit_solution(14093841531271326696)
XLA Ops:
  6.5 0.0 copy-start.2
  6.5 1.6 %copy.23 = bf16[512,1024]{0,1:T(8,128)(2,1)S(1)} copy(bf16[512,1024]{1,0:T(8,128)(2,1)} %param.7) | data formatting | bytes 2097152 | tf_op args[1]
  8.1 0.0 copy-done.2
  8.1 0.5 copy.18
  8.7 0.1 subtract_convert_fusion
  8.8 0.2 copy.24
  9.0 0.8 copy.25
  9.9 4.1 %all-to-all-start.3 = ((bf16[4,128,2,256]{3,1,2,0:T(8,128)(2,1)}), bf16[4,128,2,256]{3,1,2,0:T(8,128)(2,1)S(1)}, u32[]{:S(2)}, u32[]{:S(2)}) async-start(bf16[4,128,2,256]{3,1,2,0:T(8,128)(2,1)} %copy.25), calls=%async_computation.3 | async-start | bytes 1048576 | tf_op jit(solution)/shard_map/all_to_all | solution.py:42
  14.0 0.2 copy.19
  14.3 7.7 %all-to-all-done.3 = bf16[4,128,2,256]{3,1,2,0:T(8,128)(2,1)S(1)} async-done(((bf16[4,128,2,256]{3,1,2,0:T(8,128)(2,1)}), bf16[4,128,2,256]{3,1,2,0:T(8,128)(2,1)S(1)}, u32[]{:S(2)}, u32[]{:S(2)}) %all-to-all-start.3) | async-done | bytes 524320 | tf_op jit(solution)/shard_map/all_to_all | solution.py:42
  22.0 11.1 %all_to_all.38 = bf16[4,128,2,256]{3,1,2,0:T(8,128)(2,1)S(1)} all-to-all(bf16[4,128,2,256]{3,1,2,0:T(8,128)(2,1)S(1)} %copy.20), channel_id=1, replica_groups=mesh['row'=8,'col'=4] {'col'}, dimensions={0} | all-to-all | bytes 1048576 | tf_op jit(solution)/shard_map/all_to_all | solution.py:41
  33.0 17.3 %all_to_all.39 = bf16[1,8,128,256]{3,2,0,1:T(8,128)(2,1)} all-to-all(bf16[1,8,128,256]{3,2,0,1:T(8,128)(2,1)S(1)} %bitcast.32), channel_id=1, replica_groups=mesh['row'=8,'col'=4] {'row'}, dimensions={1} | all-to-all | bytes 1048576 | tf_op jit(solution)/shard_map/all_to_all | solution.py:50
  50.3 0.0 copy-start.1
  50.3 0.0 copy-start.3
  50.3 17.7 %all_to_all.40 = bf16[1,8,128,256]{3,2,0,1:T(8,128)(2,1)} all-to-all(bf16[1,8,128,256]{3,2,0,1:T(8,128)(2,1)S(1)} %bitcast.33), channel_id=1, replica_groups=mesh['row'=8,'col'=4] {'row'}, dimensions={1} | all-to-all | bytes 1048576 | tf_op jit(solution)/shard_map/all_to_all | solution.py:49
  68.0 4.6 %all-to-all-start.2 = ((bf16[2,4,128,256]{3,2,0,1:T(8,128)(2,1)}), bf16[2,4,128,256]{3,2,0,1:T(8,128)(2,1)S(1)}, u32[]{:S(2)}, u32[]{:S(2)}) async-start(bf16[2,4,128,256]{3,2,0,1:T(8,128)(2,1)} %bitcast.7), calls=%async_computation.2 | async-start | bytes 1048576 | tf_op jit(solution)/shard_map/all_to_all | solution.py:58
  72.6 8.0 %all-to-all-done.2 = bf16[2,4,128,256]{3,2,0,1:T(8,128)(2,1)S(1)} async-done(((bf16[2,4,128,256]{3,2,0,1:T(8,128)(2,1)}), bf16[2,4,128,256]{3,2,0,1:T(8,128)(2,1)S(1)}, u32[]{:S(2)}, u32[]{:S(2)}) %all-to-all-start.2) | async-done | bytes 524320 | tf_op jit(solution)/shard_map/all_to_all | solution.py:58
  80.6 4.3 %all-to-all-start.5 = ((bf16[2,4,128,256]{3,2,0,1:T(8,128)(2,1)}), bf16[2,4,128,256]{3,2,0,1:T(8,128)(2,1)S(1)}, u32[]{:S(2)}, u32[]{:S(2)}) async-start(bf16[2,4,128,256]{3,2,0,1:T(8,128)(2,1)} %bitcast.15), calls=%async_computation.5 | async-start | bytes 1048576 | tf_op jit(solution)/shard_map/all_to_all | solution.py:59
  84.9 0.0 all-gather.3.cloned.1.call-start
  84.9 0.0 copy-done.1
  84.9 0.0 copy-done.3
  84.9 2.3 %fusion.3 = f32[512,256]{1,0:T(8,128)S(1)} fusion(bf16[1024,256]{1,0:T(8,128)(2,1)S(1)} %bitcast.37, bf16[512,1024]{1,0:T(8,128)(2,1)} %param.9, bf16[512,1024]{1,0:T(8,128)(2,1)S(1)} %copy-done.1, bf16[512,1024]{1,0:T(8,128)(2,1)} %param.8, bf16[512,1024]{1,0:T(8,128)(2,1)S(1)} %copy-done.3, s32[1024]{0:T(1024)S(1)} %iota_add_fusion, s32[512]{0:T(512)S(1)} %iota_add_fusion.1), kind=kOutput, calls=%fused_computation.7 | convolution fusion | flops 273678336 | bytes 5249024 | tf_op jit(solution)/shard_map/dot_general | solution.py:75
  87.2 5.6 %all-to-all-done.5 = bf16[2,4,128,256]{3,2,0,1:T(8,128)(2,1)S(1)} async-done(((bf16[2,4,128,256]{3,2,0,1:T(8,128)(2,1)}), bf16[2,4,128,256]{3,2,0,1:T(8,128)(2,1)S(1)}, u32[]{:S(2)}, u32[]{:S(2)}) %all-to-all-start.5) | async-done | bytes 524320 | tf_op jit(solution)/shard_map/all_to_all | solution.py:59
  92.9 2.6 %fusion.1 = f32[512,256]{1,0:T(8,128)} fusion(f32[512,256]{1,0:T(8,128)S(1)} %fusion.3, bf16[512,1024]{1,0:T(8,128)(2,1)} %param.8, bf16[512,1024]{1,0:T(8,128)(2,1)S(1)} %copy-done.3, bf16[1024,256]{1,0:T(8,128)(2,1)S(1)} %bitcast.36, s32[256]{0:T(256)S(1)} %iota_add_fusion.2, s32[1024]{0:T(1024)S(1)} %iota_add_fusion), kind=kOutput, calls=%fused_computation.5 | convolution fusion | flops 271319040 | bytes 3675136 | tf_op jit(solution)/shard_map/dot_general | solution.py:76
  95.5 0.0 all-gather.3.cloned.1.call-update
  95.5 23.6 %all-gather.3.cloned.1.call-done = f32[2048,256]{1,0:T(8,128)} async-done(((f32[512,256]{1,0:T(8,128)}), f32[2048,256]{1,0:T(8,128)}) %all-gather.3.cloned.1.call-update) | async-done | bytes 2097168 | tf_op jit(solution)/shard_map/all_gather | solution.py:11
  119.2 0.0 copy-start
  119.2 1.2 while.10
  119.2 1.2 bitcast_add_fusion.2
  120.4 0.0 copy-done
  120.5 0.9 add.57
  (8 shorter events, 0.2 us)
Async XLA Ops:
  6.5 1.6 %copy-start.2 = (bf16[512,1024]{1,0:T(8,128)(2,1)S(1)}, bf16[512,1024]{1,0:T(8,128)(2,1)}, u32[]{:S(2)}) copy-start(bf16[512,1024]{1,0:T(8,128)(2,1)} %param.6) | copy-start | bytes 3145732
  9.9 12.1 %all-to-all-start.3 = ((bf16[4,128,2,256]{3,1,2,0:T(8,128)(2,1)}), bf16[4,128,2,256]{3,1,2,0:T(8,128)(2,1)S(1)}, u32[]{:S(2)}, u32[]{:S(2)}) async-start(bf16[4,128,2,256]{3,1,2,0:T(8,128)(2,1)} %copy.25), calls=%async_computation.3 | async-start | bytes 1048576 | tf_op jit(solution)/shard_map/all_to_all | solution.py:42
  50.3 34.6 %copy-start.1 = (bf16[512,1024]{1,0:T(8,128)(2,1)S(1)}, bf16[512,1024]{1,0:T(8,128)(2,1)}, u32[]{:S(2)}) copy-start(bf16[512,1024]{1,0:T(8,128)(2,1)} %param.7) | copy-start | bytes 3145732
  50.3 34.6 %copy-start.3 = (bf16[512,1024]{1,0:T(8,128)(2,1)S(1)}, bf16[512,1024]{1,0:T(8,128)(2,1)}, u32[]{:S(2)}) copy-start(bf16[512,1024]{1,0:T(8,128)(2,1)} %param.6) | copy-start | bytes 3145732
  68.0 12.6 %all-to-all-start.2 = ((bf16[2,4,128,256]{3,2,0,1:T(8,128)(2,1)}), bf16[2,4,128,256]{3,2,0,1:T(8,128)(2,1)S(1)}, u32[]{:S(2)}, u32[]{:S(2)}) async-start(bf16[2,4,128,256]{3,2,0,1:T(8,128)(2,1)} %bitcast.7), calls=%async_computation.2 | async-start | bytes 1048576 | tf_op jit(solution)/shard_map/all_to_all | solution.py:58
  80.6 12.3 %all-to-all-start.5 = ((bf16[2,4,128,256]{3,2,0,1:T(8,128)(2,1)}), bf16[2,4,128,256]{3,2,0,1:T(8,128)(2,1)S(1)}, u32[]{:S(2)}, u32[]{:S(2)}) async-start(bf16[2,4,128,256]{3,2,0,1:T(8,128)(2,1)} %bitcast.15), calls=%async_computation.5 | async-start | bytes 1048576 | tf_op jit(solution)/shard_map/all_to_all | solution.py:59
  84.9 34.3 %all-gather.3.cloned.1.call-start = ((), (), s32[]{:S(2)}) async-start(), calls=%async_computation.6 | async-start | bytes 2621440 | tf_op jit(solution)/shard_map/all_gather | solution.py:11
  119.2 1.3 copy-start
Sparse Core Ops, SparseCore 0:
  95.7 23.4 all-gather.2
where the time goes:
time: 130 us; the launch traced here: 128 us
  blocking collectives  46 us (35%)
  waiting for transfers between devices  44.9 us (35%)
  between operations  13.5 us (10%)
  starting transfers between devices  13 us (10%)
  matrix products  4.89 us (4%)
  local copies, waits for them, and re-layouts  3.55 us (3%)
  other arithmetic  2.22 us (2%)
    all_gather x1, waiting for transfers between devices, carried_in(): gathered = lax.all_gather(part, axis)  23.6 us
    all_to_all x1, blocking collectives, local(): lax.all_to_all(to_rows(spread[0]), 'row', split_axis=1, concat_axis=0, ti...  17.7 us
    all_to_all x1, blocking collectives, local(): lax.all_to_all(to_rows(spread[1]), 'row', split_axis=1, concat_axis=0, ti...  17.3 us
    all_to_all x1, blocking collectives, local(): lax.all_to_all(first_green, 'col', split_axis=0, concat_axis=0, tiled=True)  11.1 us
    all_to_all x1, waiting for transfers between devices, local(): lax.all_to_all(to_cols(crossed[0]), 'col', split_axis=1, concat_axis=1, t...  7.97 us
    all_to_all x1, waiting for transfers between devices, local(): lax.all_to_all(first_diff, 'col', split_axis=0, concat_axis=0, tiled=True)  7.69 us
    all_to_all x1, waiting for transfers between devices, local(): lax.all_to_all(to_cols(crossed[1]), 'col', split_axis=1, concat_axis=1, t...  5.62 us
    all_to_all x1, starting transfers between devices, local(): lax.all_to_all(to_cols(crossed[0]), 'col', split_axis=1, concat_axis=1, t...  4.6 us
  transfers between devices with their start and end apart: 4, of which 4 were waited for; matrix products, arithmetic and copies ran while one was open for 2% of the time, Pallas kernels for 0%

commit v1 on v0

v1 whole, which is shorter than its diff:
```python
import functools

import jax
import jax.numpy as jnp
from jax import lax
from jax.experimental import pallas as pl
from jax.experimental.pallas import tpu as pltpu
from jax.sharding import PartitionSpec as P

WINDOW = 256
LANES = 128
AXES = ("row", "col")
BF16 = jnp.bfloat16
F32 = jnp.float32
ROOM = pltpu.CompilerParams(vmem_limit_bytes=16 * 2**20)


def routes(row_devices, col_devices):
    ratio = row_devices // col_devices
    half = col_devices // 2

    def at(z, y, g):
        return (z * ratio + y) * col_devices + g

    first = [
        (at(z, y, g), at(z, y, g - half)) for z in range(half) for y in range(ratio) for g in range(half, col_devices)
    ]
    near, far, second = [], [], []
    for s in range(ratio):
        near.append([])
        far.append([])
        second.append([])
        for z in range(col_devices):
            for y in range(ratio):
                to = (y + s) % ratio
                for g in range(z, col_devices):
                    if z < half <= g:
                        far[s].append((at(z, y, g), at(g, to, z)))
                        second[s].append((at(z, y, g - half), at(g, to, z)))
                    elif z < g or y < to:
                        near[s].append((at(z, y, g), at(g, to, z)))
    later, d = [], 1
    while d < col_devices:
        d *= 2
    for d in [*range(2, d), 1][: d - 1]:
        pairs = []
        for z in range(col_devices):
            for y in range(ratio):
                for c in range(z + 1):
                    if c < c ^ d < col_devices:
                        pairs.append((at(z, y, c), at(z, y, c ^ d)))
        later.append(pairs)
    return near, far, first, second, later


def held(shape, dtype):
    return pltpu.VMEM(shape, dtype)


def keep(x):
    return pltpu.with_memory_space_constraint(x, pltpu.VMEM)


def place():
    return lax.axis_index("row"), lax.axis_index("col")


def copies(jobs, sem):
    out = [pltpu.make_async_copy(src, dst, sem.at[i]) for i, (src, dst) in enumerate(jobs)]
    for copy in out:
        copy.start()
    for copy in out:
        copy.wait()


def pack(lesser, greater, spans):
    rows, width = lesser.shape
    ratio = width // rows

    def kernel(less_ref, great_ref, *refs):
        outs, sem = refs[:-1], refs[-1]
        my_row, _ = place()
        jobs = []
        for out, (s, r0, r1, c0, c1) in zip(outs, spans):
            block = lax.rem(my_row + s, ratio)
            start = pl.multiple_of(block * rows + c0, LANES)
            for i, ref in enumerate((less_ref, great_ref)):
                jobs.append((ref.at[pl.ds(r0, r1 - r0), pl.ds(start, c1 - c0)], out.at[i]))
        copies(jobs, sem)

    return pl.pallas_call(
        kernel,
        out_shape=[held((2, r1 - r0, c1 - c0), BF16) for _, r0, r1, c0, c1 in spans],
        in_specs=[pl.BlockSpec(memory_space=pl.ANY)] * 2,
        out_specs=[pl.BlockSpec(memory_space=pltpu.VMEM)] * len(spans),
        scratch_shapes=[pltpu.SemaphoreType.DMA((2 * len(spans),))],
        compiler_params=ROOM,
        name="pack_windows",
    )(lesser, greater)


def sigmas(lesser, greater, screened_lesser, screened_greater):
    rows, width = lesser.shape
    ratio = width // rows
    tile = rows // 2

    def kernel(less_ref, great_ref, wless_ref, wgreat_ref, ret_ref, out_ref):
        my_row, my_col = place()
        k, i = pl.program_id(0), pl.program_id(1)
        prod_less = less_ref[...].astype(F32) * wless_ref[...].astype(F32)
        prod_great = great_ref[...].astype(F32) * wgreat_ref[...].astype(F32)
        later = my_row * rows + i * tile + lax.broadcasted_iota(jnp.int32, (tile, rows), 0)
        inner = my_col * width + k * rows + lax.broadcasted_iota(jnp.int32, (tile, rows), 1)
        ret_ref[0] = jnp.where(inner <= later, prod_great - prod_less, 0.0).astype(BF16)
        out_ref[0] = prod_less.astype(BF16)

    return pl.pallas_call(
        kernel,
        grid=(ratio, rows // tile),
        out_shape=[held((ratio, rows, rows), BF16)] * 2,
        in_specs=[pl.BlockSpec((tile, rows), lambda k, i: (i, k))] * 4,
        out_specs=[pl.BlockSpec((1, tile, rows), lambda k, i: (k, i, 0))] * 2,
        compiler_params=ROOM,
        name="sigma_blocks",
    )(lesser, greater, screened_lesser, screened_greater)


def block_term(ret_ref, less_ref, k, win, my_row, my_col, rows, width, first):
    green, great = win(0), win(1)
    diff = (green.astype(F32) - great.astype(F32)).astype(BF16)
    inner = my_col * width + k * rows + lax.broadcasted_iota(jnp.int32, diff.shape, 0)
    times = my_row * rows + first + lax.broadcasted_iota(jnp.int32, diff.shape, 1)
    diff = jnp.where(inner <= times, diff, jnp.zeros((), BF16))
    return jnp.dot(ret_ref[k], green, preferred_element_type=F32) + jnp.dot(
        less_ref[k], diff, preferred_element_type=F32
    )


def partial(ret, less, own, wins, first, cols, width, scale):
    ratio, rows, _ = ret.shape
    counts = [len(pieces) for pieces in wins]

    def kernel(ret_ref, less_ref, own_ref, *refs):
        out_ref, send_ref = refs[-2:]
        my_row, my_col = place()
        total, at = None, 0
        for s in range(ratio):
            k = lax.rem(my_row + ratio - s, ratio)
            mine = refs[at : at + counts[s]]
            at += counts[s]

            def win(i, s=s, mine=mine):
                got = None
                for (start, _), ref in zip(wins[s], mine):
                    piece = ref[i, :, start : start + cols]
                    got = piece if got is None else got + piece
                if s == 0:
                    got = jnp.where(my_col == my_row // ratio, own_ref[i], got)
                return got

            term = block_term(ret_ref, less_ref, k, win, my_row, my_col, rows, width, first)
            total = term if total is None else total + term
        total = scale * total
        out_ref[...] = total
        send_ref[...] = total.astype(BF16)

    return pl.pallas_call(
        kernel,
        out_shape=[held((rows, cols), F32), held((rows, cols), BF16)],
        in_specs=[pl.BlockSpec(memory_space=pltpu.VMEM)] * (3 + sum(counts)),
        out_specs=[pl.BlockSpec(memory_space=pltpu.VMEM)] * 2,
        compiler_params=ROOM,
        name="partial",
    )(*map(keep, [ret, less, own]), *[keep(x) for pieces in wins for _, x in pieces])


def accumulate(parts, got):
    rows, cols = parts[0].shape
    n = len(parts)

    def kernel(*refs):
        part_refs, out_ref = refs[:n], refs[-1]
        got_refs = refs[n:-1]
        each = len(got_refs) // n
        for q in range(n):
            total = part_refs[q][...]
            for ref in got_refs[q * each : (q + 1) * each]:
                total = total + ref[...].astype(F32)
            out_ref[:, q * cols : (q + 1) * cols] = total

    return pl.pallas_call(
        kernel,
        out_shape=jax.ShapeDtypeStruct((rows, n * cols), F32),
        in_specs=[pl.BlockSpec(memory_space=pltpu.VMEM)] * (n + sum(map(len, got))),
        out_specs=pl.BlockSpec(memory_space=pltpu.VMEM),
        compiler_params=ROOM,
        name="accumulate",
    )(*map(keep, parts), *[keep(g) for group in got for g in group])


def local(lesser, greater, screened_lesser, screened_greater):
    rows, width = lesser.shape
    row_devices, col_devices = lax.axis_size("row"), lax.axis_size("col")
    ratio = row_devices // col_devices
    scale = float(width * col_devices) ** (-0.5)
    near, far, first, second, later = routes(row_devices, col_devices)
    chunks = WINDOW // LANES

    def send(x, pairs):
        return lax.ppermute(x, AXES, pairs)

    jobs = [(s, q) for q in range(chunks) for s in reversed(range(ratio))]
    spans = [(s, 0, rows, q * LANES, (q + 1) * LANES) for s, q in jobs]
    odd = range(1, ratio, 2)
    spans += [(s, 0, rows, 0, WINDOW) for s in odd]
    packed = pack(lesser, greater, spans)
    ready = dict(zip(jobs, packed))
    wins, hops = {}, {}
    for s, q in jobs:
        if s % 2:
            hops[s, q] = send(ready[s, q], first)
        else:
            wins[s, q] = [(0, send(ready[s, q], near[s] + far[s]))]
    beside = {s: send(x, near[s]) for s, x in zip(odd, packed[len(jobs) :])}
    for s, q in jobs:
        if s % 2:
            wins[s, q] = [(0, send(hops[s, q], second[s])), (q * LANES, beside[s])]
    ret, less = sigmas(lesser, greater, screened_lesser, screened_greater)
    parts, got = [], []
    for q in range(chunks):
        mine = [wins[s, q] for s in range(ratio)]
        part, out = partial(ret, less, ready[0, q], mine, q * LANES, LANES, width, scale)
        parts.append(part)
        got.append([send(out, pairs) for pairs in later])
    return accumulate(parts, got)


def solution(mesh):
    in_specs = (P("row", "col"),) * 4
    return jax.shard_map(local, mesh=mesh, in_specs=in_specs, out_specs=P("row", "col"), check_vma=False)
```

time: 130 us -> 50.4 us (0.39)
  the two profiles are of different devices: /device:TPU:25 before, /device:TPU:31 now
where the time goes in v1:
time: 50.4 us; the launch traced here: 50 us
  waiting for transfers between devices  30 us (60%)
  starting transfers between devices  13.2 us (26%)
  Pallas kernels  4.08 us (8%)
  local copies, waits for them, and re-layouts  2.46 us (5%)
    ppermute x13, waiting for transfers between devices, send(): return lax.ppermute(x, AXES, pairs)  30 us
    ppermute x13, starting transfers between devices, send(): return lax.ppermute(x, AXES, pairs)  13.2 us
    unnamed x8, local copies, waits for them, and re-layouts  2.46 us
    pallas_call x2, Pallas kernels, partial(): pl.pallas_call(kernel, out_shape=[held((rows, cols), F32), held((rows, co...  1.53 us
    pallas_call x1, Pallas kernels, sigmas(): pl.pallas_call(kernel, grid=(ratio, rows // tile), out_shape=[held((ratio...  1.2 us
  transfers between devices with their start and end apart: 13, of which 4 were waited for; matrix products, arithmetic and copies ran while one was open for 0% of the time, Pallas kernels for 5%

profile of v1, /device:TPU:31, one launch (start us, length us, event | category | flops | bytes accessed | tf_op | source)
XLA Modules:
  0.0 50.0 jit_solution(10468370562576464432)
XLA Ops:
  0.0 1.2 %copy-done = bf16[512,1024]{1,0:T(8,128)(2,1)S(1)} copy-done((bf16[512,1024]{1,0:T(8,128)(2,1)S(1)}, bf16[512,1024]{1,0:T(8,128)(2,1)}, u32[]{:S(2)}) %copy-start) | copy-done | bytes 1048600
  1.2 1.2 %copy-done.1 = bf16[512,1024]{1,0:T(8,128)(2,1)S(1)} copy-done((bf16[512,1024]{1,0:T(8,128)(2,1)S(1)}, bf16[512,1024]{1,0:T(8,128)(2,1)}, u32[]{:S(2)}) %copy-start.1) | copy-done | bytes 1048600
  2.5 0.5 pack_windows.1
  2.9 1.4 %collective-permute-start.3 = (bf16[2,512,256]{2,1,0:T(8,128)(2,1)S(1)}, bf16[2,512,256]{2,1,0:T(8,128)(2,1)S(1)}, u32[]{:S(2)}, u32[]{:S(2)}) collective-permute-start(bf16[2,512,256]{2,1,0:T(8,128)(2,1)S(1)} %get-tuple-element.20), channel_id=1, source_target_pairs={{0,4},{1,12},{5,8},{9,13},{18,22},{19,30},{23,26},{27,31}} | collective-permute-start | bytes 1572872 | tf_op jit(solution)/shard_map/ppermute | solution.py:210
  4.3 0.7 %collective-permute-start.5 = (bf16[2,512,128]{2,1,0:T(8,128)(2,1)S(1)}, bf16[2,512,128]{2,1,0:T(8,128)(2,1)S(1)}, u32[]{:S(2)}, u32[]{:S(2)}) collective-permute-start(bf16[2,512,128]{2,1,0:T(8,128)(2,1)S(1)} %get-tuple-element.23), channel_id=1, source_target_pairs={{2,0},{3,1},{6,4},{7,5},{10,8},{11,9},{14,12},{15,13}} | collective-permute-start | bytes 786440 | tf_op jit(solution)/shard_map/ppermute | solution.py:210
  5.0 0.7 %collective-permute-start.1 = (bf16[2,512,128]{2,1,0:T(8,128)(2,1)S(1)}, bf16[2,512,128]{2,1,0:T(8,128)(2,1)S(1)}, u32[]{:S(2)}, u32[]{:S(2)}) collective-permute-start(bf16[2,512,128]{2,1,0:T(8,128)(2,1)S(1)} %get-tuple-element.19), channel_id=1, source_target_pairs={{2,0},{3,1},{6,4},{7,5},{10,8},{11,9},{14,12},{15,13}} | collective-permute-start | bytes 786440 | tf_op jit(solution)/shard_map/ppermute | solution.py:210
  5.7 0.7 %collective-permute-start.4 = (bf16[2,512,128]{2,1,0:T(8,128)(2,1)S(1)}, bf16[2,512,128]{2,1,0:T(8,128)(2,1)S(1)}, u32[]{:S(2)}, u32[]{:S(2)}) collective-permute-start(bf16[2,512,128]{2,1,0:T(8,128)(2,1)S(1)} %get-tuple-element.22.own_ref), channel_id=1, source_target_pairs={{1,8},{5,12},{19,26},{23,30},{2,16},{3,24},{6,20},{7,28},{10,17},{... | collective-permute-start | bytes 786440 | tf_op jit(solution)/shard_map/ppermute | solution.py:210
  6.4 0.0 collective-permute-done.5
  6.4 0.7 %collective-permute-start.6 = (bf16[2,512,128]{2,1,0:T(8,128)(2,1)S(1)}, bf16[2,512,128]{2,1,0:T(8,128)(2,1)S(1)}, u32[]{:S(2)}, u32[]{:S(2)}) collective-permute-start(bf16[2,512,128]{2,1,0:T(8,128)(2,1)S(1)} %collective-permute-done.5), channel_id=1, source_target_pairs={{0,20},{1,28},{4,16},{5,24},{8,21},{9,29},{12,17},{13,25}} | collective-permute-start | bytes 786440 | tf_op jit(solution)/shard_map/ppermute | solution.py:210
  7.1 0.7 %collective-permute-start = (bf16[2,512,128]{2,1,0:T(8,128)(2,1)S(1)}, bf16[2,512,128]{2,1,0:T(8,128)(2,1)S(1)}, u32[]{:S(2)}, u32[]{:S(2)}) collective-permute-start(bf16[2,512,128]{2,1,0:T(8,128)(2,1)S(1)} %get-tuple-element.18.own_ref), channel_id=1, source_target_pairs={{1,8},{5,12},{19,26},{23,30},{2,16},{3,24},{6,20},{7,28},{10,17},{... | collective-permute-start | bytes 786440 | tf_op jit(solution)/shard_map/ppermute | solution.py:210
  7.8 0.0 collective-permute-done.1
  7.8 0.7 %collective-permute-start.2 = (bf16[2,512,128]{2,1,0:T(8,128)(2,1)S(1)}, bf16[2,512,128]{2,1,0:T(8,128)(2,1)S(1)}, u32[]{:S(2)}, u32[]{:S(2)}) collective-permute-start(bf16[2,512,128]{2,1,0:T(8,128)(2,1)S(1)} %collective-permute-done.1), channel_id=1, source_target_pairs={{0,20},{1,28},{4,16},{5,24},{8,21},{9,29},{12,17},{13,25}} | collective-permute-start | bytes 786440 | tf_op jit(solution)/shard_map/ppermute | solution.py:210
  8.5 1.2 %sigma_blocks.1 = (bf16[2,512,512]{2,1,0:T(8,128)(2,1)S(1)}, bf16[2,512,512]{2,1,0:T(8,128)(2,1)S(1)}) custom-call(bf16[512,1024]{1,0:T(8,128)(2,1)S(1)} %copy-done, bf16[512,1024]{1,0:T(8,128)(2,1)S(1)} %copy-done.1, bf16[512,1024]{1,0:T(8,128)(2,1)S(1)} %copy-done.2, bf16[512,1024]{1,0:T(8,128)(2,1)S(1)} %copy-done.3), custom_call_target="tpu_custom_call" | custom-call | tf_op jit(solution)/shard_map/sigma_blocks/pallas_call | solution.py:117
  9.7 0.0 collective-permute-done.4.refs_0_
  9.7 9.2 %collective-permute-done.3.refs_2_ = bf16[2,512,256]{2,1,0:T(8,128)(2,1)S(1)} collective-permute-done((bf16[2,512,256]{2,1,0:T(8,128)(2,1)S(1)}, bf16[2,512,256]{2,1,0:T(8,128)(2,1)S(1)}, u32[]{:S(2)}, u32[]{:S(2)}) %collective-permute-start.3) | collective-permute-done | bytes 524320 | tf_op jit(solution)/shard_map/ppermute | solution.py:210
  18.9 0.0 collective-permute-done.6.refs_1_
  18.9 0.8 %partial.3 = (f32[512,128]{1,0:T(8,128)S(1)}, bf16[512,128]{1,0:T(8,128)(2,1)S(1)}) custom-call(bf16[2,512,512]{2,1,0:T(8,128)(2,1)S(1)} %get-tuple-element.16.ret_ref, bf16[2,512,512]{2,1,0:T(8,128)(2,1)S(1)} %get-tuple-element.17.less_ref, bf16[2,512,128]{2,1,0:T(8,128)(2,1)S(1)} %get-tuple-element.22.own_ref, ...), custom_call_target="tpu_custom_call" | custom-call | tf_op jit(solution)/shard_map/partial/pallas_call | solution.py:167
  19.7 1.3 %collective-permute-start.10 = (bf16[512,128]{1,0:T(8,128)(2,1)S(1)}, bf16[512,128]{1,0:T(8,128)(2,1)S(1)}, u32[]{:S(2)}, u32[]{:S(2)}) collective-permute-start(bf16[512,128]{1,0:T(8,128)(2,1)S(1)} %get-tuple-element.26), channel_id=1, source_target_pairs={{0,2},{4,6},{8,10},{9,11},{12,14},{13,15},{16,18},{17,19},{20,22},... | collective-permute-start | bytes 393224 | tf_op jit(solution)/shard_map/ppermute | solution.py:210
  21.0 1.3 %collective-permute-start.11 = (bf16[512,128]{1,0:T(8,128)(2,1)S(1)}, bf16[512,128]{1,0:T(8,128)(2,1)S(1)}, u32[]{:S(2)}, u32[]{:S(2)}) collective-permute-start(bf16[512,128]{1,0:T(8,128)(2,1)S(1)} %get-tuple-element.26), channel_id=1, source_target_pairs={{0,3},{4,7},{8,11},{9,10},{12,15},{13,14},{16,19},{17,18},{20,23},... | collective-permute-start | bytes 393224 | tf_op jit(solution)/shard_map/ppermute | solution.py:210
  22.3 1.3 %collective-permute-start.12 = (bf16[512,128]{1,0:T(8,128)(2,1)S(1)}, bf16[512,128]{1,0:T(8,128)(2,1)S(1)}, u32[]{:S(2)}, u32[]{:S(2)}) collective-permute-start(bf16[512,128]{1,0:T(8,128)(2,1)S(1)} %get-tuple-element.26), channel_id=1, source_target_pairs={{0,1},{4,5},{8,9},{12,13},{16,17},{18,19},{20,21},{22,23},{24,25},... | collective-permute-start | bytes 393224 | tf_op jit(solution)/shard_map/ppermute | solution.py:210
  23.6 0.0 collective-permute-done.refs_0_
  23.6 0.0 collective-permute-done.2.refs_1_
  23.6 0.8 %partial.2 = (f32[512,128]{1,0:T(8,128)S(1)}, bf16[512,128]{1,0:T(8,128)(2,1)S(1)}) custom-call(bf16[2,512,512]{2,1,0:T(8,128)(2,1)S(1)} %get-tuple-element.16.ret_ref, bf16[2,512,512]{2,1,0:T(8,128)(2,1)S(1)} %get-tuple-element.17.less_ref, bf16[2,512,128]{2,1,0:T(8,128)(2,1)S(1)} %get-tuple-element.18.own_ref, ...), custom_call_target="tpu_custom_call" | custom-call | tf_op jit(solution)/shard_map/partial/pallas_call | solution.py:167
  24.4 1.3 %collective-permute-start.7 = (bf16[512,128]{1,0:T(8,128)(2,1)S(1)}, bf16[512,128]{1,0:T(8,128)(2,1)S(1)}, u32[]{:S(2)}, u32[]{:S(2)}) collective-permute-start(bf16[512,128]{1,0:T(8,128)(2,1)S(1)} %get-tuple-element.25), channel_id=1, source_target_pairs={{0,2},{4,6},{8,10},{9,11},{12,14},{13,15},{16,18},{17,19},{20,22},... | collective-permute-start | bytes 393224 | tf_op jit(solution)/shard_map/ppermute | solution.py:210
  25.7 1.3 %collective-permute-start.8 = (bf16[512,128]{1,0:T(8,128)(2,1)S(1)}, bf16[512,128]{1,0:T(8,128)(2,1)S(1)}, u32[]{:S(2)}, u32[]{:S(2)}) collective-permute-start(bf16[512,128]{1,0:T(8,128)(2,1)S(1)} %get-tuple-element.25), channel_id=1, source_target_pairs={{0,3},{4,7},{8,11},{9,10},{12,15},{13,14},{16,19},{17,18},{20,23},... | collective-permute-start | bytes 393224 | tf_op jit(solution)/shard_map/ppermute | solution.py:210
  27.0 13.2 %collective-permute-done.10.refs_5_ = bf16[512,128]{1,0:T(8,128)(2,1)S(1)} collective-permute-done((bf16[512,128]{1,0:T(8,128)(2,1)S(1)}, bf16[512,128]{1,0:T(8,128)(2,1)S(1)}, u32[]{:S(2)}, u32[]{:S(2)}) %collective-permute-start.10) | collective-permute-done | bytes 131104 | tf_op jit(solution)/shard_map/ppermute | solution.py:210
  40.1 1.3 %collective-permute-start.9 = (bf16[512,128]{1,0:T(8,128)(2,1)S(1)}, bf16[512,128]{1,0:T(8,128)(2,1)S(1)}, u32[]{:S(2)}, u32[]{:S(2)}) collective-permute-start(bf16[512,128]{1,0:T(8,128)(2,1)S(1)} %get-tuple-element.25), channel_id=1, source_target_pairs={{0,1},{4,5},{8,9},{12,13},{16,17},{18,19},{20,21},{22,23},{24,25},... | collective-permute-start | bytes 393224 | tf_op jit(solution)/shard_map/ppermute | solution.py:210
  41.4 0.0 collective-permute-done.11.refs_6_
  41.4 0.0 collective-permute-done.12.refs_7_
  41.5 3.8 %collective-permute-done.7.refs_2_ = bf16[512,128]{1,0:T(8,128)(2,1)S(1)} collective-permute-done((bf16[512,128]{1,0:T(8,128)(2,1)S(1)}, bf16[512,128]{1,0:T(8,128)(2,1)S(1)}, u32[]{:S(2)}, u32[]{:S(2)}) %collective-permute-start.7) | collective-permute-done | bytes 131104 | tf_op jit(solution)/shard_map/ppermute | solution.py:210
  45.3 3.8 %collective-permute-done.8.refs_3_ = bf16[512,128]{1,0:T(8,128)(2,1)S(1)} collective-permute-done((bf16[512,128]{1,0:T(8,128)(2,1)S(1)}, bf16[512,128]{1,0:T(8,128)(2,1)S(1)}, u32[]{:S(2)}, u32[]{:S(2)}) %collective-permute-start.8) | collective-permute-done | bytes 131104 | tf_op jit(solution)/shard_map/ppermute | solution.py:210
  49.1 0.9 %accumulate.1 = f32[512,256]{1,0:T(8,128)} custom-call(f32[512,128]{1,0:T(8,128)S(1)} %get-tuple-element.21.refs_0_, f32[512,128]{1,0:T(8,128)S(1)} %get-tuple-element.24.refs_1_, bf16[512,128]{1,0:T(8,128)(2,1)S(1)} %collective-permute-done.7.refs_2_, bf16[512,128]{1,0:T(8,128)(2,1)S(1)} %collective-permute-done.8.refs_3_, ...), custom_call_target="tpu_custom_call" | custom-call | tf_op jit(solution)/shard_map/accumulate/pallas_call | solution.py:191
  (7 shorter events, 0.0 us)
Async XLA Ops:
  0.0 1.2 %copy-start = (bf16[512,1024]{1,0:T(8,128)(2,1)S(1)}, bf16[512,1024]{1,0:T(8,128)(2,1)}, u32[]{:S(2)}) copy-start(bf16[512,1024]{1,0:T(8,128)(2,1)} %less_ref.3) | copy-start | bytes 3145732
  1.2 1.2 %copy-start.1 = (bf16[512,1024]{1,0:T(8,128)(2,1)S(1)}, bf16[512,1024]{1,0:T(8,128)(2,1)}, u32[]{:S(2)}) copy-start(bf16[512,1024]{1,0:T(8,128)(2,1)} %great_ref.3) | copy-start | bytes 3145732
  2.5 6.0 %copy-start.2 = (bf16[512,1024]{1,0:T(8,128)(2,1)S(1)}, bf16[512,1024]{1,0:T(8,128)(2,1)}, u32[]{:S(2)}) copy-start(bf16[512,1024]{1,0:T(8,128)(2,1)} %wless_ref.1) | copy-start | bytes 3145732
  2.5 6.0 %copy-start.3 = (bf16[512,1024]{1,0:T(8,128)(2,1)S(1)}, bf16[512,1024]{1,0:T(8,128)(2,1)}, u32[]{:S(2)}) copy-start(bf16[512,1024]{1,0:T(8,128)(2,1)} %wgreat_ref.1) | copy-start | bytes 3145732
  2.9 16.0 %collective-permute-start.3 = (bf16[2,512,256]{2,1,0:T(8,128)(2,1)S(1)}, bf16[2,512,256]{2,1,0:T(8,128)(2,1)S(1)}, u32[]{:S(2)}, u32[]{:S(2)}) collective-permute-start(bf16[2,512,256]{2,1,0:T(8,128)(2,1)S(1)} %get-tuple-element.20), channel_id=1, source_target_pairs={{0,4},{1,12},{5,8},{9,13},{18,22},{19,30},{23,26},{27,31}} | collective-permute-start | bytes 1572872 | tf_op jit(solution)/shard_map/ppermute | solution.py:210
  4.3 2.1 %collective-permute-start.5 = (bf16[2,512,128]{2,1,0:T(8,128)(2,1)S(1)}, bf16[2,512,128]{2,1,0:T(8,128)(2,1)S(1)}, u32[]{:S(2)}, u32[]{:S(2)}) collective-permute-start(bf16[2,512,128]{2,1,0:T(8,128)(2,1)S(1)} %get-tuple-element.23), channel_id=1, source_target_pairs={{2,0},{3,1},{6,4},{7,5},{10,8},{11,9},{14,12},{15,13}} | collective-permute-start | bytes 786440 | tf_op jit(solution)/shard_map/ppermute | solution.py:210
  5.0 2.8 %collective-permute-start.1 = (bf16[2,512,128]{2,1,0:T(8,128)(2,1)S(1)}, bf16[2,512,128]{2,1,0:T(8,128)(2,1)S(1)}, u32[]{:S(2)}, u32[]{:S(2)}) collective-permute-start(bf16[2,512,128]{2,1,0:T(8,128)(2,1)S(1)} %get-tuple-element.19), channel_id=1, source_target_pairs={{2,0},{3,1},{6,4},{7,5},{10,8},{11,9},{14,12},{15,13}} | collective-permute-start | bytes 786440 | tf_op jit(solution)/shard_map/ppermute | solution.py:210
  5.7 4.0 %collective-permute-start.4 = (bf16[2,512,128]{2,1,0:T(8,128)(2,1)S(1)}, bf16[2,512,128]{2,1,0:T(8,128)(2,1)S(1)}, u32[]{:S(2)}, u32[]{:S(2)}) collective-permute-start(bf16[2,512,128]{2,1,0:T(8,128)(2,1)S(1)} %get-tuple-element.22.own_ref), channel_id=1, source_target_pairs={{1,8},{5,12},{19,26},{23,30},{2,16},{3,24},{6,20},{7,28},{10,17},{... | collective-permute-start | bytes 786440 | tf_op jit(solution)/shard_map/ppermute | solution.py:210
  6.4 12.5 %collective-permute-start.6 = (bf16[2,512,128]{2,1,0:T(8,128)(2,1)S(1)}, bf16[2,512,128]{2,1,0:T(8,128)(2,1)S(1)}, u32[]{:S(2)}, u32[]{:S(2)}) collective-permute-start(bf16[2,512,128]{2,1,0:T(8,128)(2,1)S(1)} %collective-permute-done.5), channel_id=1, source_target_pairs={{0,20},{1,28},{4,16},{5,24},{8,21},{9,29},{12,17},{13,25}} | collective-permute-start | bytes 786440 | tf_op jit(solution)/shard_map/ppermute | solution.py:210
  7.1 16.5 %collective-permute-start = (bf16[2,512,128]{2,1,0:T(8,128)(2,1)S(1)}, bf16[2,512,128]{2,1,0:T(8,128)(2,1)S(1)}, u32[]{:S(2)}, u32[]{:S(2)}) collective-permute-start(bf16[2,512,128]{2,1,0:T(8,128)(2,1)S(1)} %get-tuple-element.18.own_ref), channel_id=1, source_target_pairs={{1,8},{5,12},{19,26},{23,30},{2,16},{3,24},{6,20},{7,28},{10,17},{... | collective-permute-start | bytes 786440 | tf_op jit(solution)/shard_map/ppermute | solution.py:210
  7.8 15.8 %collective-permute-start.2 = (bf16[2,512,128]{2,1,0:T(8,128)(2,1)S(1)}, bf16[2,512,128]{2,1,0:T(8,128)(2,1)S(1)}, u32[]{:S(2)}, u32[]{:S(2)}) collective-permute-start(bf16[2,512,128]{2,1,0:T(8,128)(2,1)S(1)} %collective-permute-done.1), channel_id=1, source_target_pairs={{0,20},{1,28},{4,16},{5,24},{8,21},{9,29},{12,17},{13,25}} | collective-permute-start | bytes 786440 | tf_op jit(solution)/shard_map/ppermute | solution.py:210
  19.7 20.5 %collective-permute-start.10 = (bf16[512,128]{1,0:T(8,128)(2,1)S(1)}, bf16[512,128]{1,0:T(8,128)(2,1)S(1)}, u32[]{:S(2)}, u32[]{:S(2)}) collective-permute-start(bf16[512,128]{1,0:T(8,128)(2,1)S(1)} %get-tuple-element.26), channel_id=1, source_target_pairs={{0,2},{4,6},{8,10},{9,11},{12,14},{13,15},{16,18},{17,19},{20,22},... | collective-permute-start | bytes 393224 | tf_op jit(solution)/shard_map/ppermute | solution.py:210
  21.0 20.5 %collective-permute-start.11 = (bf16[512,128]{1,0:T(8,128)(2,1)S(1)}, bf16[512,128]{1,0:T(8,128)(2,1)S(1)}, u32[]{:S(2)}, u32[]{:S(2)}) collective-permute-start(bf16[512,128]{1,0:T(8,128)(2,1)S(1)} %get-tuple-element.26), channel_id=1, source_target_pairs={{0,3},{4,7},{8,11},{9,10},{12,15},{13,14},{16,19},{17,18},{20,23},... | collective-permute-start | bytes 393224 | tf_op jit(solution)/shard_map/ppermute | solution.py:210
  22.3 19.2 %collective-permute-start.12 = (bf16[512,128]{1,0:T(8,128)(2,1)S(1)}, bf16[512,128]{1,0:T(8,128)(2,1)S(1)}, u32[]{:S(2)}, u32[]{:S(2)}) collective-permute-start(bf16[512,128]{1,0:T(8,128)(2,1)S(1)} %get-tuple-element.26), channel_id=1, source_target_pairs={{0,1},{4,5},{8,9},{12,13},{16,17},{18,19},{20,21},{22,23},{24,25},... | collective-permute-start | bytes 393224 | tf_op jit(solution)/shard_map/ppermute | solution.py:210
  24.4 20.9 %collective-permute-start.7 = (bf16[512,128]{1,0:T(8,128)(2,1)S(1)}, bf16[512,128]{1,0:T(8,128)(2,1)S(1)}, u32[]{:S(2)}, u32[]{:S(2)}) collective-permute-start(bf16[512,128]{1,0:T(8,128)(2,1)S(1)} %get-tuple-element.25), channel_id=1, source_target_pairs={{0,2},{4,6},{8,10},{9,11},{12,14},{13,15},{16,18},{17,19},{20,22},... | collective-permute-start | bytes 393224 | tf_op jit(solution)/shard_map/ppermute | solution.py:210
  25.7 23.4 %collective-permute-start.8 = (bf16[512,128]{1,0:T(8,128)(2,1)S(1)}, bf16[512,128]{1,0:T(8,128)(2,1)S(1)}, u32[]{:S(2)}, u32[]{:S(2)}) collective-permute-start(bf16[512,128]{1,0:T(8,128)(2,1)S(1)} %get-tuple-element.25), channel_id=1, source_target_pairs={{0,3},{4,7},{8,11},{9,10},{12,15},{13,14},{16,19},{17,18},{20,23},... | collective-permute-start | bytes 393224 | tf_op jit(solution)/shard_map/ppermute | solution.py:210
  40.1 9.0 %collective-permute-start.9 = (bf16[512,128]{1,0:T(8,128)(2,1)S(1)}, bf16[512,128]{1,0:T(8,128)(2,1)S(1)}, u32[]{:S(2)}, u32[]{:S(2)}) collective-permute-start(bf16[512,128]{1,0:T(8,128)(2,1)S(1)} %get-tuple-element.25), channel_id=1, source_target_pairs={{0,1},{4,5},{8,9},{12,13},{16,17},{18,19},{20,21},{22,23},{24,25},... | collective-permute-start | bytes 393224 | tf_op jit(solution)/shard_map/ppermute | solution.py:210

commit v2 on v1

v2 whole, which is shorter than its diff:
```python
import functools

import jax
import jax.numpy as jnp
from jax import lax
from jax.experimental import pallas as pl
from jax.experimental.pallas import tpu as pltpu
from jax.sharding import PartitionSpec as P

WINDOW = 256
LANES = 128
AXES = ("row", "col")
BF16 = jnp.bfloat16
F32 = jnp.float32
ROOM = pltpu.CompilerParams(vmem_limit_bytes=16 * 2**20)


def routes(row_devices, col_devices):
    ratio = row_devices // col_devices
    half = col_devices // 2
    straight = col_devices - half // 2

    def at(z, y, g):
        return (z * ratio + y) * col_devices + g

    plan = []
    for s in range(ratio):
        first, second, left = [], [], []
        near, hops = {}, []
        for z in range(col_devices):
            for y in range(ratio):
                to = (y + s) % ratio
                for g in range(z, col_devices):
                    src, dst = at(z, y, g), at(g, to, z)
                    if z < half and g >= straight:
                        hops.append((z, y, src, dst))
                    elif z < half <= g:
                        first.append((src, dst))
                    elif z < g or y < to:
                        near[dst] = src
        relays, kept = set(), set()
        for z, y, src, dst in hops:
            choice = None
            for g in range(half):
                relay = at(z, y, g)
                if relay in relays or relay in kept:
                    continue
                if relay not in near:
                    choice = relay
                    break
                if choice is None and near[relay] not in relays:
                    choice = relay
            if choice is None:
                left.append((src, dst))
                continue
            relays.add(choice)
            if choice in near:
                kept.add(near[choice])
            first.append((src, choice))
            second.append((choice, dst))
        for dst, src in near.items():
            if dst not in relays and src not in kept:
                first.append((src, dst))
            elif dst in relays and src in kept and (src, src) not in first:
                first.append((src, src))
                second.append((src, dst))
            else:
                left.append((src, dst))
        brings = {dst for src, dst in first if src != dst and dst not in relays}
        plan.append((first, second, left, brings))
    later, d = [], 1
    while d < col_devices:
        d *= 2
    for d in [*range(2, d), 1][: d - 1]:
        pairs = []
        for z in range(col_devices):
            for y in range(ratio):
                for c in range(z + 1):
                    if c < c ^ d < col_devices:
                        pairs.append((at(z, y, c), at(z, y, c ^ d)))
        later.append(pairs)
    return plan, later


def member(devices, index):
    found = jnp.int32(0)
    for word in range(max(devices, default=0) // 31 + 1):
        bits = sum(1 << (d % 31) for d in devices if d // 31 == word)
        found = found + jnp.where(index // 31 == word, (jnp.int32(bits) >> (index % 31)) & 1, 0)
    return found != 0


def held(shape, dtype):
    return pltpu.VMEM(shape, dtype)


def keep(x):
    return pltpu.with_memory_space_constraint(x, pltpu.VMEM)


def place():
    return lax.axis_index("row"), lax.axis_index("col")


def copies(jobs, sem):
    out = [pltpu.make_async_copy(src, dst, sem.at[i]) for i, (src, dst) in enumerate(jobs)]
    for copy in out:
        copy.start()
    for copy in out:
        copy.wait()


def pack(lesser, greater, spans):
    rows, width = lesser.shape
    ratio = width // rows

    def kernel(less_ref, great_ref, *refs):
        outs, sem = refs[:-1], refs[-1]
        my_row, _ = place()
        jobs = []
        for out, (s, r0, r1, c0, c1) in zip(outs, spans):
            block = lax.rem(my_row + s, ratio)
            start = pl.multiple_of(block * rows + c0, LANES)
            for i, ref in enumerate((less_ref, great_ref)):
                jobs.append((ref.at[pl.ds(r0, r1 - r0), pl.ds(start, c1 - c0)], out.at[i]))
        copies(jobs, sem)

    return pl.pallas_call(
        kernel,
        out_shape=[held((2, r1 - r0, c1 - c0), BF16) for _, r0, r1, c0, c1 in spans],
        in_specs=[pl.BlockSpec(memory_space=pl.ANY)] * 2,
        out_specs=[pl.BlockSpec(memory_space=pltpu.VMEM)] * len(spans),
        scratch_shapes=[pltpu.SemaphoreType.DMA((2 * len(spans),))],
        compiler_params=ROOM,
        name="pack_windows",
    )(*(pltpu.with_memory_space_constraint(x, pltpu.HBM) for x in (lesser, greater)))


def sigmas(lesser, greater, screened_lesser, screened_greater):
    rows, width = lesser.shape
    ratio = width // rows
    steps = 4
    tile = rows // steps

    def kernel(*refs):
        ins, (ret_ref, out_ref), bufs, sem = refs[:4], refs[4:6], refs[6:10], refs[10]
        my_row, my_col = place()
        loads = []
        for i in range(steps):
            at = pl.ds(i * tile, tile)
            loads.append([])
            for n in range(4):
                copy = pltpu.make_async_copy(ins[n].at[at], bufs[n].at[at], sem.at[4 * i + n])
                copy.start()
                loads[i].append(copy)
        for i in range(steps):
            for copy in loads[i]:
                copy.wait()
            at = pl.ds(i * tile, tile)
            for k in range(ratio):
                cols = pl.ds(k * rows, rows)
                less, great, wless, wgreat = (buf[at, cols].astype(F32) for buf in bufs)
                prod_less = less * wless
                later = my_row * rows + i * tile + lax.broadcasted_iota(jnp.int32, (tile, rows), 0)
                inner = my_col * width + k * rows + lax.broadcasted_iota(jnp.int32, (tile, rows), 1)
                ret_ref[k, at] = jnp.where(inner <= later, great * wgreat - prod_less, 0.0).astype(BF16)
                out_ref[k, at] = prod_less.astype(BF16)

    args = (lesser, greater, screened_lesser, screened_greater)
    return pl.pallas_call(
        kernel,
        out_shape=[held((ratio, rows, rows), BF16)] * 2,
        in_specs=[pl.BlockSpec(memory_space=pl.ANY)] * 4,
        out_specs=[pl.BlockSpec(memory_space=pltpu.VMEM)] * 2,
        scratch_shapes=[pltpu.VMEM((rows, width), BF16)] * 4 + [pltpu.SemaphoreType.DMA((4 * steps,))],
        compiler_params=ROOM,
        name="sigma_blocks",
    )(*(pltpu.with_memory_space_constraint(x, pltpu.HBM) for x in args))


def block_term(ret_ref, less_ref, k, win, my_row, my_col, rows, width, first):
    green, great = win(0), win(1)
    diff = (green.astype(F32) - great.astype(F32)).astype(BF16)
    inner = my_col * width + k * rows + lax.broadcasted_iota(jnp.int32, diff.shape, 0)
    times = my_row * rows + first + lax.broadcasted_iota(jnp.int32, diff.shape, 1)
    diff = jnp.where(inner <= times, diff, jnp.zeros((), BF16))
    return jnp.dot(ret_ref[k], green, preferred_element_type=F32) + jnp.dot(
        less_ref[k], diff, preferred_element_type=F32
    )


def partial(ret, less, own, wins, brings, first, width, scale, sent=()):
    ratio, rows, _ = ret.shape
    cols = own.shape[-1]
    counts = [len(pieces) for pieces in wins]
    col_devices = lax.axis_size("col")

    def kernel(ret_ref, less_ref, own_ref, *refs):
        outs = refs[len(refs) - (3 if sent else 2) :]
        my_row, my_col = place()
        total, at = None, len(sent)
        for s in range(ratio):
            k = lax.rem(my_row + ratio - s, ratio)
            mine = refs[at : at + counts[s]]
            at += counts[s]
            valid = member(brings[s], my_row * col_devices + my_col)

            def win(i, s=s, mine=mine, valid=valid):
                got = jnp.where(valid, mine[0][i], jnp.zeros((), BF16))
                for ref in mine[1:]:
                    got = got + ref[i]
                if s == 0:
                    got = jnp.where(my_col == my_row // ratio, own_ref[i], got)
                return got

            term = block_term(ret_ref, less_ref, k, win, my_row, my_col, rows, width, first)
            total = term if total is None else total + term
        total = scale * total
        outs[0][...] = total
        outs[1][...] = total.astype(BF16)
        if sent:
            for n in range(len(sent)):
                outs[2][:, n * cols : (n + 1) * cols] = refs[n][...]
            outs[2][:, len(sent) * cols :] = total.astype(BF16)

    shapes = [held((rows, cols), F32), held((rows, cols), BF16)]
    if sent:
        shapes.append(held((rows, (1 + len(sent)) * cols), BF16))
    return pl.pallas_call(
        kernel,
        out_shape=shapes,
        in_specs=[pl.BlockSpec(memory_space=pltpu.VMEM)] * (3 + len(sent) + sum(counts)),
        out_specs=[pl.BlockSpec(memory_space=pltpu.VMEM)] * len(shapes),
        compiler_params=ROOM,
        name="partial",
    )(*map(keep, [ret, less, own, *sent]), *[keep(x) for pieces in wins for x in pieces])


def accumulate(parts, got, beside):
    rows, cols = parts[0].shape
    n = len(parts)
    each = len(got[0])

    def kernel(*refs):
        part_refs, got_refs, beside_refs, out_ref = refs[:n], refs[n : n + n * each], refs[n + n * each : -1], refs[-1]
        for q in range(n):
            here = slice(q * cols, (q + 1) * cols)
            total = part_refs[q][...]
            for ref in got_refs[q * each : (q + 1) * each]:
                total = total + ref[...].astype(F32)
            for ref in beside_refs:
                total = total + ref[:, here].astype(F32)
            out_ref[:, here] = total

    args = [*parts, *[g for group in got for g in group], *beside]
    return pl.pallas_call(
        kernel,
        out_shape=jax.ShapeDtypeStruct((rows, n * cols), F32),
        in_specs=[pl.BlockSpec(memory_space=pltpu.VMEM)] * len(args),
        out_specs=pl.BlockSpec(memory_space=pltpu.VMEM),
        compiler_params=ROOM,
        name="accumulate",
    )(*map(keep, args))


def local(lesser, greater, screened_lesser, screened_greater):
    rows, width = lesser.shape
    row_devices, col_devices = lax.axis_size("row"), lax.axis_size("col")
    ratio = row_devices // col_devices
    scale = float(width * col_devices) ** (-0.5)
    plan, later = routes(row_devices, col_devices)
    chunks = WINDOW // LANES

    def send(x, pairs):
        return lax.ppermute(x, AXES, pairs)

    jobs = [(s, q) for q in range(chunks) for s in range(ratio)]
    packed = pack(lesser, greater, [(s, 0, rows, q * LANES, (q + 1) * LANES) for s, q in jobs])
    ready = dict(zip(jobs, packed))
    hop = {(s, q): send(ready[s, q], plan[s][0]) for s, q in jobs}
    ret, less = sigmas(lesser, greater, screened_lesser, screened_greater)
    if ratio > 1:
        hop[0, 0], ret, less = lax.optimization_barrier((hop[0, 0], ret, less))
    wins = {(s, q): [hop[s, q], send(hop[s, q], plan[s][1])] for s, q in jobs}
    for s, q in jobs:
        if plan[s][2]:
            wins[s, q].append(send(ready[s, q], plan[s][2]))
    brings = [p[3] for p in plan]
    parts, sent, got = [], [], []
    for q in range(chunks):
        mine = [wins[s, q] for s in range(ratio)]
        last = q == chunks - 1
        part, out, *both = partial(
            ret, less, ready[0, q], mine, brings, q * LANES, width, scale, ()
        )
        parts.append(part)
        sent.append(out)
        got.append([send(out, pairs) for pairs in later])
    return accumulate(parts, got, [])


def solution(mesh):
    in_specs = (P("row", "col"),) * 4
    return jax.shard_map(local, mesh=mesh, in_specs=in_specs, out_specs=P("row", "col"), check_vma=False)
```

time: 50.4 us -> 46.6 us (0.925)
  the two profiles are of different devices: /device:TPU:31 before, /device:TPU:27 now
where the time goes in v2:
time: 46.6 us; the launch traced here: 46.2 us
  waiting for transfers between devices  23.4 us (50%)
  starting transfers between devices  16.3 us (35%)
  Pallas kernels  6.35 us (14%)
    ppermute x14, waiting for transfers between devices, send(): return lax.ppermute(x, AXES, pairs)  23.4 us
    ppermute x14, starting transfers between devices, send(): return lax.ppermute(x, AXES, pairs)  16.3 us
    pallas_call x1, Pallas kernels, sigmas(): pl.pallas_call(kernel, out_shape=[held((ratio, rows, rows), BF16)] * 2, i...  2.46 us
    pallas_call x2, Pallas kernels, partial(): pl.pallas_call(kernel, out_shape=shapes, in_specs=[pl.BlockSpec(memory_sp...  1.61 us
    pallas_call x1, Pallas kernels, pack(): pl.pallas_call(kernel, out_shape=[held((2, r1 - r0, c1 - c0), BF16) for _...  1.38 us
  transfers between devices with their start and end apart: 14, of which 4 were waited for; matrix products, arithmetic and copies ran while one was open for 0% of the time, Pallas kernels for 9%

profile of v2, /device:TPU:27, one launch (start us, length us, event | category | flops | bytes accessed | tf_op | source)
XLA Modules:
  0.0 46.2 jit_solution(14554787022739236091)
XLA Ops:
  0.0 1.4 %pack_windows.1 = (bf16[2,512,128]{2,1,0:T(8,128)(2,1)S(1)}, bf16[2,512,128]{2,1,0:T(8,128)(2,1)S(1)}, bf16[2,512,128]{2,1,0:T(8,128)(2,1)S(1)}, bf16[2,512,128]{2,1,0:T(8,128)(2,1)S(1)}) custom-call(bf16[512,1024]{1,0:T(8,128)(2,1)} %refs_0_.1, bf16[512,1024]{1,0:T(8,128)(2,1)} %refs_1_.1), custom_call_target="tpu_custom_call" | custom-call | tf_op jit(solution)/shard_map/pack_windows/pallas_call | solution.py:128
  1.4 0.7 %collective-permute-start = (bf16[2,512,128]{2,1,0:T(8,128)(2,1)S(1)}, bf16[2,512,128]{2,1,0:T(8,128)(2,1)S(1)}, u32[]{:S(2)}, u32[]{:S(2)}) collective-permute-start(bf16[2,512,128]{2,1,0:T(8,128)(2,1)S(1)} %get-tuple-element.18.own_ref), channel_id=1, source_target_pairs={{2,16},{6,20},{10,17},{14,21},{3,0},{7,4},{11,9},{15,13},{1,8},{5,... | collective-permute-start | bytes 786440 | tf_op jit(solution)/shard_map/ppermute | solution.py:275
  2.1 3.2 %collective-permute-start.2 = (bf16[2,512,128]{2,1,0:T(8,128)(2,1)S(1)}, bf16[2,512,128]{2,1,0:T(8,128)(2,1)S(1)}, u32[]{:S(2)}, u32[]{:S(2)}) collective-permute-start(bf16[2,512,128]{2,1,0:T(8,128)(2,1)S(1)} %get-tuple-element.24), channel_id=1, source_target_pairs={{2,20},{6,16},{10,21},{14,17},{3,0},{7,5},{11,9},{15,12},{0,4},{1,... | collective-permute-start | bytes 786440 | tf_op jit(solution)/shard_map/ppermute | solution.py:275
  5.2 0.7 %collective-permute-start.4 = (bf16[2,512,128]{2,1,0:T(8,128)(2,1)S(1)}, bf16[2,512,128]{2,1,0:T(8,128)(2,1)S(1)}, u32[]{:S(2)}, u32[]{:S(2)}) collective-permute-start(bf16[2,512,128]{2,1,0:T(8,128)(2,1)S(1)} %get-tuple-element.26.own_ref), channel_id=1, source_target_pairs={{2,16},{6,20},{10,17},{14,21},{3,0},{7,4},{11,9},{15,13},{1,8},{5,... | collective-permute-start | bytes 786440 | tf_op jit(solution)/shard_map/ppermute | solution.py:275
  5.9 1.3 %collective-permute-start.6 = (bf16[2,512,128]{2,1,0:T(8,128)(2,1)S(1)}, bf16[2,512,128]{2,1,0:T(8,128)(2,1)S(1)}, u32[]{:S(2)}, u32[]{:S(2)}) collective-permute-start(bf16[2,512,128]{2,1,0:T(8,128)(2,1)S(1)} %get-tuple-element.27), channel_id=1, source_target_pairs={{2,20},{6,16},{10,21},{14,17},{3,0},{7,5},{11,9},{15,12},{0,4},{1,... | collective-permute-start | bytes 786440 | tf_op jit(solution)/shard_map/ppermute | solution.py:275
  7.2 2.5 %sigma_blocks.1 = (bf16[2,512,512]{2,1,0:T(8,128)(2,1)S(1)}, bf16[2,512,512]{2,1,0:T(8,128)(2,1)S(1)}) custom-call(bf16[512,1024]{1,0:T(8,128)(2,1)} %refs_0_.1, bf16[512,1024]{1,0:T(8,128)(2,1)} %refs_1_.1, bf16[512,1024]{1,0:T(8,128)(2,1)} %refs_2_.1, bf16[512,1024]{1,0:T(8,128)(2,1)} %refs_3_.1), custom_call_target="tpu_custom_call" | custom-call | tf_op jit(solution)/shard_map/sigma_blocks/pallas_call | solution.py:170
  9.7 0.0 collective-permute-done.refs_0_
  9.7 0.7 %collective-permute-start.1 = (bf16[2,512,128]{2,1,0:T(8,128)(2,1)S(1)}, bf16[2,512,128]{2,1,0:T(8,128)(2,1)S(1)}, u32[]{:S(2)}, u32[]{:S(2)}) collective-permute-start(bf16[2,512,128]{2,1,0:T(8,128)(2,1)S(1)} %collective-permute-done.refs_0_), channel_id=1, source_target_pairs={{0,24},{4,28},{9,25},{13,29}} | collective-permute-start | bytes 786440 | tf_op jit(solution)/shard_map/ppermute | solution.py:275
  10.4 0.0 collective-permute-done.2.refs_2_
  10.4 0.7 %collective-permute-start.3 = (bf16[2,512,128]{2,1,0:T(8,128)(2,1)S(1)}, bf16[2,512,128]{2,1,0:T(8,128)(2,1)S(1)}, u32[]{:S(2)}, u32[]{:S(2)}) collective-permute-start(bf16[2,512,128]{2,1,0:T(8,128)(2,1)S(1)} %collective-permute-done.2.refs_2_), channel_id=1, source_target_pairs={{0,28},{5,24},{9,29},{12,25},{1,12}} | collective-permute-start | bytes 786440 | tf_op jit(solution)/shard_map/ppermute | solution.py:275
  11.1 0.0 collective-permute-done.4.refs_0_
  11.1 0.7 %collective-permute-start.5 = (bf16[2,512,128]{2,1,0:T(8,128)(2,1)S(1)}, bf16[2,512,128]{2,1,0:T(8,128)(2,1)S(1)}, u32[]{:S(2)}, u32[]{:S(2)}) collective-permute-start(bf16[2,512,128]{2,1,0:T(8,128)(2,1)S(1)} %collective-permute-done.4.refs_0_), channel_id=1, source_target_pairs={{0,24},{4,28},{9,25},{13,29}} | collective-permute-start | bytes 786440 | tf_op jit(solution)/shard_map/ppermute | solution.py:275
  11.8 2.3 %collective-permute-done.6.refs_2_ = bf16[2,512,128]{2,1,0:T(8,128)(2,1)S(1)} collective-permute-done((bf16[2,512,128]{2,1,0:T(8,128)(2,1)S(1)}, bf16[2,512,128]{2,1,0:T(8,128)(2,1)S(1)}, u32[]{:S(2)}, u32[]{:S(2)}) %collective-permute-start.6) | collective-permute-done | bytes 262176 | tf_op jit(solution)/shard_map/ppermute | solution.py:275
  14.1 0.7 %collective-permute-start.7 = (bf16[2,512,128]{2,1,0:T(8,128)(2,1)S(1)}, bf16[2,512,128]{2,1,0:T(8,128)(2,1)S(1)}, u32[]{:S(2)}, u32[]{:S(2)}) collective-permute-start(bf16[2,512,128]{2,1,0:T(8,128)(2,1)S(1)} %collective-permute-done.6.refs_2_), channel_id=1, source_target_pairs={{0,28},{5,24},{9,29},{12,25},{1,12}} | collective-permute-start | bytes 786440 | tf_op jit(solution)/shard_map/ppermute | solution.py:275
  14.8 0.0 collective-permute-done.1.refs_1_
  14.8 0.0 collective-permute-done.3.refs_3_
  14.8 0.8 %partial.2 = (f32[512,128]{1,0:T(8,128)S(1)}, bf16[512,128]{1,0:T(8,128)(2,1)S(1)}) custom-call(bf16[2,512,512]{2,1,0:T(8,128)(2,1)S(1)} %get-tuple-element.21.ret_ref, bf16[2,512,512]{2,1,0:T(8,128)(2,1)S(1)} %get-tuple-element.22.less_ref, bf16[2,512,128]{2,1,0:T(8,128)(2,1)S(1)} %get-tuple-element.18.own_ref, ...), custom_call_target="tpu_custom_call" | custom-call | tf_op jit(solution)/shard_map/partial/pallas_call | solution.py:229
  15.6 1.3 %collective-permute-start.8 = (bf16[512,128]{1,0:T(8,128)(2,1)S(1)}, bf16[512,128]{1,0:T(8,128)(2,1)S(1)}, u32[]{:S(2)}, u32[]{:S(2)}) collective-permute-start(bf16[512,128]{1,0:T(8,128)(2,1)S(1)} %get-tuple-element.29), channel_id=1, source_target_pairs={{0,2},{4,6},{8,10},{9,11},{12,14},{13,15},{16,18},{17,19},{20,22},... | collective-permute-start | bytes 393224 | tf_op jit(solution)/shard_map/ppermute | solution.py:275
  16.9 1.3 %collective-permute-start.9 = (bf16[512,128]{1,0:T(8,128)(2,1)S(1)}, bf16[512,128]{1,0:T(8,128)(2,1)S(1)}, u32[]{:S(2)}, u32[]{:S(2)}) collective-permute-start(bf16[512,128]{1,0:T(8,128)(2,1)S(1)} %get-tuple-element.29), channel_id=1, source_target_pairs={{0,3},{4,7},{8,11},{9,10},{12,15},{13,14},{16,19},{17,18},{20,23},... | collective-permute-start | bytes 393224 | tf_op jit(solution)/shard_map/ppermute | solution.py:275
  18.2 1.3 %collective-permute-start.10 = (bf16[512,128]{1,0:T(8,128)(2,1)S(1)}, bf16[512,128]{1,0:T(8,128)(2,1)S(1)}, u32[]{:S(2)}, u32[]{:S(2)}) collective-permute-start(bf16[512,128]{1,0:T(8,128)(2,1)S(1)} %get-tuple-element.29), channel_id=1, source_target_pairs={{0,1},{4,5},{8,9},{12,13},{16,17},{18,19},{20,21},{22,23},{24,25},... | collective-permute-start | bytes 393224 | tf_op jit(solution)/shard_map/ppermute | solution.py:275
  19.5 0.0 collective-permute-done.5.refs_1_
  19.6 0.0 collective-permute-done.7.refs_3_
  19.6 0.8 %partial.3 = (f32[512,128]{1,0:T(8,128)S(1)}, bf16[512,128]{1,0:T(8,128)(2,1)S(1)}) custom-call(bf16[2,512,512]{2,1,0:T(8,128)(2,1)S(1)} %get-tuple-element.21.ret_ref, bf16[2,512,512]{2,1,0:T(8,128)(2,1)S(1)} %get-tuple-element.22.less_ref, bf16[2,512,128]{2,1,0:T(8,128)(2,1)S(1)} %get-tuple-element.26.own_ref, ...), custom_call_target="tpu_custom_call" | custom-call | tf_op jit(solution)/shard_map/partial/pallas_call | solution.py:229
  20.4 1.3 %collective-permute-start.11 = (bf16[512,128]{1,0:T(8,128)(2,1)S(1)}, bf16[512,128]{1,0:T(8,128)(2,1)S(1)}, u32[]{:S(2)}, u32[]{:S(2)}) collective-permute-start(bf16[512,128]{1,0:T(8,128)(2,1)S(1)} %get-tuple-element.30), channel_id=1, source_target_pairs={{0,2},{4,6},{8,10},{9,11},{12,14},{13,15},{16,18},{17,19},{20,22},... | collective-permute-start | bytes 393224 | tf_op jit(solution)/shard_map/ppermute | solution.py:275
  21.7 1.3 %collective-permute-start.12 = (bf16[512,128]{1,0:T(8,128)(2,1)S(1)}, bf16[512,128]{1,0:T(8,128)(2,1)S(1)}, u32[]{:S(2)}, u32[]{:S(2)}) collective-permute-start(bf16[512,128]{1,0:T(8,128)(2,1)S(1)} %get-tuple-element.30), channel_id=1, source_target_pairs={{0,3},{4,7},{8,11},{9,10},{12,15},{13,14},{16,19},{17,18},{20,23},... | collective-permute-start | bytes 393224 | tf_op jit(solution)/shard_map/ppermute | solution.py:275
  23.0 13.4 %collective-permute-done.8.refs_2_ = bf16[512,128]{1,0:T(8,128)(2,1)S(1)} collective-permute-done((bf16[512,128]{1,0:T(8,128)(2,1)S(1)}, bf16[512,128]{1,0:T(8,128)(2,1)S(1)}, u32[]{:S(2)}, u32[]{:S(2)}) %collective-permute-start.8) | collective-permute-done | bytes 131104 | tf_op jit(solution)/shard_map/ppermute | solution.py:275
  36.4 1.3 %collective-permute-start.13 = (bf16[512,128]{1,0:T(8,128)(2,1)S(1)}, bf16[512,128]{1,0:T(8,128)(2,1)S(1)}, u32[]{:S(2)}, u32[]{:S(2)}) collective-permute-start(bf16[512,128]{1,0:T(8,128)(2,1)S(1)} %get-tuple-element.30), channel_id=1, source_target_pairs={{0,1},{4,5},{8,9},{12,13},{16,17},{18,19},{20,21},{22,23},{24,25},... | collective-permute-start | bytes 393224 | tf_op jit(solution)/shard_map/ppermute | solution.py:275
  37.7 0.0 collective-permute-done.10.refs_4_
  37.7 3.8 %collective-permute-done.11.refs_5_ = bf16[512,128]{1,0:T(8,128)(2,1)S(1)} collective-permute-done((bf16[512,128]{1,0:T(8,128)(2,1)S(1)}, bf16[512,128]{1,0:T(8,128)(2,1)S(1)}, u32[]{:S(2)}, u32[]{:S(2)}) %collective-permute-start.11) | collective-permute-done | bytes 131104 | tf_op jit(solution)/shard_map/ppermute | solution.py:275
  41.4 3.9 %collective-permute-done.12.refs_6_ = bf16[512,128]{1,0:T(8,128)(2,1)S(1)} collective-permute-done((bf16[512,128]{1,0:T(8,128)(2,1)S(1)}, bf16[512,128]{1,0:T(8,128)(2,1)S(1)}, u32[]{:S(2)}, u32[]{:S(2)}) %collective-permute-start.12) | collective-permute-done | bytes 131104 | tf_op jit(solution)/shard_map/ppermute | solution.py:275
  45.3 0.0 collective-permute-done.13.refs_7_
  45.3 0.9 %accumulate.1 = f32[512,256]{1,0:T(8,128)} custom-call(f32[512,128]{1,0:T(8,128)S(1)} %get-tuple-element.25.refs_0_, f32[512,128]{1,0:T(8,128)S(1)} %get-tuple-element.28.refs_1_, bf16[512,128]{1,0:T(8,128)(2,1)S(1)} %collective-permute-done.8.refs_2_, bf16[512,128]{1,0:T(8,128)(2,1)S(1)} %collective-permute-done.9.refs_3_, ...), custom_call_target="tpu_custom_call" | custom-call | tf_op jit(solution)/shard_map/accumulate/pallas_call | solution.py:256
  (1 shorter events, 0.0 us)
Async XLA Ops:
  1.4 8.3 %collective-permute-start = (bf16[2,512,128]{2,1,0:T(8,128)(2,1)S(1)}, bf16[2,512,128]{2,1,0:T(8,128)(2,1)S(1)}, u32[]{:S(2)}, u32[]{:S(2)}) collective-permute-start(bf16[2,512,128]{2,1,0:T(8,128)(2,1)S(1)} %get-tuple-element.18.own_ref), channel_id=1, source_target_pairs={{2,16},{6,20},{10,17},{14,21},{3,0},{7,4},{11,9},{15,13},{1,8},{5,... | collective-permute-start | bytes 786440 | tf_op jit(solution)/shard_map/ppermute | solution.py:275
  2.1 8.3 %collective-permute-start.2 = (bf16[2,512,128]{2,1,0:T(8,128)(2,1)S(1)}, bf16[2,512,128]{2,1,0:T(8,128)(2,1)S(1)}, u32[]{:S(2)}, u32[]{:S(2)}) collective-permute-start(bf16[2,512,128]{2,1,0:T(8,128)(2,1)S(1)} %get-tuple-element.24), channel_id=1, source_target_pairs={{2,20},{6,16},{10,21},{14,17},{3,0},{7,5},{11,9},{15,12},{0,4},{1,... | collective-permute-start | bytes 786440 | tf_op jit(solution)/shard_map/ppermute | solution.py:275
  5.2 5.9 %collective-permute-start.4 = (bf16[2,512,128]{2,1,0:T(8,128)(2,1)S(1)}, bf16[2,512,128]{2,1,0:T(8,128)(2,1)S(1)}, u32[]{:S(2)}, u32[]{:S(2)}) collective-permute-start(bf16[2,512,128]{2,1,0:T(8,128)(2,1)S(1)} %get-tuple-element.26.own_ref), channel_id=1, source_target_pairs={{2,16},{6,20},{10,17},{14,21},{3,0},{7,4},{11,9},{15,13},{1,8},{5,... | collective-permute-start | bytes 786440 | tf_op jit(solution)/shard_map/ppermute | solution.py:275
  5.9 8.2 %collective-permute-start.6 = (bf16[2,512,128]{2,1,0:T(8,128)(2,1)S(1)}, bf16[2,512,128]{2,1,0:T(8,128)(2,1)S(1)}, u32[]{:S(2)}, u32[]{:S(2)}) collective-permute-start(bf16[2,512,128]{2,1,0:T(8,128)(2,1)S(1)} %get-tuple-element.27), channel_id=1, source_target_pairs={{2,20},{6,16},{10,21},{14,17},{3,0},{7,5},{11,9},{15,12},{0,4},{1,... | collective-permute-start | bytes 786440 | tf_op jit(solution)/shard_map/ppermute | solution.py:275
  9.7 5.1 %collective-permute-start.1 = (bf16[2,512,128]{2,1,0:T(8,128)(2,1)S(1)}, bf16[2,512,128]{2,1,0:T(8,128)(2,1)S(1)}, u32[]{:S(2)}, u32[]{:S(2)}) collective-permute-start(bf16[2,512,128]{2,1,0:T(8,128)(2,1)S(1)} %collective-permute-done.refs_0_), channel_id=1, source_target_pairs={{0,24},{4,28},{9,25},{13,29}} | collective-permute-start | bytes 786440 | tf_op jit(solution)/shard_map/ppermute | solution.py:275
  10.4 4.4 %collective-permute-start.3 = (bf16[2,512,128]{2,1,0:T(8,128)(2,1)S(1)}, bf16[2,512,128]{2,1,0:T(8,128)(2,1)S(1)}, u32[]{:S(2)}, u32[]{:S(2)}) collective-permute-start(bf16[2,512,128]{2,1,0:T(8,128)(2,1)S(1)} %collective-permute-done.2.refs_2_), channel_id=1, source_target_pairs={{0,28},{5,24},{9,29},{12,25},{1,12}} | collective-permute-start | bytes 786440 | tf_op jit(solution)/shard_map/ppermute | solution.py:275
  11.1 8.4 %collective-permute-start.5 = (bf16[2,512,128]{2,1,0:T(8,128)(2,1)S(1)}, bf16[2,512,128]{2,1,0:T(8,128)(2,1)S(1)}, u32[]{:S(2)}, u32[]{:S(2)}) collective-permute-start(bf16[2,512,128]{2,1,0:T(8,128)(2,1)S(1)} %collective-permute-done.4.refs_0_), channel_id=1, source_target_pairs={{0,24},{4,28},{9,25},{13,29}} | collective-permute-start | bytes 786440 | tf_op jit(solution)/shard_map/ppermute | solution.py:275
  14.1 5.4 %collective-permute-start.7 = (bf16[2,512,128]{2,1,0:T(8,128)(2,1)S(1)}, bf16[2,512,128]{2,1,0:T(8,128)(2,1)S(1)}, u32[]{:S(2)}, u32[]{:S(2)}) collective-permute-start(bf16[2,512,128]{2,1,0:T(8,128)(2,1)S(1)} %collective-permute-done.6.refs_2_), channel_id=1, source_target_pairs={{0,28},{5,24},{9,29},{12,25},{1,12}} | collective-permute-start | bytes 786440 | tf_op jit(solution)/shard_map/ppermute | solution.py:275
  15.6 20.7 %collective-permute-start.8 = (bf16[512,128]{1,0:T(8,128)(2,1)S(1)}, bf16[512,128]{1,0:T(8,128)(2,1)S(1)}, u32[]{:S(2)}, u32[]{:S(2)}) collective-permute-start(bf16[512,128]{1,0:T(8,128)(2,1)S(1)} %get-tuple-element.29), channel_id=1, source_target_pairs={{0,2},{4,6},{8,10},{9,11},{12,14},{13,15},{16,18},{17,19},{20,22},... | collective-permute-start | bytes 393224 | tf_op jit(solution)/shard_map/ppermute | solution.py:275
  16.9 20.7 %collective-permute-start.9 = (bf16[512,128]{1,0:T(8,128)(2,1)S(1)}, bf16[512,128]{1,0:T(8,128)(2,1)S(1)}, u32[]{:S(2)}, u32[]{:S(2)}) collective-permute-start(bf16[512,128]{1,0:T(8,128)(2,1)S(1)} %get-tuple-element.29), channel_id=1, source_target_pairs={{0,3},{4,7},{8,11},{9,10},{12,15},{13,14},{16,19},{17,18},{20,23},... | collective-permute-start | bytes 393224 | tf_op jit(solution)/shard_map/ppermute | solution.py:275
  18.2 19.4 %collective-permute-start.10 = (bf16[512,128]{1,0:T(8,128)(2,1)S(1)}, bf16[512,128]{1,0:T(8,128)(2,1)S(1)}, u32[]{:S(2)}, u32[]{:S(2)}) collective-permute-start(bf16[512,128]{1,0:T(8,128)(2,1)S(1)} %get-tuple-element.29), channel_id=1, source_target_pairs={{0,1},{4,5},{8,9},{12,13},{16,17},{18,19},{20,21},{22,23},{24,25},... | collective-permute-start | bytes 393224 | tf_op jit(solution)/shard_map/ppermute | solution.py:275
  20.4 21.1 %collective-permute-start.11 = (bf16[512,128]{1,0:T(8,128)(2,1)S(1)}, bf16[512,128]{1,0:T(8,128)(2,1)S(1)}, u32[]{:S(2)}, u32[]{:S(2)}) collective-permute-start(bf16[512,128]{1,0:T(8,128)(2,1)S(1)} %get-tuple-element.30), channel_id=1, source_target_pairs={{0,2},{4,6},{8,10},{9,11},{12,14},{13,15},{16,18},{17,19},{20,22},... | collective-permute-start | bytes 393224 | tf_op jit(solution)/shard_map/ppermute | solution.py:275
  21.7 23.6 %collective-permute-start.12 = (bf16[512,128]{1,0:T(8,128)(2,1)S(1)}, bf16[512,128]{1,0:T(8,128)(2,1)S(1)}, u32[]{:S(2)}, u32[]{:S(2)}) collective-permute-start(bf16[512,128]{1,0:T(8,128)(2,1)S(1)} %get-tuple-element.30), channel_id=1, source_target_pairs={{0,3},{4,7},{8,11},{9,10},{12,15},{13,14},{16,19},{17,18},{20,23},... | collective-permute-start | bytes 393224 | tf_op jit(solution)/shard_map/ppermute | solution.py:275
  36.4 9.0 %collective-permute-start.13 = (bf16[512,128]{1,0:T(8,128)(2,1)S(1)}, bf16[512,128]{1,0:T(8,128)(2,1)S(1)}, u32[]{:S(2)}, u32[]{:S(2)}) collective-permute-start(bf16[512,128]{1,0:T(8,128)(2,1)S(1)} %get-tuple-element.30), channel_id=1, source_target_pairs={{0,1},{4,5},{8,9},{12,13},{16,17},{18,19},{20,21},{22,23},{24,25},... | collective-permute-start | bytes 393224 | tf_op jit(solution)/shard_map/ppermute | solution.py:275

commit v3 on v2

--- a/solution.py
+++ b/solution.py
@@ -15,7 +15,7 @@
 ROOM = pltpu.CompilerParams(vmem_limit_bytes=16 * 2**20)
 
 
-def routes(row_devices, col_devices):
+def route(row_devices, col_devices, s, eased):
     ratio = row_devices // col_devices
     half = col_devices // 2
     straight = col_devices - half // 2
@@ -23,63 +23,72 @@
     def at(z, y, g):
         return (z * ratio + y) * col_devices + g
 
-    plan = []
-    for s in range(ratio):
-        first, second, left = [], [], []
-        near, hops = {}, []
+    first, second, left = [], [], []
+    near, hops = {}, []
+    for z in range(col_devices):
+        for y in range(ratio):
+            to = (y + s) % ratio
+            for g in range(z, col_devices):
+                src, dst = at(z, y, g), at(g, to, z)
+                if z < half and g >= straight and not (eased and z % 2):
+                    hops.append((z, y, src, dst))
+                elif z < half <= g:
+                    first.append((src, dst))
+                elif z < g or y < to:
+                    near[dst] = src
+    relays, kept = set(), set()
+    for z, y, src, dst in hops:
+        choice = None
+        for g in range(half):
+            relay = at(z, y, g)
+            if relay in relays or relay in kept:
+                continue
+            if relay not in near:
+                choice = relay
+                break
+            if choice is None and near[relay] not in relays:
+                choice = relay
+        if choice is None:
+            left.append((src, dst))
+            continue
+        relays.add(choice)
+        if choice in near:
+            kept.add(near[choice])
+        first.append((src, choice))
+        second.append((choice, dst))
+    for dst, src in near.items():
+        if dst not in relays and src not in kept:
+            first.append((src, dst))
+        elif dst in relays and src in kept and (src, src) not in first:
+            first.append((src, src))
+            second.append((src, dst))
+        else:
+            left.append((src, dst))
+    brings = {dst for src, dst in first if src != dst and dst not in relays}
+    return first, second, left, brings
+
+
+def onward(row_devices, col_devices):
+    ratio = row_devices // col_devices
+
+    def at(z, y, c):
+        return (z * ratio + y) * col_devices + c
+
+    across = []
+    for d in range(2, col_devices, 2):
+        across.append([])
         for z in range(col_devices):
             for y in range(ratio):
-                to = (y + s) % ratio
-                for g in range(z, col_devices):
-                    src, dst = at(z, y, g), at(g, to, z)
-                    if z < half and g >= straight:
-                        hops.append((z, y, src, dst))
-                    elif z < half <= g:
-                        first.append((src, dst))
-                    elif z < g or y < to:
-                        near[dst] = src
-        relays, kept = set(), set()
-        for z, y, src, dst in hops:
-            choice = None
-            for g in range(half):
-                relay = at(z, y, g)
-                if relay in relays or relay in kept:
-                    continue
-                if relay not in near:
-                    choice = relay
-                    break
-                if choice is None and near[relay] not in relays:
-                    choice = relay
-            if choice is None:
-                left.append((src, dst))
-                continue
-            relays.add(choice)
-            if choice in near:
-                kept.add(near[choice])
-            first.append((src, choice))
-            second.append((choice, dst))
-        for dst, src in near.items():
-            if dst not in relays and src not in kept:
-                first.append((src, dst))
-            elif dst in relays and src in kept and (src, src) not in first:
-                first.append((src, src))
-                second.append((src, dst))
-            else:
-                left.append((src, dst))
-        brings = {dst for src, dst in first if src != dst and dst not in relays}
-        plan.append((first, second, left, brings))
-    later, d = [], 1
-    while d < col_devices:
-        d *= 2
-    for d in [*range(2, d), 1][: d - 1]:
-        pairs = []
-        for z in range(col_devices):
-            for y in range(ratio):
-                for c in range(z + 1):
-                    if c < c ^ d < col_devices:
-                        pairs.append((at(z, y, c), at(z, y, c ^ d)))
-        later.append(pairs)
-    return plan, later
+                for c in range(min(z + 1, col_devices - d)):
+                    across[-1].append((at(z, y, c), at(z, y, c + d)))
+    along = []
+    for z in range(col_devices):
+        for y in range(ratio):
+            for c in range(0, col_devices, 2):
+                along.append((at(z, y, c), at(z, y, c + 1)))
+                if c and z:
+                    along.append((at(z, y, c + 1), at(z, y, c)))
+    return across, along
 
 
 def member(devices, index):
@@ -236,31 +245,46 @@
     )(*map(keep, [ret, less, own, *sent]), *[keep(x) for pieces in wins for x in pieces])
 
 
-def accumulate(parts, got, beside):
-    rows, cols = parts[0].shape
-    n = len(parts)
-    each = len(got[0])
+def chunk_sums(before, part, got):
+    rows, cols = part.shape
+    start = before[0].shape[1] if before else 0
 
     def kernel(*refs):
-        part_refs, got_refs, beside_refs, out_ref = refs[:n], refs[n : n + n * each], refs[n + n * each : -1], refs[-1]
-        for q in range(n):
-            here = slice(q * cols, (q + 1) * cols)
-            total = part_refs[q][...]
-            for ref in got_refs[q * each : (q + 1) * each]:
-                total = total + ref[...].astype(F32)
-            for ref in beside_refs:
-                total = total + ref[:, here].astype(F32)
-            out_ref[:, here] = total
-
-    args = [*parts, *[g for group in got for g in group], *beside]
-    return pl.pallas_call(
-        kernel,
-        out_shape=jax.ShapeDtypeStruct((rows, n * cols), F32),
+        part_ref, got_refs, (total_ref, message_ref) = refs[0], refs[1 : 1 + len(got)], refs[-2:]
+        _, my_col = place()
+        came = jnp.zeros((rows, cols), F32)
+        for ref in got_refs:
+            came = came + ref[...].astype(F32)
+        total = came + part_ref[...]
+        if start:
+            total_ref[:, :start] = refs[-4][...]
+            message_ref[:, :start] = refs[-3][...]
+        total_ref[:, start:] = total
+        message_ref[:, start:] = jnp.where(lax.rem(my_col, 2) == 0, total, came).astype(BF16)
+
+    args = [part, *got, *before]
+    return pl.pallas_call(
+        kernel,
+        out_shape=[held((rows, start + cols), F32), held((rows, start + cols), BF16)],
         in_specs=[pl.BlockSpec(memory_space=pltpu.VMEM)] * len(args),
+        out_specs=[pl.BlockSpec(memory_space=pltpu.VMEM)] * 2,
+        compiler_params=ROOM,
+        name="chunk_sums",
+    )(*map(keep, args))
+
+
+def accumulate(total, came):
+    def kernel(total_ref, came_ref, out_ref):
+        out_ref[...] = total_ref[...] + came_ref[...].astype(F32)
+
+    return pl.pallas_call(
+        kernel,
+        out_shape=jax.ShapeDtypeStruct(total.shape, F32),
+        in_specs=[pl.BlockSpec(memory_space=pltpu.VMEM)] * 2,
         out_specs=pl.BlockSpec(memory_space=pltpu.VMEM),
         compiler_params=ROOM,
         name="accumulate",
-    )(*map(keep, args))
+    )(keep(total), keep(came))
 
 
 def local(lesser, greater, screened_lesser, screened_greater):
@@ -268,35 +292,39 @@
     row_devices, col_devices = lax.axis_size("row"), lax.axis_size("col")
     ratio = row_devices // col_devices
     scale = float(width * col_devices) ** (-0.5)
-    plan, later = routes(row_devices, col_devices)
+    across, along = onward(row_devices, col_devices)
     chunks = WINDOW // LANES
 
     def send(x, pairs):
         return lax.ppermute(x, AXES, pairs)
 
-    jobs = [(s, q) for q in range(chunks) for s in range(ratio)]
+    jobs = [(s, q) for q in range(chunks) for s in reversed(range(ratio))]
     packed = pack(lesser, greater, [(s, 0, rows, q * LANES, (q + 1) * LANES) for s, q in jobs])
     ready = dict(zip(jobs, packed))
-    hop = {(s, q): send(ready[s, q], plan[s][0]) for s, q in jobs}
-    ret, less = sigmas(lesser, greater, screened_lesser, screened_greater)
-    if ratio > 1:
-        hop[0, 0], ret, less = lax.optimization_barrier((hop[0, 0], ret, less))
-    wins = {(s, q): [hop[s, q], send(hop[s, q], plan[s][1])] for s, q in jobs}
+    plan = {job: route(row_devices, col_devices, job[0], n in ()) for n, job in enumerate(jobs)}
+
+    def send(x, pairs):
+        return lax.ppermute(x, AXES, pairs)
+
+    hop = {(s, q): send(ready[s, q], plan[s, q][0]) for s, q in jobs}
+    inputs = (lesser, greater, screened_lesser, screened_greater)
+    tie = jobs[1 % len(jobs)]
+    hop[tie], inputs = lax.optimization_barrier((hop[tie], inputs))
+    ret, less = sigmas(*inputs)
+    tie = jobs[2 % len(jobs)]
+    hop[tie], ret, less = lax.optimization_barrier((hop[tie], ret, less))
+    wins = {(s, q): [hop[s, q], send(hop[s, q], plan[s, q][1])] for s, q in jobs}
     for s, q in jobs:
-        if plan[s][2]:
-            wins[s, q].append(send(ready[s, q], plan[s][2]))
-    brings = [p[3] for p in plan]
-    parts, sent, got = [], [], []
+        if plan[s, q][2]:
+            wins[s, q].append(send(ready[s, q], plan[s, q][2]))
+    sums = ()
     for q in range(chunks):
         mine = [wins[s, q] for s in range(ratio)]
-        last = q == chunks - 1
-        part, out, *both = partial(
-            ret, less, ready[0, q], mine, brings, q * LANES, width, scale, ()
-        )
-        parts.append(part)
-        sent.append(out)
-        got.append([send(out, pairs) for pairs in later])
-    return accumulate(parts, got, [])
+        brings = [plan[s, q][3] for s in range(ratio)]
+        part, out = partial(ret, less, ready[0, q], mine, brings, q * LANES, width, scale)
+        sums = chunk_sums(sums, part, [send(out, pairs) for pairs in across])
+    total, message = sums
+    return accumulate(total, send(message, along))
 
 
 def solution(mesh):

time: 46.6 us -> 44.5 us (0.955)
  the two profiles are of different devices: /device:TPU:27 before, /device:TPU:11 now
where the time goes in v3:
time: 44.5 us; the launch traced here: 44.1 us
  waiting for transfers between devices  21.1 us (47%)
  starting transfers between devices  16.4 us (37%)
  Pallas kernels  6.44 us (14%)
    ppermute x11, waiting for transfers between devices, send(): return lax.ppermute(x, AXES, pairs)  21.1 us
    ppermute x11, starting transfers between devices, send(): return lax.ppermute(x, AXES, pairs)  16.4 us
    pallas_call x1, Pallas kernels, sigmas(): pl.pallas_call(kernel, out_shape=[held((ratio, rows, rows), BF16)] * 2, i...  2.46 us
    pallas_call x2, Pallas kernels, partial(): pl.pallas_call(kernel, out_shape=shapes, in_specs=[pl.BlockSpec(memory_sp...  1.62 us
    pallas_call x1, Pallas kernels, pack(): pl.pallas_call(kernel, out_shape=[held((2, r1 - r0, c1 - c0), BF16) for _...  1.38 us
  transfers between devices with their start and end apart: 11, of which 4 were waited for; matrix products, arithmetic and copies ran while one was open for 0% of the time, Pallas kernels for 9%

profile of v3, /device:TPU:11, one launch (start us, length us, event | category | flops | bytes accessed | tf_op | source)
XLA Modules:
  0.0 44.1 jit_solution(9412845064857630150)
XLA Ops:
  0.0 1.4 %pack_windows.1 = (bf16[2,512,128]{2,1,0:T(8,128)(2,1)S(1)}, bf16[2,512,128]{2,1,0:T(8,128)(2,1)S(1)}, bf16[2,512,128]{2,1,0:T(8,128)(2,1)S(1)}, bf16[2,512,128]{2,1,0:T(8,128)(2,1)S(1)}) custom-call(bf16[512,1024]{1,0:T(8,128)(2,1)} %refs_0_, bf16[512,1024]{1,0:T(8,128)(2,1)} %refs_1_), custom_call_target="tpu_custom_call" | custom-call | tf_op jit(solution)/shard_map/pack_windows/pallas_call | solution.py:137
  1.4 2.2 %collective-permute-start.1 = (bf16[2,512,128]{2,1,0:T(8,128)(2,1)S(1)}, bf16[2,512,128]{2,1,0:T(8,128)(2,1)S(1)}, u32[]{:S(2)}, u32[]{:S(2)}) collective-permute-start(bf16[2,512,128]{2,1,0:T(8,128)(2,1)S(1)} %get-tuple-element.28.own_ref), channel_id=1, source_target_pairs={{2,16},{6,20},{10,17},{14,21},{3,0},{7,4},{11,9},{15,13},{1,8},{5,... | collective-permute-start | bytes 786440 | tf_op jit(solution)/shard_map/ppermute | solution.py:307
  3.6 1.3 %collective-permute-start.7 = (bf16[2,512,128]{2,1,0:T(8,128)(2,1)S(1)}, bf16[2,512,128]{2,1,0:T(8,128)(2,1)S(1)}, u32[]{:S(2)}, u32[]{:S(2)}) collective-permute-start(bf16[2,512,128]{2,1,0:T(8,128)(2,1)S(1)} %get-tuple-element.42), channel_id=1, source_target_pairs={{2,20},{6,16},{10,21},{14,17},{3,0},{7,5},{11,9},{15,12},{0,4},{1,... | collective-permute-start | bytes 786440 | tf_op jit(solution)/shard_map/ppermute | solution.py:307
  4.9 3.1 %collective-permute-start = (bf16[2,512,128]{2,1,0:T(8,128)(2,1)S(1)}, bf16[2,512,128]{2,1,0:T(8,128)(2,1)S(1)}, u32[]{:S(2)}, u32[]{:S(2)}) collective-permute-start(bf16[2,512,128]{2,1,0:T(8,128)(2,1)S(1)} %get-tuple-element.27), channel_id=1, source_target_pairs={{2,20},{6,16},{10,21},{14,17},{3,0},{7,5},{11,9},{15,12},{0,4},{1,... | collective-permute-start | bytes 786440 | tf_op jit(solution)/shard_map/ppermute | solution.py:307
  8.0 1.9 %collective-permute-start.2 = (bf16[2,512,128]{2,1,0:T(8,128)(2,1)S(1)}, bf16[2,512,128]{2,1,0:T(8,128)(2,1)S(1)}, u32[]{:S(2)}, u32[]{:S(2)}) collective-permute-start(bf16[2,512,128]{2,1,0:T(8,128)(2,1)S(1)} %get-tuple-element.37.own_ref), channel_id=1, source_target_pairs={{2,16},{6,20},{10,17},{14,21},{3,0},{7,4},{11,9},{15,13},{1,8},{5,... | collective-permute-start | bytes 786440 | tf_op jit(solution)/shard_map/ppermute | solution.py:307
  10.0 0.0 collective-permute-done.1.refs_0_
  10.0 0.7 %collective-permute-start.6 = (bf16[2,512,128]{2,1,0:T(8,128)(2,1)S(1)}, bf16[2,512,128]{2,1,0:T(8,128)(2,1)S(1)}, u32[]{:S(2)}, u32[]{:S(2)}) collective-permute-start(bf16[2,512,128]{2,1,0:T(8,128)(2,1)S(1)} %collective-permute-done.1.refs_0_), channel_id=1, source_target_pairs={{0,24},{4,28},{9,25},{13,29}} | collective-permute-start | bytes 786440 | tf_op jit(solution)/shard_map/ppermute | solution.py:307
  10.6 2.5 %sigma_blocks.1 = (bf16[2,512,512]{2,1,0:T(8,128)(2,1)S(1)}, bf16[2,512,512]{2,1,0:T(8,128)(2,1)S(1)}) custom-call(bf16[512,1024]{1,0:T(8,128)(2,1)} %refs_0_, bf16[512,1024]{1,0:T(8,128)(2,1)} %refs_1_, bf16[512,1024]{1,0:T(8,128)(2,1)} %refs_2_, bf16[512,1024]{1,0:T(8,128)(2,1)} %refs_3_), custom_call_target="tpu_custom_call" | custom-call | tf_op jit(solution)/shard_map/sigma_blocks/pallas_call | solution.py:179
  13.1 0.0 collective-permute-done.7.refs_2_
  13.1 0.7 %collective-permute-start.8 = (bf16[2,512,128]{2,1,0:T(8,128)(2,1)S(1)}, bf16[2,512,128]{2,1,0:T(8,128)(2,1)S(1)}, u32[]{:S(2)}, u32[]{:S(2)}) collective-permute-start(bf16[2,512,128]{2,1,0:T(8,128)(2,1)S(1)} %collective-permute-done.7.refs_2_), channel_id=1, source_target_pairs={{0,28},{5,24},{9,29},{12,25},{1,12}} | collective-permute-start | bytes 786440 | tf_op jit(solution)/shard_map/ppermute | solution.py:307
  13.8 0.0 collective-permute-done.refs_2_
  13.8 0.7 %collective-permute-start.4 = (bf16[2,512,128]{2,1,0:T(8,128)(2,1)S(1)}, bf16[2,512,128]{2,1,0:T(8,128)(2,1)S(1)}, u32[]{:S(2)}, u32[]{:S(2)}) collective-permute-start(bf16[2,512,128]{2,1,0:T(8,128)(2,1)S(1)} %collective-permute-done.refs_2_), channel_id=1, source_target_pairs={{0,28},{5,24},{9,29},{12,25},{1,12}} | collective-permute-start | bytes 786440 | tf_op jit(solution)/shard_map/ppermute | solution.py:307
  14.5 0.8 %collective-permute-done.2.refs_0_ = bf16[2,512,128]{2,1,0:T(8,128)(2,1)S(1)} collective-permute-done((bf16[2,512,128]{2,1,0:T(8,128)(2,1)S(1)}, bf16[2,512,128]{2,1,0:T(8,128)(2,1)S(1)}, u32[]{:S(2)}, u32[]{:S(2)}) %collective-permute-start.2) | collective-permute-done | bytes 262176 | tf_op jit(solution)/shard_map/ppermute | solution.py:307
  15.3 0.7 %collective-permute-start.3 = (bf16[2,512,128]{2,1,0:T(8,128)(2,1)S(1)}, bf16[2,512,128]{2,1,0:T(8,128)(2,1)S(1)}, u32[]{:S(2)}, u32[]{:S(2)}) collective-permute-start(bf16[2,512,128]{2,1,0:T(8,128)(2,1)S(1)} %collective-permute-done.2.refs_0_), channel_id=1, source_target_pairs={{0,24},{4,28},{9,25},{13,29}} | collective-permute-start | bytes 786440 | tf_op jit(solution)/shard_map/ppermute | solution.py:307
  16.0 0.0 collective-permute-done.6.refs_1_
  16.0 0.0 collective-permute-done.8.refs_3_
  16.0 0.8 %partial.3 = (f32[512,128]{1,0:T(8,128)S(1)}, bf16[512,128]{1,0:T(8,128)(2,1)S(1)}) custom-call(bf16[2,512,512]{2,1,0:T(8,128)(2,1)S(1)} %get-tuple-element.35.ret_ref, bf16[2,512,512]{2,1,0:T(8,128)(2,1)S(1)} %get-tuple-element.36.less_ref, bf16[2,512,128]{2,1,0:T(8,128)(2,1)S(1)} %get-tuple-element.28.own_ref, ...), custom_call_target="tpu_custom_call" | custom-call | tf_op jit(solution)/shard_map/partial/pallas_call | solution.py:238
  16.8 1.3 %collective-permute-start.9 = (bf16[512,128]{1,0:T(8,128)(2,1)S(1)}, bf16[512,128]{1,0:T(8,128)(2,1)S(1)}, u32[]{:S(2)}, u32[]{:S(2)}) collective-permute-start(bf16[512,128]{1,0:T(8,128)(2,1)S(1)} %get-tuple-element.44), channel_id=1, source_target_pairs={{0,2},{4,6},{8,10},{9,11},{12,14},{13,15},{16,18},{17,19},{20,22},... | collective-permute-start | bytes 393224 | tf_op jit(solution)/shard_map/ppermute | solution.py:307
  18.1 0.0 collective-permute-done.4.refs_3_
  18.1 0.0 collective-permute-done.3.refs_1_
  18.1 0.8 %partial.2 = (f32[512,128]{1,0:T(8,128)S(1)}, bf16[512,128]{1,0:T(8,128)(2,1)S(1)}) custom-call(bf16[2,512,512]{2,1,0:T(8,128)(2,1)S(1)} %get-tuple-element.35.ret_ref, bf16[2,512,512]{2,1,0:T(8,128)(2,1)S(1)} %get-tuple-element.36.less_ref, bf16[2,512,128]{2,1,0:T(8,128)(2,1)S(1)} %get-tuple-element.37.own_ref, ...), custom_call_target="tpu_custom_call" | custom-call | tf_op jit(solution)/shard_map/partial/pallas_call | solution.py:238
  18.9 1.3 %collective-permute-start.5 = (bf16[512,128]{1,0:T(8,128)(2,1)S(1)}, bf16[512,128]{1,0:T(8,128)(2,1)S(1)}, u32[]{:S(2)}, u32[]{:S(2)}) collective-permute-start(bf16[512,128]{1,0:T(8,128)(2,1)S(1)} %get-tuple-element.40), channel_id=1, source_target_pairs={{0,2},{4,6},{8,10},{9,11},{12,14},{13,15},{16,18},{17,19},{20,22},... | collective-permute-start | bytes 393224 | tf_op jit(solution)/shard_map/ppermute | solution.py:307
  20.2 8.8 %collective-permute-done.9.refs_1_ = bf16[512,128]{1,0:T(8,128)(2,1)S(1)} collective-permute-done((bf16[512,128]{1,0:T(8,128)(2,1)S(1)}, bf16[512,128]{1,0:T(8,128)(2,1)S(1)}, u32[]{:S(2)}, u32[]{:S(2)}) %collective-permute-start.9) | collective-permute-done | bytes 131104 | tf_op jit(solution)/shard_map/ppermute | solution.py:307
  29.1 0.1 chunk_sums.2
  29.1 10.3 %collective-permute-done.5.refs_1_ = bf16[512,128]{1,0:T(8,128)(2,1)S(1)} collective-permute-done((bf16[512,128]{1,0:T(8,128)(2,1)S(1)}, bf16[512,128]{1,0:T(8,128)(2,1)S(1)}, u32[]{:S(2)}, u32[]{:S(2)}) %collective-permute-start.5) | collective-permute-done | bytes 131104 | tf_op jit(solution)/shard_map/ppermute | solution.py:307
  39.4 0.1 chunk_sums.3
  39.5 2.6 %collective-permute-start.10 = (bf16[512,256]{1,0:T(8,128)(2,1)S(1)}, bf16[512,256]{1,0:T(8,128)(2,1)S(1)}, u32[]{:S(2)}, u32[]{:S(2)}) collective-permute-start(bf16[512,256]{1,0:T(8,128)(2,1)S(1)} %get-tuple-element.48), channel_id=1, source_target_pairs={{0,1},{2,3},{4,5},{6,7},{8,9},{10,11},{11,10},{12,13},{14,15},{15,... | collective-permute-start | bytes 786440 | tf_op jit(solution)/shard_map/ppermute | solution.py:307
  42.1 1.1 %collective-permute-done.10.came_ref = bf16[512,256]{1,0:T(8,128)(2,1)S(1)} collective-permute-done((bf16[512,256]{1,0:T(8,128)(2,1)S(1)}, bf16[512,256]{1,0:T(8,128)(2,1)S(1)}, u32[]{:S(2)}, u32[]{:S(2)}) %collective-permute-start.10) | collective-permute-done | bytes 262176 | tf_op jit(solution)/shard_map/ppermute | solution.py:307
  43.3 0.8 %accumulate.1 = f32[512,256]{1,0:T(8,128)} custom-call(f32[512,256]{1,0:T(8,128)S(1)} %get-tuple-element.47.total_ref, bf16[512,256]{1,0:T(8,128)(2,1)S(1)} %collective-permute-done.10.came_ref), custom_call_target="tpu_custom_call" | custom-call | tf_op jit(solution)/shard_map/accumulate/pallas_call | solution.py:280
Async XLA Ops:
  1.4 8.6 %collective-permute-start.1 = (bf16[2,512,128]{2,1,0:T(8,128)(2,1)S(1)}, bf16[2,512,128]{2,1,0:T(8,128)(2,1)S(1)}, u32[]{:S(2)}, u32[]{:S(2)}) collective-permute-start(bf16[2,512,128]{2,1,0:T(8,128)(2,1)S(1)} %get-tuple-element.28.own_ref), channel_id=1, source_target_pairs={{2,16},{6,20},{10,17},{14,21},{3,0},{7,4},{11,9},{15,13},{1,8},{5,... | collective-permute-start | bytes 786440 | tf_op jit(solution)/shard_map/ppermute | solution.py:307
  3.6 9.5 %collective-permute-start.7 = (bf16[2,512,128]{2,1,0:T(8,128)(2,1)S(1)}, bf16[2,512,128]{2,1,0:T(8,128)(2,1)S(1)}, u32[]{:S(2)}, u32[]{:S(2)}) collective-permute-start(bf16[2,512,128]{2,1,0:T(8,128)(2,1)S(1)} %get-tuple-element.42), channel_id=1, source_target_pairs={{2,20},{6,16},{10,21},{14,17},{3,0},{7,5},{11,9},{15,12},{0,4},{1,... | collective-permute-start | bytes 786440 | tf_op jit(solution)/shard_map/ppermute | solution.py:307
  4.9 8.9 %collective-permute-start = (bf16[2,512,128]{2,1,0:T(8,128)(2,1)S(1)}, bf16[2,512,128]{2,1,0:T(8,128)(2,1)S(1)}, u32[]{:S(2)}, u32[]{:S(2)}) collective-permute-start(bf16[2,512,128]{2,1,0:T(8,128)(2,1)S(1)} %get-tuple-element.27), channel_id=1, source_target_pairs={{2,20},{6,16},{10,21},{14,17},{3,0},{7,5},{11,9},{15,12},{0,4},{1,... | collective-permute-start | bytes 786440 | tf_op jit(solution)/shard_map/ppermute | solution.py:307
  8.0 7.3 %collective-permute-start.2 = (bf16[2,512,128]{2,1,0:T(8,128)(2,1)S(1)}, bf16[2,512,128]{2,1,0:T(8,128)(2,1)S(1)}, u32[]{:S(2)}, u32[]{:S(2)}) collective-permute-start(bf16[2,512,128]{2,1,0:T(8,128)(2,1)S(1)} %get-tuple-element.37.own_ref), channel_id=1, source_target_pairs={{2,16},{6,20},{10,17},{14,21},{3,0},{7,4},{11,9},{15,13},{1,8},{5,... | collective-permute-start | bytes 786440 | tf_op jit(solution)/shard_map/ppermute | solution.py:307
  10.0 6.0 %collective-permute-start.6 = (bf16[2,512,128]{2,1,0:T(8,128)(2,1)S(1)}, bf16[2,512,128]{2,1,0:T(8,128)(2,1)S(1)}, u32[]{:S(2)}, u32[]{:S(2)}) collective-permute-start(bf16[2,512,128]{2,1,0:T(8,128)(2,1)S(1)} %collective-permute-done.1.refs_0_), channel_id=1, source_target_pairs={{0,24},{4,28},{9,25},{13,29}} | collective-permute-start | bytes 786440 | tf_op jit(solution)/shard_map/ppermute | solution.py:307
  13.1 2.8 %collective-permute-start.8 = (bf16[2,512,128]{2,1,0:T(8,128)(2,1)S(1)}, bf16[2,512,128]{2,1,0:T(8,128)(2,1)S(1)}, u32[]{:S(2)}, u32[]{:S(2)}) collective-permute-start(bf16[2,512,128]{2,1,0:T(8,128)(2,1)S(1)} %collective-permute-done.7.refs_2_), channel_id=1, source_target_pairs={{0,28},{5,24},{9,29},{12,25},{1,12}} | collective-permute-start | bytes 786440 | tf_op jit(solution)/shard_map/ppermute | solution.py:307
  13.8 4.3 %collective-permute-start.4 = (bf16[2,512,128]{2,1,0:T(8,128)(2,1)S(1)}, bf16[2,512,128]{2,1,0:T(8,128)(2,1)S(1)}, u32[]{:S(2)}, u32[]{:S(2)}) collective-permute-start(bf16[2,512,128]{2,1,0:T(8,128)(2,1)S(1)} %collective-permute-done.refs_2_), channel_id=1, source_target_pairs={{0,28},{5,24},{9,29},{12,25},{1,12}} | collective-permute-start | bytes 786440 | tf_op jit(solution)/shard_map/ppermute | solution.py:307
  15.3 2.8 %collective-permute-start.3 = (bf16[2,512,128]{2,1,0:T(8,128)(2,1)S(1)}, bf16[2,512,128]{2,1,0:T(8,128)(2,1)S(1)}, u32[]{:S(2)}, u32[]{:S(2)}) collective-permute-start(bf16[2,512,128]{2,1,0:T(8,128)(2,1)S(1)} %collective-permute-done.2.refs_0_), channel_id=1, source_target_pairs={{0,24},{4,28},{9,25},{13,29}} | collective-permute-start | bytes 786440 | tf_op jit(solution)/shard_map/ppermute | solution.py:307
  16.8 12.3 %collective-permute-start.9 = (bf16[512,128]{1,0:T(8,128)(2,1)S(1)}, bf16[512,128]{1,0:T(8,128)(2,1)S(1)}, u32[]{:S(2)}, u32[]{:S(2)}) collective-permute-start(bf16[512,128]{1,0:T(8,128)(2,1)S(1)} %get-tuple-element.44), channel_id=1, source_target_pairs={{0,2},{4,6},{8,10},{9,11},{12,14},{13,15},{16,18},{17,19},{20,22},... | collective-permute-start | bytes 393224 | tf_op jit(solution)/shard_map/ppermute | solution.py:307
  18.9 20.5 %collective-permute-start.5 = (bf16[512,128]{1,0:T(8,128)(2,1)S(1)}, bf16[512,128]{1,0:T(8,128)(2,1)S(1)}, u32[]{:S(2)}, u32[]{:S(2)}) collective-permute-start(bf16[512,128]{1,0:T(8,128)(2,1)S(1)} %get-tuple-element.40), channel_id=1, source_target_pairs={{0,2},{4,6},{8,10},{9,11},{12,14},{13,15},{16,18},{17,19},{20,22},... | collective-permute-start | bytes 393224 | tf_op jit(solution)/shard_map/ppermute | solution.py:307
  39.5 3.7 %collective-permute-start.10 = (bf16[512,256]{1,0:T(8,128)(2,1)S(1)}, bf16[512,256]{1,0:T(8,128)(2,1)S(1)}, u32[]{:S(2)}, u32[]{:S(2)}) collective-permute-start(bf16[512,256]{1,0:T(8,128)(2,1)S(1)} %get-tuple-element.48), channel_id=1, source_target_pairs={{0,1},{2,3},{4,5},{6,7},{8,9},{10,11},{11,10},{12,13},{14,15},{15,... | collective-permute-start | bytes 786440 | tf_op jit(solution)/shard_map/ppermute | solution.py:307

commit v4 on v3

--- a/solution.py
+++ b/solution.py
@@ -74,21 +74,16 @@
     def at(z, y, c):
         return (z * ratio + y) * col_devices + c
 
-    across = []
+    rows = [(z, y) for z in range(col_devices) for y in range(ratio)]
+    across, askew = [], []
     for d in range(2, col_devices, 2):
-        across.append([])
-        for z in range(col_devices):
-            for y in range(ratio):
-                for c in range(min(z + 1, col_devices - d)):
-                    across[-1].append((at(z, y, c), at(z, y, c + d)))
-    along = []
-    for z in range(col_devices):
-        for y in range(ratio):
-            for c in range(0, col_devices, 2):
-                along.append((at(z, y, c), at(z, y, c + 1)))
-                if c and z:
-                    along.append((at(z, y, c + 1), at(z, y, c)))
-    return across, along
+        sources = [(z, y, c) for z, y in rows for c in range(min(z + 1, col_devices - d))]
+        across.append([(at(z, y, c), at(z, y, c + d)) for z, y, c in sources])
+        askew.append([(at(z, y, c), at(z, y, (c + d) ^ 1)) for z, y, c in sources])
+    beside = [(at(z, y, c), at(z, y, c + 1)) for z, y in rows for c in range(0, min(z + 1, col_devices), 2)]
+    along = [(at(z, y, c), at(z, y, c + 1)) for z, y in rows for c in range(0, col_devices, 2)]
+    along += [(at(z, y, c + 1), at(z, y, c)) for z, y in rows for c in range(2, col_devices, 2) if z]
+    return across, askew, along, beside
 
 
 def member(devices, index):
@@ -148,11 +143,11 @@
 def sigmas(lesser, greater, screened_lesser, screened_greater):
     rows, width = lesser.shape
     ratio = width // rows
-    steps = 4
+    steps = 8
     tile = rows // steps
 
     def kernel(*refs):
-        ins, (ret_ref, out_ref), bufs, sem = refs[:4], refs[4:6], refs[6:10], refs[10]
+        ins, both_ref, bufs, sem = refs[:4], refs[4], refs[5:9], refs[9]
         my_row, my_col = place()
         loads = []
         for i in range(steps):
@@ -172,65 +167,72 @@
                 prod_less = less * wless
                 later = my_row * rows + i * tile + lax.broadcasted_iota(jnp.int32, (tile, rows), 0)
                 inner = my_col * width + k * rows + lax.broadcasted_iota(jnp.int32, (tile, rows), 1)
-                ret_ref[k, at] = jnp.where(inner <= later, great * wgreat - prod_less, 0.0).astype(BF16)
-                out_ref[k, at] = prod_less.astype(BF16)
+                both_ref[k, at, :rows] = jnp.where(inner <= later, great * wgreat - prod_less, 0.0).astype(BF16)
+                both_ref[k, at, rows:] = prod_less.astype(BF16)
 
     args = (lesser, greater, screened_lesser, screened_greater)
     return pl.pallas_call(
         kernel,
-        out_shape=[held((ratio, rows, rows), BF16)] * 2,
+        out_shape=held((ratio, rows, 2 * rows), BF16),
         in_specs=[pl.BlockSpec(memory_space=pl.ANY)] * 4,
-        out_specs=[pl.BlockSpec(memory_space=pltpu.VMEM)] * 2,
+        out_specs=pl.BlockSpec(memory_space=pltpu.VMEM),
         scratch_shapes=[pltpu.VMEM((rows, width), BF16)] * 4 + [pltpu.SemaphoreType.DMA((4 * steps,))],
         compiler_params=ROOM,
         name="sigma_blocks",
     )(*(pltpu.with_memory_space_constraint(x, pltpu.HBM) for x in args))
 
 
-def block_term(ret_ref, less_ref, k, win, my_row, my_col, rows, width, first):
+def block_term(both_ref, k, win, my_row, my_col, rows, width, first):
     green, great = win(0), win(1)
     diff = (green.astype(F32) - great.astype(F32)).astype(BF16)
     inner = my_col * width + k * rows + lax.broadcasted_iota(jnp.int32, diff.shape, 0)
     times = my_row * rows + first + lax.broadcasted_iota(jnp.int32, diff.shape, 1)
     diff = jnp.where(inner <= times, diff, jnp.zeros((), BF16))
-    return jnp.dot(ret_ref[k], green, preferred_element_type=F32) + jnp.dot(
-        less_ref[k], diff, preferred_element_type=F32
-    )
-
-
-def partial(ret, less, own, wins, brings, first, width, scale, sent=()):
-    ratio, rows, _ = ret.shape
+    return jnp.dot(both_ref[k], jnp.concatenate([green, diff], axis=0), preferred_element_type=F32)
+
+
+def partial(both, own, wins, brings, first, width, scale, sent=()):
+    ratio, rows, _ = both.shape
     cols = own.shape[-1]
     counts = [len(pieces) for pieces in wins]
     col_devices = lax.axis_size("col")
 
-    def kernel(ret_ref, less_ref, own_ref, *refs):
+    def kernel(both_ref, own_ref, *refs):
         outs = refs[len(refs) - (3 if sent else 2) :]
         my_row, my_col = place()
-        total, at = None, len(sent)
-        for s in range(ratio):
-            k = lax.rem(my_row + ratio - s, ratio)
-            mine = refs[at : at + counts[s]]
-            at += counts[s]
-            valid = member(brings[s], my_row * col_devices + my_col)
-
-            def win(i, s=s, mine=mine, valid=valid):
-                got = jnp.where(valid, mine[0][i], jnp.zeros((), BF16))
-                for ref in mine[1:]:
-                    got = got + ref[i]
-                if s == 0:
-                    got = jnp.where(my_col == my_row // ratio, own_ref[i], got)
-                return got
-
-            term = block_term(ret_ref, less_ref, k, win, my_row, my_col, rows, width, first)
-            total = term if total is None else total + term
-        total = scale * total
-        outs[0][...] = total
-        outs[1][...] = total.astype(BF16)
-        if sent:
-            for n in range(len(sent)):
-                outs[2][:, n * cols : (n + 1) * cols] = refs[n][...]
-            outs[2][:, len(sent) * cols :] = total.astype(BF16)
+        some = my_col <= my_row // ratio
+
+        @pl.when(some)
+        def _():
+            total, at = None, len(sent)
+            for s in range(ratio):
+                k = lax.rem(my_row + ratio - s, ratio)
+                mine = refs[at : at + counts[s]]
+                at += counts[s]
+                valid = member(brings[s], my_row * col_devices + my_col)
+
+                def win(i, s=s, mine=mine, valid=valid):
+                    got = jnp.where(valid, mine[0][i], jnp.zeros((), BF16))
+                    for ref in mine[1:]:
+                        got = got + ref[i]
+                    if s == 0:
+                        got = jnp.where(my_col == my_row // ratio, own_ref[i], got)
+                    return got
+
+                term = block_term(both_ref, k, win, my_row, my_col, rows, width, first)
+                total = term if total is None else total + term
+            total = scale * total
+            outs[0][...] = total
+            outs[1][...] = total.astype(BF16)
+            if sent:
+                for n in range(len(sent)):
+                    outs[2][:, n * cols : (n + 1) * cols] = refs[n][...]
+                outs[2][:, len(sent) * cols :] = total.astype(BF16)
+
+        @pl.when(jnp.logical_not(some))
+        def _():
+            for ref in outs:
+                ref[...] = jnp.zeros(ref.shape, ref.dtype)
 
     shapes = [held((rows, cols), F32), held((rows, cols), BF16)]
     if sent:
@@ -238,34 +240,27 @@
     return pl.pallas_call(
         kernel,
         out_shape=shapes,
-        in_specs=[pl.BlockSpec(memory_space=pltpu.VMEM)] * (3 + len(sent) + sum(counts)),
+        in_specs=[pl.BlockSpec(memory_space=pltpu.VMEM)] * (2 + len(sent) + sum(counts)),
         out_specs=[pl.BlockSpec(memory_space=pltpu.VMEM)] * len(shapes),
         compiler_params=ROOM,
         name="partial",
-    )(*map(keep, [ret, less, own, *sent]), *[keep(x) for pieces in wins for x in pieces])
-
-
-def chunk_sums(before, part, got):
-    rows, cols = part.shape
-    start = before[0].shape[1] if before else 0
-
-    def kernel(*refs):
-        part_ref, got_refs, (total_ref, message_ref) = refs[0], refs[1 : 1 + len(got)], refs[-2:]
+    )(*map(keep, [both, own, *sent]), *[keep(x) for pieces in wins for x in pieces])
+
+
+def chunk_sums(part, got):
+    def kernel(part_ref, *refs):
         _, my_col = place()
-        came = jnp.zeros((rows, cols), F32)
-        for ref in got_refs:
+        came = jnp.zeros(part_ref.shape, F32)
+        for ref in refs[:-2]:
             came = came + ref[...].astype(F32)
         total = came + part_ref[...]
-        if start:
-            total_ref[:, :start] = refs[-4][...]
-            message_ref[:, :start] = refs[-3][...]
-        total_ref[:, start:] = total
-        message_ref[:, start:] = jnp.where(lax.rem(my_col, 2) == 0, total, came).astype(BF16)
-
-    args = [part, *got, *before]
-    return pl.pallas_call(
-        kernel,
-        out_shape=[held((rows, start + cols), F32), held((rows, start + cols), BF16)],
+        refs[-2][...] = total
+        refs[-1][...] = jnp.where(lax.rem(my_col, 2) == 0, total, came).astype(BF16)
+
+    args = [part, *got]
+    return pl.pallas_call(
+        kernel,
+        out_shape=[held(part.shape, F32), held(part.shape, BF16)],
         in_specs=[pl.BlockSpec(memory_space=pltpu.VMEM)] * len(args),
         out_specs=[pl.BlockSpec(memory_space=pltpu.VMEM)] * 2,
         compiler_params=ROOM,
@@ -273,18 +268,22 @@
     )(*map(keep, args))
 
 
-def accumulate(total, came):
-    def kernel(total_ref, came_ref, out_ref):
-        out_ref[...] = total_ref[...] + came_ref[...].astype(F32)
-
-    return pl.pallas_call(
-        kernel,
-        out_shape=jax.ShapeDtypeStruct(total.shape, F32),
-        in_specs=[pl.BlockSpec(memory_space=pltpu.VMEM)] * 2,
+def accumulate(totals, came):
+    rows, cols = totals[0].shape
+    n = len(totals)
+
+    def kernel(*refs):
+        for q in range(n):
+            refs[-1][:, q * cols : (q + 1) * cols] = refs[q][...] + refs[n + q][...].astype(F32)
+
+    return pl.pallas_call(
+        kernel,
+        out_shape=jax.ShapeDtypeStruct((rows, n * cols), F32),
+        in_specs=[pl.BlockSpec(memory_space=pltpu.VMEM)] * (2 * n),
         out_specs=pl.BlockSpec(memory_space=pltpu.VMEM),
         compiler_params=ROOM,
         name="accumulate",
-    )(keep(total), keep(came))
+    )(*map(keep, [*totals, *came]))
 
 
 def local(lesser, greater, screened_lesser, screened_greater):
@@ -292,13 +291,13 @@
     row_devices, col_devices = lax.axis_size("row"), lax.axis_size("col")
     ratio = row_devices // col_devices
     scale = float(width * col_devices) ** (-0.5)
-    across, along = onward(row_devices, col_devices)
+    across, askew, along, beside = onward(row_devices, col_devices)
     chunks = WINDOW // LANES
 
     def send(x, pairs):
         return lax.ppermute(x, AXES, pairs)
 
-    jobs = [(s, q) for q in range(chunks) for s in reversed(range(ratio))]
+    jobs = [(s, q) for q in range(chunks) for s in range(ratio)]
     packed = pack(lesser, greater, [(s, 0, rows, q * LANES, (q + 1) * LANES) for s, q in jobs])
     ready = dict(zip(jobs, packed))
     plan = {job: route(row_devices, col_devices, job[0], n in ()) for n, job in enumerate(jobs)}
@@ -308,23 +307,26 @@
 
     hop = {(s, q): send(ready[s, q], plan[s, q][0]) for s, q in jobs}
     inputs = (lesser, greater, screened_lesser, screened_greater)
-    tie = jobs[1 % len(jobs)]
-    hop[tie], inputs = lax.optimization_barrier((hop[tie], inputs))
-    ret, less = sigmas(*inputs)
-    tie = jobs[2 % len(jobs)]
-    hop[tie], ret, less = lax.optimization_barrier((hop[tie], ret, less))
+    both = sigmas(*inputs)
+    tie = jobs[3 % len(jobs)]
+    hop[tie], both = lax.optimization_barrier((hop[tie], both))
     wins = {(s, q): [hop[s, q], send(hop[s, q], plan[s, q][1])] for s, q in jobs}
     for s, q in jobs:
         if plan[s, q][2]:
             wins[s, q].append(send(ready[s, q], plan[s, q][2]))
-    sums = ()
+    totals, came = [], []
     for q in range(chunks):
         mine = [wins[s, q] for s in range(ratio)]
         brings = [plan[s, q][3] for s in range(ratio)]
-        part, out = partial(ret, less, ready[0, q], mine, brings, q * LANES, width, scale)
-        sums = chunk_sums(sums, part, [send(out, pairs) for pairs in across])
-    total, message = sums
-    return accumulate(total, send(message, along))
+        part, out = partial(both, ready[0, q], mine, brings, q * LANES, width, scale)
+        if q < chunks - 1:
+            total, message = chunk_sums(part, [send(out, pairs) for pairs in across])
+            came.append(send(message, along))
+        else:
+            total, _ = chunk_sums(part, [send(out, pairs) for pairs in across + askew])
+            came.append(send(out, beside))
+        totals.append(total)
+    return accumulate(totals, came)
 
 
 def solution(mesh):

time: 44.5 us -> 43.7 us (0.982)
  the two profiles are of different devices: /device:TPU:11 before, /device:TPU:25 now
where the time goes in v4:
time: 43.7 us; the launch traced here: 43.3 us
  waiting for transfers between devices  21.7 us (50%)
  starting transfers between devices  14.4 us (33%)
  Pallas kernels  7.07 us (16%)
    ppermute x13, waiting for transfers between devices, send(): return lax.ppermute(x, AXES, pairs)  21.7 us
    ppermute x13, starting transfers between devices, send(): return lax.ppermute(x, AXES, pairs)  14.4 us
    pallas_call x1, Pallas kernels, sigmas(): pl.pallas_call(kernel, out_shape=held((ratio, rows, 2 * rows), BF16), in_...  2.6 us
    pallas_call x2, Pallas kernels, partial(): pl.pallas_call(kernel, out_shape=shapes, in_specs=[pl.BlockSpec(memory_sp...  1.49 us
    pallas_call x1, Pallas kernels, pack(): pl.pallas_call(kernel, out_shape=[held((2, r1 - r0, c1 - c0), BF16) for _...  1.38 us
  transfers between devices with their start and end apart: 13, of which 4 were waited for; matrix products, arithmetic and copies ran while one was open for 0% of the time, Pallas kernels for 11%

profile of v4, /device:TPU:25, one launch (start us, length us, event | category | flops | bytes accessed | tf_op | source)
XLA Modules:
  0.0 43.3 jit_solution(13264916686430446508)
XLA Ops:
  0.0 1.4 %pack_windows.1 = (bf16[2,512,128]{2,1,0:T(8,128)(2,1)S(1)}, bf16[2,512,128]{2,1,0:T(8,128)(2,1)S(1)}, bf16[2,512,128]{2,1,0:T(8,128)(2,1)S(1)}, bf16[2,512,128]{2,1,0:T(8,128)(2,1)S(1)}) custom-call(bf16[512,1024]{1,0:T(8,128)(2,1)} %refs_0_.1, bf16[512,1024]{1,0:T(8,128)(2,1)} %refs_1_.1), custom_call_target="tpu_custom_call" | custom-call | tf_op jit(solution)/shard_map/pack_windows/pallas_call | solution.py:132
  1.4 0.7 %collective-permute-start.1 = (bf16[2,512,128]{2,1,0:T(8,128)(2,1)S(1)}, bf16[2,512,128]{2,1,0:T(8,128)(2,1)S(1)}, u32[]{:S(2)}, u32[]{:S(2)}) collective-permute-start(bf16[2,512,128]{2,1,0:T(8,128)(2,1)S(1)} %get-tuple-element.20.own_ref), channel_id=1, source_target_pairs={{2,16},{6,20},{10,17},{14,21},{3,0},{7,4},{11,9},{15,13},{1,8},{5,... | collective-permute-start | bytes 786440 | tf_op jit(solution)/shard_map/ppermute | solution.py:306
  2.1 0.7 %collective-permute-start.3 = (bf16[2,512,128]{2,1,0:T(8,128)(2,1)S(1)}, bf16[2,512,128]{2,1,0:T(8,128)(2,1)S(1)}, u32[]{:S(2)}, u32[]{:S(2)}) collective-permute-start(bf16[2,512,128]{2,1,0:T(8,128)(2,1)S(1)} %get-tuple-element.21), channel_id=1, source_target_pairs={{2,20},{6,16},{10,21},{14,17},{3,0},{7,5},{11,9},{15,12},{0,4},{1,... | collective-permute-start | bytes 786440 | tf_op jit(solution)/shard_map/ppermute | solution.py:306
  2.8 0.7 %collective-permute-start = (bf16[2,512,128]{2,1,0:T(8,128)(2,1)S(1)}, bf16[2,512,128]{2,1,0:T(8,128)(2,1)S(1)}, u32[]{:S(2)}, u32[]{:S(2)}) collective-permute-start(bf16[2,512,128]{2,1,0:T(8,128)(2,1)S(1)} %get-tuple-element.18), channel_id=1, source_target_pairs={{2,20},{6,16},{10,21},{14,17},{3,0},{7,5},{11,9},{15,12},{0,4},{1,... | collective-permute-start | bytes 786440 | tf_op jit(solution)/shard_map/ppermute | solution.py:306
  3.4 0.7 %collective-permute-start.6 = (bf16[2,512,128]{2,1,0:T(8,128)(2,1)S(1)}, bf16[2,512,128]{2,1,0:T(8,128)(2,1)S(1)}, u32[]{:S(2)}, u32[]{:S(2)}) collective-permute-start(bf16[2,512,128]{2,1,0:T(8,128)(2,1)S(1)} %get-tuple-element.25.own_ref), channel_id=1, source_target_pairs={{2,16},{6,20},{10,17},{14,21},{3,0},{7,4},{11,9},{15,13},{1,8},{5,... | collective-permute-start | bytes 786440 | tf_op jit(solution)/shard_map/ppermute | solution.py:306
  4.1 0.0 collective-permute-done.1.refs_0_
  4.1 1.3 %collective-permute-start.2 = (bf16[2,512,128]{2,1,0:T(8,128)(2,1)S(1)}, bf16[2,512,128]{2,1,0:T(8,128)(2,1)S(1)}, u32[]{:S(2)}, u32[]{:S(2)}) collective-permute-start(bf16[2,512,128]{2,1,0:T(8,128)(2,1)S(1)} %collective-permute-done.1.refs_0_), channel_id=1, source_target_pairs={{0,24},{4,28},{9,25},{13,29}} | collective-permute-start | bytes 786440 | tf_op jit(solution)/shard_map/ppermute | solution.py:306
  5.4 0.0 collective-permute-done.3.refs_2_
  5.4 1.3 %collective-permute-start.4 = (bf16[2,512,128]{2,1,0:T(8,128)(2,1)S(1)}, bf16[2,512,128]{2,1,0:T(8,128)(2,1)S(1)}, u32[]{:S(2)}, u32[]{:S(2)}) collective-permute-start(bf16[2,512,128]{2,1,0:T(8,128)(2,1)S(1)} %collective-permute-done.3.refs_2_), channel_id=1, source_target_pairs={{0,28},{5,24},{9,29},{12,25},{1,12}} | collective-permute-start | bytes 786440 | tf_op jit(solution)/shard_map/ppermute | solution.py:306
  6.7 2.6 %sigma_blocks.1.both_ref = bf16[2,512,1024]{2,1,0:T(8,128)(2,1)S(1)} custom-call(bf16[512,1024]{1,0:T(8,128)(2,1)} %refs_0_.1, bf16[512,1024]{1,0:T(8,128)(2,1)} %refs_1_.1, bf16[512,1024]{1,0:T(8,128)(2,1)} %refs_2_.1, bf16[512,1024]{1,0:T(8,128)(2,1)} %refs_3_.1), custom_call_target="tpu_custom_call" | custom-call | tf_op jit(solution)/shard_map/sigma_blocks/pallas_call | solution.py:174
  9.4 0.0 collective-permute-done.refs_2_
  9.4 1.3 %collective-permute-start.8 = (bf16[2,512,128]{2,1,0:T(8,128)(2,1)S(1)}, bf16[2,512,128]{2,1,0:T(8,128)(2,1)S(1)}, u32[]{:S(2)}, u32[]{:S(2)}) collective-permute-start(bf16[2,512,128]{2,1,0:T(8,128)(2,1)S(1)} %collective-permute-done.refs_2_), channel_id=1, source_target_pairs={{0,28},{5,24},{9,29},{12,25},{1,12}} | collective-permute-start | bytes 786440 | tf_op jit(solution)/shard_map/ppermute | solution.py:306
  10.7 0.0 collective-permute-done.6.refs_0_
  10.7 1.3 %collective-permute-start.7 = (bf16[2,512,128]{2,1,0:T(8,128)(2,1)S(1)}, bf16[2,512,128]{2,1,0:T(8,128)(2,1)S(1)}, u32[]{:S(2)}, u32[]{:S(2)}) collective-permute-start(bf16[2,512,128]{2,1,0:T(8,128)(2,1)S(1)} %collective-permute-done.6.refs_0_), channel_id=1, source_target_pairs={{0,24},{4,28},{9,25},{13,29}} | collective-permute-start | bytes 786440 | tf_op jit(solution)/shard_map/ppermute | solution.py:306
  12.0 7.8 %collective-permute-done.2.refs_1_ = bf16[2,512,128]{2,1,0:T(8,128)(2,1)S(1)} collective-permute-done((bf16[2,512,128]{2,1,0:T(8,128)(2,1)S(1)}, bf16[2,512,128]{2,1,0:T(8,128)(2,1)S(1)}, u32[]{:S(2)}, u32[]{:S(2)}) %collective-permute-start.2) | collective-permute-done | bytes 262176 | tf_op jit(solution)/shard_map/ppermute | solution.py:306
  19.8 0.9 %collective-permute-done.4.refs_3_ = bf16[2,512,128]{2,1,0:T(8,128)(2,1)S(1)} collective-permute-done((bf16[2,512,128]{2,1,0:T(8,128)(2,1)S(1)}, bf16[2,512,128]{2,1,0:T(8,128)(2,1)S(1)}, u32[]{:S(2)}, u32[]{:S(2)}) %collective-permute-start.4) | collective-permute-done | bytes 262176 | tf_op jit(solution)/shard_map/ppermute | solution.py:306
  20.7 0.7 %partial.2 = (f32[512,128]{1,0:T(8,128)S(1)}, bf16[512,128]{1,0:T(8,128)(2,1)S(1)}) custom-call(bf16[2,512,1024]{2,1,0:T(8,128)(2,1)S(1)} %sigma_blocks.1.both_ref, bf16[2,512,128]{2,1,0:T(8,128)(2,1)S(1)} %get-tuple-element.20.own_ref, bf16[2,512,128]{2,1,0:T(8,128)(2,1)S(1)} %collective-permute-done.1.refs_0_, ...), custom_call_target="tpu_custom_call" | custom-call | tf_op jit(solution)/shard_map/partial/pallas_call | solution.py:240
  21.4 1.3 %collective-permute-start.5 = (bf16[512,128]{1,0:T(8,128)(2,1)S(1)}, bf16[512,128]{1,0:T(8,128)(2,1)S(1)}, u32[]{:S(2)}, u32[]{:S(2)}) collective-permute-start(bf16[512,128]{1,0:T(8,128)(2,1)S(1)} %get-tuple-element.23), channel_id=1, source_target_pairs={{0,2},{4,6},{8,10},{9,11},{12,14},{13,15},{16,18},{17,19},{20,22},... | collective-permute-start | bytes 393224 | tf_op jit(solution)/shard_map/ppermute | solution.py:306
  22.7 11.8 %collective-permute-done.8.refs_3_ = bf16[2,512,128]{2,1,0:T(8,128)(2,1)S(1)} collective-permute-done((bf16[2,512,128]{2,1,0:T(8,128)(2,1)S(1)}, bf16[2,512,128]{2,1,0:T(8,128)(2,1)S(1)}, u32[]{:S(2)}, u32[]{:S(2)}) %collective-permute-start.8) | collective-permute-done | bytes 262176 | tf_op jit(solution)/shard_map/ppermute | solution.py:306
  34.5 0.0 collective-permute-done.7.refs_1_
  34.5 0.8 %partial.3 = (f32[512,128]{1,0:T(8,128)S(1)}, bf16[512,128]{1,0:T(8,128)(2,1)S(1)}) custom-call(bf16[2,512,1024]{2,1,0:T(8,128)(2,1)S(1)} %sigma_blocks.1.both_ref, bf16[2,512,128]{2,1,0:T(8,128)(2,1)S(1)} %get-tuple-element.25.own_ref, bf16[2,512,128]{2,1,0:T(8,128)(2,1)S(1)} %collective-permute-done.6.refs_0_, ...), custom_call_target="tpu_custom_call" | custom-call | tf_op jit(solution)/shard_map/partial/pallas_call | solution.py:240
  35.3 1.3 %collective-permute-start.10 = (bf16[512,128]{1,0:T(8,128)(2,1)S(1)}, bf16[512,128]{1,0:T(8,128)(2,1)S(1)}, u32[]{:S(2)}, u32[]{:S(2)}) collective-permute-start(bf16[512,128]{1,0:T(8,128)(2,1)S(1)} %get-tuple-element.28), channel_id=1, source_target_pairs={{0,3},{4,7},{8,11},{9,10},{12,15},{13,14},{16,19},{17,18},{20,23},... | collective-permute-start | bytes 393224 | tf_op jit(solution)/shard_map/ppermute | solution.py:306
  36.6 1.3 %collective-permute-start.9 = (bf16[512,128]{1,0:T(8,128)(2,1)S(1)}, bf16[512,128]{1,0:T(8,128)(2,1)S(1)}, u32[]{:S(2)}, u32[]{:S(2)}) collective-permute-start(bf16[512,128]{1,0:T(8,128)(2,1)S(1)} %get-tuple-element.28), channel_id=1, source_target_pairs={{0,2},{4,6},{8,10},{9,11},{12,14},{13,15},{16,18},{17,19},{20,22},... | collective-permute-start | bytes 393224 | tf_op jit(solution)/shard_map/ppermute | solution.py:306
  37.9 1.3 %collective-permute-start.12 = (bf16[512,128]{1,0:T(8,128)(2,1)S(1)}, bf16[512,128]{1,0:T(8,128)(2,1)S(1)}, u32[]{:S(2)}, u32[]{:S(2)}) collective-permute-start(bf16[512,128]{1,0:T(8,128)(2,1)S(1)} %get-tuple-element.28), channel_id=1, source_target_pairs={{0,1},{4,5},{8,9},{12,13},{16,17},{18,19},{20,21},{22,23},{24,25},... | collective-permute-start | bytes 393224 | tf_op jit(solution)/shard_map/ppermute | solution.py:306
  39.2 0.0 collective-permute-done.5.refs_0_
  39.2 0.1 chunk_sums.2
  39.2 1.3 %collective-permute-start.11 = (bf16[512,128]{1,0:T(8,128)(2,1)S(1)}, bf16[512,128]{1,0:T(8,128)(2,1)S(1)}, u32[]{:S(2)}, u32[]{:S(2)}) collective-permute-start(bf16[512,128]{1,0:T(8,128)(2,1)S(1)} %get-tuple-element.30), channel_id=1, source_target_pairs={{0,1},{2,3},{4,5},{6,7},{8,9},{10,11},{12,13},{14,15},{16,17},{18,... | collective-permute-start | bytes 393224 | tf_op jit(solution)/shard_map/ppermute | solution.py:306
  40.5 0.0 collective-permute-done.10.refs_1_
  40.6 0.7 %chunk_sums.3 = (f32[512,128]{1,0:T(8,128)S(1)}, bf16[512,128]{1,0:T(8,128)(2,1)}) custom-call(f32[512,128]{1,0:T(8,128)S(1)} %get-tuple-element.27.part_ref, bf16[512,128]{1,0:T(8,128)(2,1)S(1)} %collective-permute-done.9.refs_0_, bf16[512,128]{1,0:T(8,128)(2,1)S(1)} %collective-permute-done.10.refs_1_), custom_call_target="tpu_custom_call" | custom-call | tf_op jit(solution)/shard_map/chunk_sums/pallas_call | solution.py:261
  41.3 0.0 collective-permute-done.12.refs_3_
  41.3 1.2 %collective-permute-done.11.refs_2_ = bf16[512,128]{1,0:T(8,128)(2,1)S(1)} collective-permute-done((bf16[512,128]{1,0:T(8,128)(2,1)S(1)}, bf16[512,128]{1,0:T(8,128)(2,1)S(1)}, u32[]{:S(2)}, u32[]{:S(2)}) %collective-permute-start.11) | collective-permute-done | bytes 131104 | tf_op jit(solution)/shard_map/ppermute | solution.py:306
  42.5 0.8 %accumulate.1 = f32[512,256]{1,0:T(8,128)} custom-call(f32[512,128]{1,0:T(8,128)S(1)} %get-tuple-element.24.refs_0_, f32[512,128]{1,0:T(8,128)S(1)} %get-tuple-element.29.refs_1_, bf16[512,128]{1,0:T(8,128)(2,1)S(1)} %collective-permute-done.11.refs_2_, bf16[512,128]{1,0:T(8,128)(2,1)S(1)} %collective-permute-done.12.refs_3_), custom_call_target="tpu_custom_call" | custom-call | tf_op jit(solution)/shard_map/accumulate/pallas_call | solution.py:279
  (1 shorter events, 0.0 us)
Async XLA Ops:
  1.4 2.7 %collective-permute-start.1 = (bf16[2,512,128]{2,1,0:T(8,128)(2,1)S(1)}, bf16[2,512,128]{2,1,0:T(8,128)(2,1)S(1)}, u32[]{:S(2)}, u32[]{:S(2)}) collective-permute-start(bf16[2,512,128]{2,1,0:T(8,128)(2,1)S(1)} %get-tuple-element.20.own_ref), channel_id=1, source_target_pairs={{2,16},{6,20},{10,17},{14,21},{3,0},{7,4},{11,9},{15,13},{1,8},{5,... | collective-permute-start | bytes 786440 | tf_op jit(solution)/shard_map/ppermute | solution.py:306
  2.1 3.4 %collective-permute-start.3 = (bf16[2,512,128]{2,1,0:T(8,128)(2,1)S(1)}, bf16[2,512,128]{2,1,0:T(8,128)(2,1)S(1)}, u32[]{:S(2)}, u32[]{:S(2)}) collective-permute-start(bf16[2,512,128]{2,1,0:T(8,128)(2,1)S(1)} %get-tuple-element.21), channel_id=1, source_target_pairs={{2,20},{6,16},{10,21},{14,17},{3,0},{7,5},{11,9},{15,12},{0,4},{1,... | collective-permute-start | bytes 786440 | tf_op jit(solution)/shard_map/ppermute | solution.py:306
  2.8 6.6 %collective-permute-start = (bf16[2,512,128]{2,1,0:T(8,128)(2,1)S(1)}, bf16[2,512,128]{2,1,0:T(8,128)(2,1)S(1)}, u32[]{:S(2)}, u32[]{:S(2)}) collective-permute-start(bf16[2,512,128]{2,1,0:T(8,128)(2,1)S(1)} %get-tuple-element.18), channel_id=1, source_target_pairs={{2,20},{6,16},{10,21},{14,17},{3,0},{7,5},{11,9},{15,12},{0,4},{1,... | collective-permute-start | bytes 786440 | tf_op jit(solution)/shard_map/ppermute | solution.py:306
  3.4 7.2 %collective-permute-start.6 = (bf16[2,512,128]{2,1,0:T(8,128)(2,1)S(1)}, bf16[2,512,128]{2,1,0:T(8,128)(2,1)S(1)}, u32[]{:S(2)}, u32[]{:S(2)}) collective-permute-start(bf16[2,512,128]{2,1,0:T(8,128)(2,1)S(1)} %get-tuple-element.25.own_ref), channel_id=1, source_target_pairs={{2,16},{6,20},{10,17},{14,21},{3,0},{7,4},{11,9},{15,13},{1,8},{5,... | collective-permute-start | bytes 786440 | tf_op jit(solution)/shard_map/ppermute | solution.py:306
  4.1 15.6 %collective-permute-start.2 = (bf16[2,512,128]{2,1,0:T(8,128)(2,1)S(1)}, bf16[2,512,128]{2,1,0:T(8,128)(2,1)S(1)}, u32[]{:S(2)}, u32[]{:S(2)}) collective-permute-start(bf16[2,512,128]{2,1,0:T(8,128)(2,1)S(1)} %collective-permute-done.1.refs_0_), channel_id=1, source_target_pairs={{0,24},{4,28},{9,25},{13,29}} | collective-permute-start | bytes 786440 | tf_op jit(solution)/shard_map/ppermute | solution.py:306
  5.4 15.2 %collective-permute-start.4 = (bf16[2,512,128]{2,1,0:T(8,128)(2,1)S(1)}, bf16[2,512,128]{2,1,0:T(8,128)(2,1)S(1)}, u32[]{:S(2)}, u32[]{:S(2)}) collective-permute-start(bf16[2,512,128]{2,1,0:T(8,128)(2,1)S(1)} %collective-permute-done.3.refs_2_), channel_id=1, source_target_pairs={{0,28},{5,24},{9,29},{12,25},{1,12}} | collective-permute-start | bytes 786440 | tf_op jit(solution)/shard_map/ppermute | solution.py:306
  9.4 25.1 %collective-permute-start.8 = (bf16[2,512,128]{2,1,0:T(8,128)(2,1)S(1)}, bf16[2,512,128]{2,1,0:T(8,128)(2,1)S(1)}, u32[]{:S(2)}, u32[]{:S(2)}) collective-permute-start(bf16[2,512,128]{2,1,0:T(8,128)(2,1)S(1)} %collective-permute-done.refs_2_), channel_id=1, source_target_pairs={{0,28},{5,24},{9,29},{12,25},{1,12}} | collective-permute-start | bytes 786440 | tf_op jit(solution)/shard_map/ppermute | solution.py:306
  10.7 23.8 %collective-permute-start.7 = (bf16[2,512,128]{2,1,0:T(8,128)(2,1)S(1)}, bf16[2,512,128]{2,1,0:T(8,128)(2,1)S(1)}, u32[]{:S(2)}, u32[]{:S(2)}) collective-permute-start(bf16[2,512,128]{2,1,0:T(8,128)(2,1)S(1)} %collective-permute-done.6.refs_0_), channel_id=1, source_target_pairs={{0,24},{4,28},{9,25},{13,29}} | collective-permute-start | bytes 786440 | tf_op jit(solution)/shard_map/ppermute | solution.py:306
  21.4 17.8 %collective-permute-start.5 = (bf16[512,128]{1,0:T(8,128)(2,1)S(1)}, bf16[512,128]{1,0:T(8,128)(2,1)S(1)}, u32[]{:S(2)}, u32[]{:S(2)}) collective-permute-start(bf16[512,128]{1,0:T(8,128)(2,1)S(1)} %get-tuple-element.23), channel_id=1, source_target_pairs={{0,2},{4,6},{8,10},{9,11},{12,14},{13,15},{16,18},{17,19},{20,22},... | collective-permute-start | bytes 393224 | tf_op jit(solution)/shard_map/ppermute | solution.py:306
  35.3 5.3 %collective-permute-start.10 = (bf16[512,128]{1,0:T(8,128)(2,1)S(1)}, bf16[512,128]{1,0:T(8,128)(2,1)S(1)}, u32[]{:S(2)}, u32[]{:S(2)}) collective-permute-start(bf16[512,128]{1,0:T(8,128)(2,1)S(1)} %get-tuple-element.28), channel_id=1, source_target_pairs={{0,3},{4,7},{8,11},{9,10},{12,15},{13,14},{16,19},{17,18},{20,23},... | collective-permute-start | bytes 393224 | tf_op jit(solution)/shard_map/ppermute | solution.py:306
  36.6 4.0 %collective-permute-start.9 = (bf16[512,128]{1,0:T(8,128)(2,1)S(1)}, bf16[512,128]{1,0:T(8,128)(2,1)S(1)}, u32[]{:S(2)}, u32[]{:S(2)}) collective-permute-start(bf16[512,128]{1,0:T(8,128)(2,1)S(1)} %get-tuple-element.28), channel_id=1, source_target_pairs={{0,2},{4,6},{8,10},{9,11},{12,14},{13,15},{16,18},{17,19},{20,22},... | collective-permute-start | bytes 393224 | tf_op jit(solution)/shard_map/ppermute | solution.py:306
  37.9 3.4 %collective-permute-start.12 = (bf16[512,128]{1,0:T(8,128)(2,1)S(1)}, bf16[512,128]{1,0:T(8,128)(2,1)S(1)}, u32[]{:S(2)}, u32[]{:S(2)}) collective-permute-start(bf16[512,128]{1,0:T(8,128)(2,1)S(1)} %get-tuple-element.28), channel_id=1, source_target_pairs={{0,1},{4,5},{8,9},{12,13},{16,17},{18,19},{20,21},{22,23},{24,25},... | collective-permute-start | bytes 393224 | tf_op jit(solution)/shard_map/ppermute | solution.py:306
  39.2 3.2 %collective-permute-start.11 = (bf16[512,128]{1,0:T(8,128)(2,1)S(1)}, bf16[512,128]{1,0:T(8,128)(2,1)S(1)}, u32[]{:S(2)}, u32[]{:S(2)}) collective-permute-start(bf16[512,128]{1,0:T(8,128)(2,1)S(1)} %get-tuple-element.30), channel_id=1, source_target_pairs={{0,1},{2,3},{4,5},{6,7},{8,9},{10,11},{12,13},{14,15},{16,17},{18,... | collective-permute-start | bytes 393224 | tf_op jit(solution)/shard_map/ppermute | solution.py:306

commit v5 on v4

--- a/solution.py
+++ b/solution.py
@@ -15,7 +15,7 @@
 ROOM = pltpu.CompilerParams(vmem_limit_bytes=16 * 2**20)
 
 
-def route(row_devices, col_devices, s, eased):
+def route(row_devices, col_devices, s):
     ratio = row_devices // col_devices
     half = col_devices // 2
     straight = col_devices - half // 2
@@ -30,7 +30,7 @@
             to = (y + s) % ratio
             for g in range(z, col_devices):
                 src, dst = at(z, y, g), at(g, to, z)
-                if z < half and g >= straight and not (eased and z % 2):
+                if z < half and g >= straight:
                     hops.append((z, y, src, dst))
                 elif z < half <= g:
                     first.append((src, dst))
@@ -77,12 +77,17 @@
     rows = [(z, y) for z in range(col_devices) for y in range(ratio)]
     across, askew = [], []
     for d in range(2, col_devices, 2):
-        sources = [(z, y, c) for z, y in rows for c in range(min(z + 1, col_devices - d))]
-        across.append([(at(z, y, c), at(z, y, c + d)) for z, y, c in sources])
-        askew.append([(at(z, y, c), at(z, y, (c + d) ^ 1)) for z, y, c in sources])
+        pairs = [
+            (at(z, y, c), at(z, y, c + d), at(z, y, (c + d) ^ 1))
+            for z, y in rows
+            for c in range(min(z + 1, col_devices - d))
+        ]
+        swapped = {at(z, y, c) for z, y in rows if z < col_devices // 2 for c in range(col_devices)}
+        across.append([(src, other if src in swapped else same) for src, same, other in pairs])
+        askew.append([(src, same if src in swapped else other) for src, same, other in pairs])
     beside = [(at(z, y, c), at(z, y, c + 1)) for z, y in rows for c in range(0, min(z + 1, col_devices), 2)]
     along = [(at(z, y, c), at(z, y, c + 1)) for z, y in rows for c in range(0, col_devices, 2)]
-    along += [(at(z, y, c + 1), at(z, y, c)) for z, y in rows for c in range(2, col_devices, 2) if z]
+    along += [(at(z, y, c + 1), at(z, y, c)) for z, y in rows for c in range(2, col_devices, 2)]
     return across, askew, along, beside
 
 
@@ -143,7 +148,7 @@
 def sigmas(lesser, greater, screened_lesser, screened_greater):
     rows, width = lesser.shape
     ratio = width // rows
-    steps = 8
+    steps = 4
     tile = rows // steps
 
     def kernel(*refs):
@@ -191,20 +196,20 @@
     return jnp.dot(both_ref[k], jnp.concatenate([green, diff], axis=0), preferred_element_type=F32)
 
 
-def partial(both, own, wins, brings, first, width, scale, sent=()):
+def partial(both, own, wins, brings, first, width, scale):
     ratio, rows, _ = both.shape
     cols = own.shape[-1]
     counts = [len(pieces) for pieces in wins]
     col_devices = lax.axis_size("col")
 
     def kernel(both_ref, own_ref, *refs):
-        outs = refs[len(refs) - (3 if sent else 2) :]
+        outs = refs[-2:]
         my_row, my_col = place()
         some = my_col <= my_row // ratio
 
         @pl.when(some)
         def _():
-            total, at = None, len(sent)
+            total, at = None, 0
             for s in range(ratio):
                 k = lax.rem(my_row + ratio - s, ratio)
                 mine = refs[at : at + counts[s]]
@@ -224,10 +229,6 @@
             total = scale * total
             outs[0][...] = total
             outs[1][...] = total.astype(BF16)
-            if sent:
-                for n in range(len(sent)):
-                    outs[2][:, n * cols : (n + 1) * cols] = refs[n][...]
-                outs[2][:, len(sent) * cols :] = total.astype(BF16)
 
         @pl.when(jnp.logical_not(some))
         def _():
@@ -235,34 +236,35 @@
                 ref[...] = jnp.zeros(ref.shape, ref.dtype)
 
     shapes = [held((rows, cols), F32), held((rows, cols), BF16)]
-    if sent:
-        shapes.append(held((rows, (1 + len(sent)) * cols), BF16))
     return pl.pallas_call(
         kernel,
         out_shape=shapes,
-        in_specs=[pl.BlockSpec(memory_space=pltpu.VMEM)] * (2 + len(sent) + sum(counts)),
+        in_specs=[pl.BlockSpec(memory_space=pltpu.VMEM)] * (2 + sum(counts)),
         out_specs=[pl.BlockSpec(memory_space=pltpu.VMEM)] * len(shapes),
         compiler_params=ROOM,
         name="partial",
-    )(*map(keep, [both, own, *sent]), *[keep(x) for pieces in wins for x in pieces])
-
-
-def chunk_sums(part, got):
+    )(*map(keep, [both, own]), *[keep(x) for pieces in wins for x in pieces])
+
+
+def chunk_sums(part, got, relayed):
+    outs = [held(part.shape, F32)] + ([held(part.shape, BF16)] if relayed else [])
+
     def kernel(part_ref, *refs):
         _, my_col = place()
         came = jnp.zeros(part_ref.shape, F32)
-        for ref in refs[:-2]:
+        for ref in refs[: len(got)]:
             came = came + ref[...].astype(F32)
         total = came + part_ref[...]
-        refs[-2][...] = total
-        refs[-1][...] = jnp.where(lax.rem(my_col, 2) == 0, total, came).astype(BF16)
+        refs[len(got)][...] = total
+        if relayed:
+            refs[-1][...] = jnp.where(lax.rem(my_col, 2) == 0, total, came).astype(BF16)
 
     args = [part, *got]
     return pl.pallas_call(
         kernel,
-        out_shape=[held(part.shape, F32), held(part.shape, BF16)],
+        out_shape=outs,
         in_specs=[pl.BlockSpec(memory_space=pltpu.VMEM)] * len(args),
-        out_specs=[pl.BlockSpec(memory_space=pltpu.VMEM)] * 2,
+        out_specs=[pl.BlockSpec(memory_space=pltpu.VMEM)] * len(outs),
         compiler_params=ROOM,
         name="chunk_sums",
     )(*map(keep, args))
@@ -294,21 +296,17 @@
     across, askew, along, beside = onward(row_devices, col_devices)
     chunks = WINDOW // LANES
 
-    def send(x, pairs):
-        return lax.ppermute(x, AXES, pairs)
-
     jobs = [(s, q) for q in range(chunks) for s in range(ratio)]
     packed = pack(lesser, greater, [(s, 0, rows, q * LANES, (q + 1) * LANES) for s, q in jobs])
     ready = dict(zip(jobs, packed))
-    plan = {job: route(row_devices, col_devices, job[0], n in ()) for n, job in enumerate(jobs)}
+    plan = {job: route(row_devices, col_devices, job[0]) for job in jobs}
 
     def send(x, pairs):
         return lax.ppermute(x, AXES, pairs)
 
     hop = {(s, q): send(ready[s, q], plan[s, q][0]) for s, q in jobs}
-    inputs = (lesser, greater, screened_lesser, screened_greater)
-    both = sigmas(*inputs)
-    tie = jobs[3 % len(jobs)]
+    both = sigmas(lesser, greater, screened_lesser, screened_greater)
+    tie = jobs[-ratio]
     hop[tie], both = lax.optimization_barrier((hop[tie], both))
     wins = {(s, q): [hop[s, q], send(hop[s, q], plan[s, q][1])] for s, q in jobs}
     for s, q in jobs:
@@ -320,10 +318,10 @@
         brings = [plan[s, q][3] for s in range(ratio)]
         part, out = partial(both, ready[0, q], mine, brings, q * LANES, width, scale)
         if q < chunks - 1:
-            total, message = chunk_sums(part, [send(out, pairs) for pairs in across])
+            total, message = chunk_sums(part, [send(out, pairs) for pairs in across], True)
             came.append(send(message, along))
         else:
-            total, _ = chunk_sums(part, [send(out, pairs) for pairs in across + askew])
+            (total,) = chunk_sums(part, [send(out, pairs) for pairs in across + askew], False)
             came.append(send(out, beside))
         totals.append(total)
     return accumulate(totals, came)

time: 43.7 us -> 43.7 us (level)
  Pallas kernels: 7.07 us -> 6.27 us
  waiting for transfers between devices: 21.7 us -> 22.5 us
    ppermute x13, waiting for transfers between devices: 21.7 us -> 22.5 us  [send(): return lax.ppermute(x, AXES, pairs)]
    pallas_call x2, Pallas kernels: 0.76 us -> 0.09 us  [chunk_sums(): pl.pallas_call(kernel, out_shape=outs, in_specs=[pl.BlockSpec(memory_spac...]
  transfers between devices with their start and end apart: 13 -> 13, of which waited for: 4 -> 5; matrix products, arithmetic and copies ran while one was open for 0% -> 0% of each run, Pallas kernels for 11% -> 9%
where the time goes in v5:
time: 43.7 us; the launch traced here: 43.3 us
  waiting for transfers between devices  22.5 us (51%)
  starting transfers between devices  14.4 us (33%)
  Pallas kernels  6.27 us (14%)
    ppermute x13, waiting for transfers between devices, send(): return lax.ppermute(x, AXES, pairs)  22.5 us
    ppermute x13, starting transfers between devices, send(): return lax.ppermute(x, AXES, pairs)  14.4 us
    pallas_call x1, Pallas kernels, sigmas(): pl.pallas_call(kernel, out_shape=held((ratio, rows, 2 * rows), BF16), in_...  2.46 us
    pallas_call x2, Pallas kernels, partial(): pl.pallas_call(kernel, out_shape=shapes, in_specs=[pl.BlockSpec(memory_sp...  1.5 us
    pallas_call x1, Pallas kernels, pack(): pl.pallas_call(kernel, out_shape=[held((2, r1 - r0, c1 - c0), BF16) for _...  1.38 us
  transfers between devices with their start and end apart: 13, of which 5 were waited for; matrix products, arithmetic and copies ran while one was open for 0% of the time, Pallas kernels for 9%

profile of v5, /device:TPU:25, one launch (start us, length us, event | category | flops | bytes accessed | tf_op | source)
XLA Modules:
  0.0 43.3 jit_solution(5743762040310131178)
XLA Ops:
  0.0 1.4 %pack_windows.1 = (bf16[2,512,128]{2,1,0:T(8,128)(2,1)S(1)}, bf16[2,512,128]{2,1,0:T(8,128)(2,1)S(1)}, bf16[2,512,128]{2,1,0:T(8,128)(2,1)S(1)}, bf16[2,512,128]{2,1,0:T(8,128)(2,1)S(1)}) custom-call(bf16[512,1024]{1,0:T(8,128)(2,1)} %refs_0_.1, bf16[512,1024]{1,0:T(8,128)(2,1)} %refs_1_.1), custom_call_target="tpu_custom_call" | custom-call | tf_op jit(solution)/shard_map/pack_windows/pallas_call | solution.py:137
  1.4 0.7 %collective-permute-start.1 = (bf16[2,512,128]{2,1,0:T(8,128)(2,1)S(1)}, bf16[2,512,128]{2,1,0:T(8,128)(2,1)S(1)}, u32[]{:S(2)}, u32[]{:S(2)}) collective-permute-start(bf16[2,512,128]{2,1,0:T(8,128)(2,1)S(1)} %get-tuple-element.19.own_ref), channel_id=1, source_target_pairs={{2,16},{6,20},{10,17},{14,21},{3,0},{7,4},{11,9},{15,13},{1,8},{5,... | collective-permute-start | bytes 786440 | tf_op jit(solution)/shard_map/ppermute | solution.py:305
  2.1 0.7 %collective-permute-start.3 = (bf16[2,512,128]{2,1,0:T(8,128)(2,1)S(1)}, bf16[2,512,128]{2,1,0:T(8,128)(2,1)S(1)}, u32[]{:S(2)}, u32[]{:S(2)}) collective-permute-start(bf16[2,512,128]{2,1,0:T(8,128)(2,1)S(1)} %get-tuple-element.20), channel_id=1, source_target_pairs={{2,20},{6,16},{10,21},{14,17},{3,0},{7,5},{11,9},{15,12},{0,4},{1,... | collective-permute-start | bytes 786440 | tf_op jit(solution)/shard_map/ppermute | solution.py:305
  2.8 0.7 %collective-permute-start = (bf16[2,512,128]{2,1,0:T(8,128)(2,1)S(1)}, bf16[2,512,128]{2,1,0:T(8,128)(2,1)S(1)}, u32[]{:S(2)}, u32[]{:S(2)}) collective-permute-start(bf16[2,512,128]{2,1,0:T(8,128)(2,1)S(1)} %get-tuple-element.17.own_ref), channel_id=1, source_target_pairs={{2,16},{6,20},{10,17},{14,21},{3,0},{7,4},{11,9},{15,13},{1,8},{5,... | collective-permute-start | bytes 786440 | tf_op jit(solution)/shard_map/ppermute | solution.py:305
  3.4 0.7 %collective-permute-start.7 = (bf16[2,512,128]{2,1,0:T(8,128)(2,1)S(1)}, bf16[2,512,128]{2,1,0:T(8,128)(2,1)S(1)}, u32[]{:S(2)}, u32[]{:S(2)}) collective-permute-start(bf16[2,512,128]{2,1,0:T(8,128)(2,1)S(1)} %get-tuple-element.25), channel_id=1, source_target_pairs={{2,20},{6,16},{10,21},{14,17},{3,0},{7,5},{11,9},{15,12},{0,4},{1,... | collective-permute-start | bytes 786440 | tf_op jit(solution)/shard_map/ppermute | solution.py:305
  4.1 0.0 collective-permute-done.1.refs_0_
  4.1 1.3 %collective-permute-start.2 = (bf16[2,512,128]{2,1,0:T(8,128)(2,1)S(1)}, bf16[2,512,128]{2,1,0:T(8,128)(2,1)S(1)}, u32[]{:S(2)}, u32[]{:S(2)}) collective-permute-start(bf16[2,512,128]{2,1,0:T(8,128)(2,1)S(1)} %collective-permute-done.1.refs_0_), channel_id=1, source_target_pairs={{0,24},{4,28},{9,25},{13,29}} | collective-permute-start | bytes 786440 | tf_op jit(solution)/shard_map/ppermute | solution.py:305
  5.4 0.0 collective-permute-done.3.refs_2_
  5.4 1.3 %collective-permute-start.4 = (bf16[2,512,128]{2,1,0:T(8,128)(2,1)S(1)}, bf16[2,512,128]{2,1,0:T(8,128)(2,1)S(1)}, u32[]{:S(2)}, u32[]{:S(2)}) collective-permute-start(bf16[2,512,128]{2,1,0:T(8,128)(2,1)S(1)} %collective-permute-done.3.refs_2_), channel_id=1, source_target_pairs={{0,28},{5,24},{9,29},{12,25},{1,12}} | collective-permute-start | bytes 786440 | tf_op jit(solution)/shard_map/ppermute | solution.py:305
  6.7 2.5 %sigma_blocks.1.both_ref = bf16[2,512,1024]{2,1,0:T(8,128)(2,1)S(1)} custom-call(bf16[512,1024]{1,0:T(8,128)(2,1)} %refs_0_.1, bf16[512,1024]{1,0:T(8,128)(2,1)} %refs_1_.1, bf16[512,1024]{1,0:T(8,128)(2,1)} %refs_2_.1, bf16[512,1024]{1,0:T(8,128)(2,1)} %refs_3_.1), custom_call_target="tpu_custom_call" | custom-call | tf_op jit(solution)/shard_map/sigma_blocks/pallas_call | solution.py:179
  9.2 0.0 collective-permute-done.refs_0_
  9.2 1.3 %collective-permute-start.6 = (bf16[2,512,128]{2,1,0:T(8,128)(2,1)S(1)}, bf16[2,512,128]{2,1,0:T(8,128)(2,1)S(1)}, u32[]{:S(2)}, u32[]{:S(2)}) collective-permute-start(bf16[2,512,128]{2,1,0:T(8,128)(2,1)S(1)} %collective-permute-done.refs_0_), channel_id=1, source_target_pairs={{0,24},{4,28},{9,25},{13,29}} | collective-permute-start | bytes 786440 | tf_op jit(solution)/shard_map/ppermute | solution.py:305
  10.5 0.0 collective-permute-done.7.refs_2_
  10.5 1.3 %collective-permute-start.8 = (bf16[2,512,128]{2,1,0:T(8,128)(2,1)S(1)}, bf16[2,512,128]{2,1,0:T(8,128)(2,1)S(1)}, u32[]{:S(2)}, u32[]{:S(2)}) collective-permute-start(bf16[2,512,128]{2,1,0:T(8,128)(2,1)S(1)} %collective-permute-done.7.refs_2_), channel_id=1, source_target_pairs={{0,28},{5,24},{9,29},{12,25},{1,12}} | collective-permute-start | bytes 786440 | tf_op jit(solution)/shard_map/ppermute | solution.py:305
  11.8 8.9 %collective-permute-done.2.refs_1_ = bf16[2,512,128]{2,1,0:T(8,128)(2,1)S(1)} collective-permute-done((bf16[2,512,128]{2,1,0:T(8,128)(2,1)S(1)}, bf16[2,512,128]{2,1,0:T(8,128)(2,1)S(1)}, u32[]{:S(2)}, u32[]{:S(2)}) %collective-permute-start.2) | collective-permute-done | bytes 262176 | tf_op jit(solution)/shard_map/ppermute | solution.py:305
  20.7 10.3 %collective-permute-done.4.refs_3_ = bf16[2,512,128]{2,1,0:T(8,128)(2,1)S(1)} collective-permute-done((bf16[2,512,128]{2,1,0:T(8,128)(2,1)S(1)}, bf16[2,512,128]{2,1,0:T(8,128)(2,1)S(1)}, u32[]{:S(2)}, u32[]{:S(2)}) %collective-permute-start.4) | collective-permute-done | bytes 262176 | tf_op jit(solution)/shard_map/ppermute | solution.py:305
  31.1 0.8 %partial.2 = (f32[512,128]{1,0:T(8,128)S(1)}, bf16[512,128]{1,0:T(8,128)(2,1)S(1)}) custom-call(bf16[2,512,1024]{2,1,0:T(8,128)(2,1)S(1)} %sigma_blocks.1.both_ref, bf16[2,512,128]{2,1,0:T(8,128)(2,1)S(1)} %get-tuple-element.19.own_ref, bf16[2,512,128]{2,1,0:T(8,128)(2,1)S(1)} %collective-permute-done.1.refs_0_, ...), custom_call_target="tpu_custom_call" | custom-call | tf_op jit(solution)/shard_map/partial/pallas_call | solution.py:239
  31.8 1.3 %collective-permute-start.5 = (bf16[512,128]{1,0:T(8,128)(2,1)S(1)}, bf16[512,128]{1,0:T(8,128)(2,1)S(1)}, u32[]{:S(2)}, u32[]{:S(2)}) collective-permute-start(bf16[512,128]{1,0:T(8,128)(2,1)S(1)} %get-tuple-element.22), channel_id=1, source_target_pairs={{0,3},{4,7},{8,11},{9,10},{12,15},{13,14},{16,18},{17,19},{20,22},... | collective-permute-start | bytes 393224 | tf_op jit(solution)/shard_map/ppermute | solution.py:305
  33.1 0.0 collective-permute-done.6.refs_1_
  33.1 1.3 %collective-permute-done.8.refs_3_ = bf16[2,512,128]{2,1,0:T(8,128)(2,1)S(1)} collective-permute-done((bf16[2,512,128]{2,1,0:T(8,128)(2,1)S(1)}, bf16[2,512,128]{2,1,0:T(8,128)(2,1)S(1)}, u32[]{:S(2)}, u32[]{:S(2)}) %collective-permute-start.8) | collective-permute-done | bytes 262176 | tf_op jit(solution)/shard_map/ppermute | solution.py:305
  34.5 0.8 %partial.3 = (f32[512,128]{1,0:T(8,128)S(1)}, bf16[512,128]{1,0:T(8,128)(2,1)S(1)}) custom-call(bf16[2,512,1024]{2,1,0:T(8,128)(2,1)S(1)} %sigma_blocks.1.both_ref, bf16[2,512,128]{2,1,0:T(8,128)(2,1)S(1)} %get-tuple-element.17.own_ref, bf16[2,512,128]{2,1,0:T(8,128)(2,1)S(1)} %collective-permute-done.refs_0_, ...), custom_call_target="tpu_custom_call" | custom-call | tf_op jit(solution)/shard_map/partial/pallas_call | solution.py:239
  35.3 1.3 %collective-permute-start.10 = (bf16[512,128]{1,0:T(8,128)(2,1)S(1)}, bf16[512,128]{1,0:T(8,128)(2,1)S(1)}, u32[]{:S(2)}, u32[]{:S(2)}) collective-permute-start(bf16[512,128]{1,0:T(8,128)(2,1)S(1)} %get-tuple-element.27), channel_id=1, source_target_pairs={{0,2},{4,6},{8,10},{9,11},{12,14},{13,15},{16,19},{17,18},{20,23},... | collective-permute-start | bytes 393224 | tf_op jit(solution)/shard_map/ppermute | solution.py:305
  36.6 1.3 %collective-permute-start.9 = (bf16[512,128]{1,0:T(8,128)(2,1)S(1)}, bf16[512,128]{1,0:T(8,128)(2,1)S(1)}, u32[]{:S(2)}, u32[]{:S(2)}) collective-permute-start(bf16[512,128]{1,0:T(8,128)(2,1)S(1)} %get-tuple-element.27), channel_id=1, source_target_pairs={{0,3},{4,7},{8,11},{9,10},{12,15},{13,14},{16,18},{17,19},{20,22},... | collective-permute-start | bytes 393224 | tf_op jit(solution)/shard_map/ppermute | solution.py:305
  37.9 1.3 %collective-permute-start.12 = (bf16[512,128]{1,0:T(8,128)(2,1)S(1)}, bf16[512,128]{1,0:T(8,128)(2,1)S(1)}, u32[]{:S(2)}, u32[]{:S(2)}) collective-permute-start(bf16[512,128]{1,0:T(8,128)(2,1)S(1)} %get-tuple-element.27), channel_id=1, source_target_pairs={{0,1},{4,5},{8,9},{12,13},{16,17},{18,19},{20,21},{22,23},{24,25},... | collective-permute-start | bytes 393224 | tf_op jit(solution)/shard_map/ppermute | solution.py:305
  39.2 0.0 collective-permute-done.5.refs_0_
  39.2 0.1 chunk_sums.2
  39.2 1.3 %collective-permute-start.11 = (bf16[512,128]{1,0:T(8,128)(2,1)S(1)}, bf16[512,128]{1,0:T(8,128)(2,1)S(1)}, u32[]{:S(2)}, u32[]{:S(2)}) collective-permute-start(bf16[512,128]{1,0:T(8,128)(2,1)S(1)} %get-tuple-element.28), channel_id=1, source_target_pairs={{0,1},{2,3},{4,5},{6,7},{8,9},{10,11},{12,13},{14,15},{16,17},{18,... | collective-permute-start | bytes 393224 | tf_op jit(solution)/shard_map/ppermute | solution.py:305
  40.5 0.0 collective-permute-done.10.refs_1_
  40.5 0.0 collective-permute-done.9.refs_0_
  40.6 0.5 %collective-permute-done.12.refs_3_ = bf16[512,128]{1,0:T(8,128)(2,1)S(1)} collective-permute-done((bf16[512,128]{1,0:T(8,128)(2,1)S(1)}, bf16[512,128]{1,0:T(8,128)(2,1)S(1)}, u32[]{:S(2)}, u32[]{:S(2)}) %collective-permute-start.12) | collective-permute-done | bytes 131104 | tf_op jit(solution)/shard_map/ppermute | solution.py:305
  41.1 1.4 %collective-permute-done.11.refs_2_ = bf16[512,128]{1,0:T(8,128)(2,1)S(1)} collective-permute-done((bf16[512,128]{1,0:T(8,128)(2,1)S(1)}, bf16[512,128]{1,0:T(8,128)(2,1)S(1)}, u32[]{:S(2)}, u32[]{:S(2)}) %collective-permute-start.11) | collective-permute-done | bytes 131104 | tf_op jit(solution)/shard_map/ppermute | solution.py:305
  42.5 0.8 %accumulate.1 = f32[512,256]{1,0:T(8,128)} custom-call(f32[512,128]{1,0:T(8,128)S(1)} %get-tuple-element.23.refs_0_, f32[512,128]{1,0:T(8,128)S(1)} %chunk_sums.3.refs_1_, bf16[512,128]{1,0:T(8,128)(2,1)S(1)} %collective-permute-done.11.refs_2_, bf16[512,128]{1,0:T(8,128)(2,1)S(1)} %collective-permute-done.12.refs_3_), custom_call_target="tpu_custom_call" | custom-call | tf_op jit(solution)/shard_map/accumulate/pallas_call | solution.py:281
  (1 shorter events, 0.0 us)
Async XLA Ops:
  1.4 2.7 %collective-permute-start.1 = (bf16[2,512,128]{2,1,0:T(8,128)(2,1)S(1)}, bf16[2,512,128]{2,1,0:T(8,128)(2,1)S(1)}, u32[]{:S(2)}, u32[]{:S(2)}) collective-permute-start(bf16[2,512,128]{2,1,0:T(8,128)(2,1)S(1)} %get-tuple-element.19.own_ref), channel_id=1, source_target_pairs={{2,16},{6,20},{10,17},{14,21},{3,0},{7,4},{11,9},{15,13},{1,8},{5,... | collective-permute-start | bytes 786440 | tf_op jit(solution)/shard_map/ppermute | solution.py:305
  2.1 3.4 %collective-permute-start.3 = (bf16[2,512,128]{2,1,0:T(8,128)(2,1)S(1)}, bf16[2,512,128]{2,1,0:T(8,128)(2,1)S(1)}, u32[]{:S(2)}, u32[]{:S(2)}) collective-permute-start(bf16[2,512,128]{2,1,0:T(8,128)(2,1)S(1)} %get-tuple-element.20), channel_id=1, source_target_pairs={{2,20},{6,16},{10,21},{14,17},{3,0},{7,5},{11,9},{15,12},{0,4},{1,... | collective-permute-start | bytes 786440 | tf_op jit(solution)/shard_map/ppermute | solution.py:305
  2.8 6.5 %collective-permute-start = (bf16[2,512,128]{2,1,0:T(8,128)(2,1)S(1)}, bf16[2,512,128]{2,1,0:T(8,128)(2,1)S(1)}, u32[]{:S(2)}, u32[]{:S(2)}) collective-permute-start(bf16[2,512,128]{2,1,0:T(8,128)(2,1)S(1)} %get-tuple-element.17.own_ref), channel_id=1, source_target_pairs={{2,16},{6,20},{10,17},{14,21},{3,0},{7,4},{11,9},{15,13},{1,8},{5,... | collective-permute-start | bytes 786440 | tf_op jit(solution)/shard_map/ppermute | solution.py:305
  3.4 7.1 %collective-permute-start.7 = (bf16[2,512,128]{2,1,0:T(8,128)(2,1)S(1)}, bf16[2,512,128]{2,1,0:T(8,128)(2,1)S(1)}, u32[]{:S(2)}, u32[]{:S(2)}) collective-permute-start(bf16[2,512,128]{2,1,0:T(8,128)(2,1)S(1)} %get-tuple-element.25), channel_id=1, source_target_pairs={{2,20},{6,16},{10,21},{14,17},{3,0},{7,5},{11,9},{15,12},{0,4},{1,... | collective-permute-start | bytes 786440 | tf_op jit(solution)/shard_map/ppermute | solution.py:305
  4.1 16.6 %collective-permute-start.2 = (bf16[2,512,128]{2,1,0:T(8,128)(2,1)S(1)}, bf16[2,512,128]{2,1,0:T(8,128)(2,1)S(1)}, u32[]{:S(2)}, u32[]{:S(2)}) collective-permute-start(bf16[2,512,128]{2,1,0:T(8,128)(2,1)S(1)} %collective-permute-done.1.refs_0_), channel_id=1, source_target_pairs={{0,24},{4,28},{9,25},{13,29}} | collective-permute-start | bytes 786440 | tf_op jit(solution)/shard_map/ppermute | solution.py:305
  5.4 25.6 %collective-permute-start.4 = (bf16[2,512,128]{2,1,0:T(8,128)(2,1)S(1)}, bf16[2,512,128]{2,1,0:T(8,128)(2,1)S(1)}, u32[]{:S(2)}, u32[]{:S(2)}) collective-permute-start(bf16[2,512,128]{2,1,0:T(8,128)(2,1)S(1)} %collective-permute-done.3.refs_2_), channel_id=1, source_target_pairs={{0,28},{5,24},{9,29},{12,25},{1,12}} | collective-permute-start | bytes 786440 | tf_op jit(solution)/shard_map/ppermute | solution.py:305
  9.2 23.9 %collective-permute-start.6 = (bf16[2,512,128]{2,1,0:T(8,128)(2,1)S(1)}, bf16[2,512,128]{2,1,0:T(8,128)(2,1)S(1)}, u32[]{:S(2)}, u32[]{:S(2)}) collective-permute-start(bf16[2,512,128]{2,1,0:T(8,128)(2,1)S(1)} %collective-permute-done.refs_0_), channel_id=1, source_target_pairs={{0,24},{4,28},{9,25},{13,29}} | collective-permute-start | bytes 786440 | tf_op jit(solution)/shard_map/ppermute | solution.py:305
  10.5 24.0 %collective-permute-start.8 = (bf16[2,512,128]{2,1,0:T(8,128)(2,1)S(1)}, bf16[2,512,128]{2,1,0:T(8,128)(2,1)S(1)}, u32[]{:S(2)}, u32[]{:S(2)}) collective-permute-start(bf16[2,512,128]{2,1,0:T(8,128)(2,1)S(1)} %collective-permute-done.7.refs_2_), channel_id=1, source_target_pairs={{0,28},{5,24},{9,29},{12,25},{1,12}} | collective-permute-start | bytes 786440 | tf_op jit(solution)/shard_map/ppermute | solution.py:305
  31.8 7.3 %collective-permute-start.5 = (bf16[512,128]{1,0:T(8,128)(2,1)S(1)}, bf16[512,128]{1,0:T(8,128)(2,1)S(1)}, u32[]{:S(2)}, u32[]{:S(2)}) collective-permute-start(bf16[512,128]{1,0:T(8,128)(2,1)S(1)} %get-tuple-element.22), channel_id=1, source_target_pairs={{0,3},{4,7},{8,11},{9,10},{12,15},{13,14},{16,18},{17,19},{20,22},... | collective-permute-start | bytes 393224 | tf_op jit(solution)/shard_map/ppermute | solution.py:305
  35.3 5.3 %collective-permute-start.10 = (bf16[512,128]{1,0:T(8,128)(2,1)S(1)}, bf16[512,128]{1,0:T(8,128)(2,1)S(1)}, u32[]{:S(2)}, u32[]{:S(2)}) collective-permute-start(bf16[512,128]{1,0:T(8,128)(2,1)S(1)} %get-tuple-element.27), channel_id=1, source_target_pairs={{0,2},{4,6},{8,10},{9,11},{12,14},{13,15},{16,19},{17,18},{20,23},... | collective-permute-start | bytes 393224 | tf_op jit(solution)/shard_map/ppermute | solution.py:305
  36.6 4.0 %collective-permute-start.9 = (bf16[512,128]{1,0:T(8,128)(2,1)S(1)}, bf16[512,128]{1,0:T(8,128)(2,1)S(1)}, u32[]{:S(2)}, u32[]{:S(2)}) collective-permute-start(bf16[512,128]{1,0:T(8,128)(2,1)S(1)} %get-tuple-element.27), channel_id=1, source_target_pairs={{0,3},{4,7},{8,11},{9,10},{12,15},{13,14},{16,18},{17,19},{20,22},... | collective-permute-start | bytes 393224 | tf_op jit(solution)/shard_map/ppermute | solution.py:305
  37.9 3.2 %collective-permute-start.12 = (bf16[512,128]{1,0:T(8,128)(2,1)S(1)}, bf16[512,128]{1,0:T(8,128)(2,1)S(1)}, u32[]{:S(2)}, u32[]{:S(2)}) collective-permute-start(bf16[512,128]{1,0:T(8,128)(2,1)S(1)} %get-tuple-element.27), channel_id=1, source_target_pairs={{0,1},{4,5},{8,9},{12,13},{16,17},{18,19},{20,21},{22,23},{24,25},... | collective-permute-start | bytes 393224 | tf_op jit(solution)/shard_map/ppermute | solution.py:305
  39.2 3.2 %collective-permute-start.11 = (bf16[512,128]{1,0:T(8,128)(2,1)S(1)}, bf16[512,128]{1,0:T(8,128)(2,1)S(1)}, u32[]{:S(2)}, u32[]{:S(2)}) collective-permute-start(bf16[512,128]{1,0:T(8,128)(2,1)S(1)} %get-tuple-element.28), channel_id=1, source_target_pairs={{0,1},{2,3},{4,5},{6,7},{8,9},{10,11},{12,13},{14,15},{16,17},{18,... | collective-permute-start | bytes 393224 | tf_op jit(solution)/shard_map/ppermute | solution.py:305

commit v6 on v5

--- a/solution.py
+++ b/solution.py
@@ -196,24 +196,25 @@
     return jnp.dot(both_ref[k], jnp.concatenate([green, diff], axis=0), preferred_element_type=F32)
 
 
-def partial(both, own, wins, brings, first, width, scale):
+def partial(both, own, wins, brings, first, width, scale, shifts, before=()):
     ratio, rows, _ = both.shape
     cols = own.shape[-1]
-    counts = [len(pieces) for pieces in wins]
+    counts = [len(wins[s]) for s in shifts]
     col_devices = lax.axis_size("col")
+    shapes = [held((rows, cols), F32)] + [held((rows, cols), BF16)] * (ratio - 1 in shifts)
 
     def kernel(both_ref, own_ref, *refs):
-        outs = refs[-2:]
+        outs = refs[len(refs) - len(shapes) :]
         my_row, my_col = place()
         some = my_col <= my_row // ratio
 
         @pl.when(some)
         def _():
-            total, at = None, 0
-            for s in range(ratio):
+            total, at = None, len(before)
+            for s, count in zip(shifts, counts):
                 k = lax.rem(my_row + ratio - s, ratio)
-                mine = refs[at : at + counts[s]]
-                at += counts[s]
+                mine = refs[at : at + count]
+                at += count
                 valid = member(brings[s], my_row * col_devices + my_col)
 
                 def win(i, s=s, mine=mine, valid=valid):
@@ -227,23 +228,24 @@
                 term = block_term(both_ref, k, win, my_row, my_col, rows, width, first)
                 total = term if total is None else total + term
             total = scale * total
-            outs[0][...] = total
-            outs[1][...] = total.astype(BF16)
+            if before:
+                total = total + refs[0][...]
+            for ref in outs:
+                ref[...] = total.astype(ref.dtype)
 
         @pl.when(jnp.logical_not(some))
         def _():
             for ref in outs:
                 ref[...] = jnp.zeros(ref.shape, ref.dtype)
 
-    shapes = [held((rows, cols), F32), held((rows, cols), BF16)]
     return pl.pallas_call(
         kernel,
         out_shape=shapes,
-        in_specs=[pl.BlockSpec(memory_space=pltpu.VMEM)] * (2 + sum(counts)),
+        in_specs=[pl.BlockSpec(memory_space=pltpu.VMEM)] * (2 + len(before) + sum(counts)),
         out_specs=[pl.BlockSpec(memory_space=pltpu.VMEM)] * len(shapes),
         compiler_params=ROOM,
         name="partial",
-    )(*map(keep, [both, own]), *[keep(x) for pieces in wins for x in pieces])
+    )(*map(keep, [both, own, *before]), *[keep(x) for s in shifts for x in wins[s]])
 
 
 def chunk_sums(part, got, relayed):
@@ -316,7 +318,11 @@
     for q in range(chunks):
         mine = [wins[s, q] for s in range(ratio)]
         brings = [plan[s, q][3] for s in range(ratio)]
-        part, out = partial(both, ready[0, q], mine, brings, q * LANES, width, scale)
+        steps = [range(ratio)] if q < chunks - 1 else [[s] for s in range(ratio)]
+        found = ()
+        for shifts in steps:
+            found = partial(both, ready[0, q], mine, brings, q * LANES, width, scale, shifts, found)
+        part, out = found
         if q < chunks - 1:
             total, message = chunk_sums(part, [send(out, pairs) for pairs in across], True)
             came.append(send(message, along))

time: 43.7 us -> 43.4 us (level)
  waiting for transfers between devices: 22.5 us -> 22 us
    ppermute x13, waiting for transfers between devices: 22.5 us -> 22 us  [send(): return lax.ppermute(x, AXES, pairs)]
    pallas_call x2 -> x3, Pallas kernels: 1.5 us -> 1.72 us  [partial(): pl.pallas_call(kernel, out_shape=shapes, in_specs=[pl.BlockSpec(memory_sp...]
  transfers between devices with their start and end apart: 13 -> 13, of which waited for: 5 -> 5; matrix products, arithmetic and copies ran while one was open for 0% -> 0% of each run, Pallas kernels for 9% -> 10%
where the time goes in v6:
time: 43.4 us; the launch traced here: 43 us
  waiting for transfers between devices  22 us (51%)
  starting transfers between devices  14.4 us (33%)
  Pallas kernels  6.49 us (15%)
    ppermute x13, waiting for transfers between devices, send(): return lax.ppermute(x, AXES, pairs)  22 us
    ppermute x13, starting transfers between devices, send(): return lax.ppermute(x, AXES, pairs)  14.4 us
    pallas_call x1, Pallas kernels, sigmas(): pl.pallas_call(kernel, out_shape=held((ratio, rows, 2 * rows), BF16), in_...  2.46 us
    pallas_call x3, Pallas kernels, partial(): pl.pallas_call(kernel, out_shape=shapes, in_specs=[pl.BlockSpec(memory_sp...  1.72 us
    pallas_call x1, Pallas kernels, pack(): pl.pallas_call(kernel, out_shape=[held((2, r1 - r0, c1 - c0), BF16) for _...  1.38 us
  transfers between devices with their start and end apart: 13, of which 5 were waited for; matrix products, arithmetic and copies ran while one was open for 0% of the time, Pallas kernels for 10%

profile of v6, /device:TPU:25, one launch (start us, length us, event | category | flops | bytes accessed | tf_op | source)
XLA Modules:
  0.0 43.0 jit_solution(18412327333120684562)
XLA Ops:
  0.0 1.4 %pack_windows.1 = (bf16[2,512,128]{2,1,0:T(8,128)(2,1)S(1)}, bf16[2,512,128]{2,1,0:T(8,128)(2,1)S(1)}, bf16[2,512,128]{2,1,0:T(8,128)(2,1)S(1)}, bf16[2,512,128]{2,1,0:T(8,128)(2,1)S(1)}) custom-call(bf16[512,1024]{1,0:T(8,128)(2,1)} %refs_0_.1, bf16[512,1024]{1,0:T(8,128)(2,1)} %refs_1_.1), custom_call_target="tpu_custom_call" | custom-call | tf_op jit(solution)/shard_map/pack_windows/pallas_call | solution.py:137
  1.4 0.7 %collective-permute-start.1 = (bf16[2,512,128]{2,1,0:T(8,128)(2,1)S(1)}, bf16[2,512,128]{2,1,0:T(8,128)(2,1)S(1)}, u32[]{:S(2)}, u32[]{:S(2)}) collective-permute-start(bf16[2,512,128]{2,1,0:T(8,128)(2,1)S(1)} %get-tuple-element.19.own_ref), channel_id=1, source_target_pairs={{2,16},{6,20},{10,17},{14,21},{3,0},{7,4},{11,9},{15,13},{1,8},{5,... | collective-permute-start | bytes 786440 | tf_op jit(solution)/shard_map/ppermute | solution.py:307
  2.1 0.7 %collective-permute-start.3 = (bf16[2,512,128]{2,1,0:T(8,128)(2,1)S(1)}, bf16[2,512,128]{2,1,0:T(8,128)(2,1)S(1)}, u32[]{:S(2)}, u32[]{:S(2)}) collective-permute-start(bf16[2,512,128]{2,1,0:T(8,128)(2,1)S(1)} %get-tuple-element.20), channel_id=1, source_target_pairs={{2,20},{6,16},{10,21},{14,17},{3,0},{7,5},{11,9},{15,12},{0,4},{1,... | collective-permute-start | bytes 786440 | tf_op jit(solution)/shard_map/ppermute | solution.py:307
  2.8 0.7 %collective-permute-start = (bf16[2,512,128]{2,1,0:T(8,128)(2,1)S(1)}, bf16[2,512,128]{2,1,0:T(8,128)(2,1)S(1)}, u32[]{:S(2)}, u32[]{:S(2)}) collective-permute-start(bf16[2,512,128]{2,1,0:T(8,128)(2,1)S(1)} %get-tuple-element.17.own_ref), channel_id=1, source_target_pairs={{2,16},{6,20},{10,17},{14,21},{3,0},{7,4},{11,9},{15,13},{1,8},{5,... | collective-permute-start | bytes 786440 | tf_op jit(solution)/shard_map/ppermute | solution.py:307
  3.4 0.7 %collective-permute-start.7 = (bf16[2,512,128]{2,1,0:T(8,128)(2,1)S(1)}, bf16[2,512,128]{2,1,0:T(8,128)(2,1)S(1)}, u32[]{:S(2)}, u32[]{:S(2)}) collective-permute-start(bf16[2,512,128]{2,1,0:T(8,128)(2,1)S(1)} %get-tuple-element.25), channel_id=1, source_target_pairs={{2,20},{6,16},{10,21},{14,17},{3,0},{7,5},{11,9},{15,12},{0,4},{1,... | collective-permute-start | bytes 786440 | tf_op jit(solution)/shard_map/ppermute | solution.py:307
  4.1 0.0 collective-permute-done.1.refs_0_
  4.1 1.3 %collective-permute-start.2 = (bf16[2,512,128]{2,1,0:T(8,128)(2,1)S(1)}, bf16[2,512,128]{2,1,0:T(8,128)(2,1)S(1)}, u32[]{:S(2)}, u32[]{:S(2)}) collective-permute-start(bf16[2,512,128]{2,1,0:T(8,128)(2,1)S(1)} %collective-permute-done.1.refs_0_), channel_id=1, source_target_pairs={{0,24},{4,28},{9,25},{13,29}} | collective-permute-start | bytes 786440 | tf_op jit(solution)/shard_map/ppermute | solution.py:307
  5.4 0.0 collective-permute-done.3.refs_2_
  5.4 1.3 %collective-permute-start.4 = (bf16[2,512,128]{2,1,0:T(8,128)(2,1)S(1)}, bf16[2,512,128]{2,1,0:T(8,128)(2,1)S(1)}, u32[]{:S(2)}, u32[]{:S(2)}) collective-permute-start(bf16[2,512,128]{2,1,0:T(8,128)(2,1)S(1)} %collective-permute-done.3.refs_2_), channel_id=1, source_target_pairs={{0,28},{5,24},{9,29},{12,25},{1,12}} | collective-permute-start | bytes 786440 | tf_op jit(solution)/shard_map/ppermute | solution.py:307
  6.7 2.5 %sigma_blocks.1.both_ref = bf16[2,512,1024]{2,1,0:T(8,128)(2,1)S(1)} custom-call(bf16[512,1024]{1,0:T(8,128)(2,1)} %refs_0_.1, bf16[512,1024]{1,0:T(8,128)(2,1)} %refs_1_.1, bf16[512,1024]{1,0:T(8,128)(2,1)} %refs_2_.1, bf16[512,1024]{1,0:T(8,128)(2,1)} %refs_3_.1), custom_call_target="tpu_custom_call" | custom-call | tf_op jit(solution)/shard_map/sigma_blocks/pallas_call | solution.py:179
  9.2 0.0 collective-permute-done.refs_0_
  9.2 1.3 %collective-permute-start.6 = (bf16[2,512,128]{2,1,0:T(8,128)(2,1)S(1)}, bf16[2,512,128]{2,1,0:T(8,128)(2,1)S(1)}, u32[]{:S(2)}, u32[]{:S(2)}) collective-permute-start(bf16[2,512,128]{2,1,0:T(8,128)(2,1)S(1)} %collective-permute-done.refs_0_), channel_id=1, source_target_pairs={{0,24},{4,28},{9,25},{13,29}} | collective-permute-start | bytes 786440 | tf_op jit(solution)/shard_map/ppermute | solution.py:307
  10.5 0.0 collective-permute-done.7.refs_1_
  10.5 1.3 %collective-permute-start.8 = (bf16[2,512,128]{2,1,0:T(8,128)(2,1)S(1)}, bf16[2,512,128]{2,1,0:T(8,128)(2,1)S(1)}, u32[]{:S(2)}, u32[]{:S(2)}) collective-permute-start(bf16[2,512,128]{2,1,0:T(8,128)(2,1)S(1)} %collective-permute-done.7.refs_1_), channel_id=1, source_target_pairs={{0,28},{5,24},{9,29},{12,25},{1,12}} | collective-permute-start | bytes 786440 | tf_op jit(solution)/shard_map/ppermute | solution.py:307
  11.8 8.9 %collective-permute-done.2.refs_1_ = bf16[2,512,128]{2,1,0:T(8,128)(2,1)S(1)} collective-permute-done((bf16[2,512,128]{2,1,0:T(8,128)(2,1)S(1)}, bf16[2,512,128]{2,1,0:T(8,128)(2,1)S(1)}, u32[]{:S(2)}, u32[]{:S(2)}) %collective-permute-start.2) | collective-permute-done | bytes 262176 | tf_op jit(solution)/shard_map/ppermute | solution.py:307
  20.7 10.3 %collective-permute-done.4.refs_3_ = bf16[2,512,128]{2,1,0:T(8,128)(2,1)S(1)} collective-permute-done((bf16[2,512,128]{2,1,0:T(8,128)(2,1)S(1)}, bf16[2,512,128]{2,1,0:T(8,128)(2,1)S(1)}, u32[]{:S(2)}, u32[]{:S(2)}) %collective-permute-start.4) | collective-permute-done | bytes 262176 | tf_op jit(solution)/shard_map/ppermute | solution.py:307
  31.1 0.8 %partial.3 = (f32[512,128]{1,0:T(8,128)S(1)}, bf16[512,128]{1,0:T(8,128)(2,1)S(1)}) custom-call(bf16[2,512,1024]{2,1,0:T(8,128)(2,1)S(1)} %sigma_blocks.1.both_ref, bf16[2,512,128]{2,1,0:T(8,128)(2,1)S(1)} %get-tuple-element.19.own_ref, bf16[2,512,128]{2,1,0:T(8,128)(2,1)S(1)} %collective-permute-done.1.refs_0_, ...), custom_call_target="tpu_custom_call" | custom-call | tf_op jit(solution)/shard_map/partial/pallas_call | solution.py:241
  31.8 1.3 %collective-permute-start.5 = (bf16[512,128]{1,0:T(8,128)(2,1)S(1)}, bf16[512,128]{1,0:T(8,128)(2,1)S(1)}, u32[]{:S(2)}, u32[]{:S(2)}) collective-permute-start(bf16[512,128]{1,0:T(8,128)(2,1)S(1)} %get-tuple-element.22), channel_id=1, source_target_pairs={{0,3},{4,7},{8,11},{9,10},{12,15},{13,14},{16,18},{17,19},{20,22},... | collective-permute-start | bytes 393224 | tf_op jit(solution)/shard_map/ppermute | solution.py:307
  33.1 0.0 collective-permute-done.6.refs_1_
  33.1 0.5 %partial.4.refs_0_ = f32[512,128]{1,0:T(8,128)S(1)} custom-call(bf16[2,512,1024]{2,1,0:T(8,128)(2,1)S(1)} %sigma_blocks.1.both_ref, bf16[2,512,128]{2,1,0:T(8,128)(2,1)S(1)} %get-tuple-element.17.own_ref, bf16[2,512,128]{2,1,0:T(8,128)(2,1)S(1)} %collective-permute-done.refs_0_, bf16[2,512,128]{2,1,0:T(8,128)(2,1)S(1)} %collective-permute-done.6.refs_1_), custom_call_target="tpu_custom_call" | custom-call | tf_op jit(solution)/shard_map/partial/pallas_call | solution.py:241
  33.7 0.8 %collective-permute-done.8.refs_2_ = bf16[2,512,128]{2,1,0:T(8,128)(2,1)S(1)} collective-permute-done((bf16[2,512,128]{2,1,0:T(8,128)(2,1)S(1)}, bf16[2,512,128]{2,1,0:T(8,128)(2,1)S(1)}, u32[]{:S(2)}, u32[]{:S(2)}) %collective-permute-start.8) | collective-permute-done | bytes 262176 | tf_op jit(solution)/shard_map/ppermute | solution.py:307
  34.5 0.5 %partial.5 = (f32[512,128]{1,0:T(8,128)S(1)}, bf16[512,128]{1,0:T(8,128)(2,1)S(1)}) custom-call(bf16[2,512,1024]{2,1,0:T(8,128)(2,1)S(1)} %sigma_blocks.1.both_ref, bf16[2,512,128]{2,1,0:T(8,128)(2,1)S(1)} %get-tuple-element.17.own_ref, f32[512,128]{1,0:T(8,128)S(1)} %partial.4.refs_0_, bf16[2,512,128]{2,1,0:T(8,128)(2,1)S(1)} %collective-permute-done.7.refs_1_, ...), custom_call_target="tpu_custom_call" | custom-call | tf_op jit(solution)/shard_map/partial/pallas_call | solution.py:241
  35.0 1.3 %collective-permute-start.10 = (bf16[512,128]{1,0:T(8,128)(2,1)S(1)}, bf16[512,128]{1,0:T(8,128)(2,1)S(1)}, u32[]{:S(2)}, u32[]{:S(2)}) collective-permute-start(bf16[512,128]{1,0:T(8,128)(2,1)S(1)} %get-tuple-element.27), channel_id=1, source_target_pairs={{0,2},{4,6},{8,10},{9,11},{12,14},{13,15},{16,19},{17,18},{20,23},... | collective-permute-start | bytes 393224 | tf_op jit(solution)/shard_map/ppermute | solution.py:307
  36.3 1.3 %collective-permute-start.9 = (bf16[512,128]{1,0:T(8,128)(2,1)S(1)}, bf16[512,128]{1,0:T(8,128)(2,1)S(1)}, u32[]{:S(2)}, u32[]{:S(2)}) collective-permute-start(bf16[512,128]{1,0:T(8,128)(2,1)S(1)} %get-tuple-element.27), channel_id=1, source_target_pairs={{0,3},{4,7},{8,11},{9,10},{12,15},{13,14},{16,18},{17,19},{20,22},... | collective-permute-start | bytes 393224 | tf_op jit(solution)/shard_map/ppermute | solution.py:307
  37.6 1.3 %collective-permute-start.12 = (bf16[512,128]{1,0:T(8,128)(2,1)S(1)}, bf16[512,128]{1,0:T(8,128)(2,1)S(1)}, u32[]{:S(2)}, u32[]{:S(2)}) collective-permute-start(bf16[512,128]{1,0:T(8,128)(2,1)S(1)} %get-tuple-element.27), channel_id=1, source_target_pairs={{0,1},{4,5},{8,9},{12,13},{16,17},{18,19},{20,21},{22,23},{24,25},... | collective-permute-start | bytes 393224 | tf_op jit(solution)/shard_map/ppermute | solution.py:307
  38.9 0.0 collective-permute-done.5.refs_0_
  38.9 0.1 chunk_sums.2
  39.0 1.3 %collective-permute-start.11 = (bf16[512,128]{1,0:T(8,128)(2,1)S(1)}, bf16[512,128]{1,0:T(8,128)(2,1)S(1)}, u32[]{:S(2)}, u32[]{:S(2)}) collective-permute-start(bf16[512,128]{1,0:T(8,128)(2,1)S(1)} %get-tuple-element.28), channel_id=1, source_target_pairs={{0,1},{2,3},{4,5},{6,7},{8,9},{10,11},{12,13},{14,15},{16,17},{18,... | collective-permute-start | bytes 393224 | tf_op jit(solution)/shard_map/ppermute | solution.py:307
  40.3 0.0 collective-permute-done.10.refs_1_
  40.3 0.5 %collective-permute-done.12.refs_3_ = bf16[512,128]{1,0:T(8,128)(2,1)S(1)} collective-permute-done((bf16[512,128]{1,0:T(8,128)(2,1)S(1)}, bf16[512,128]{1,0:T(8,128)(2,1)S(1)}, u32[]{:S(2)}, u32[]{:S(2)}) %collective-permute-start.12) | collective-permute-done | bytes 131104 | tf_op jit(solution)/shard_map/ppermute | solution.py:307
  40.8 1.4 %collective-permute-done.11.refs_2_ = bf16[512,128]{1,0:T(8,128)(2,1)S(1)} collective-permute-done((bf16[512,128]{1,0:T(8,128)(2,1)S(1)}, bf16[512,128]{1,0:T(8,128)(2,1)S(1)}, u32[]{:S(2)}, u32[]{:S(2)}) %collective-permute-start.11) | collective-permute-done | bytes 131104 | tf_op jit(solution)/shard_map/ppermute | solution.py:307
  42.2 0.8 %accumulate.1 = f32[512,256]{1,0:T(8,128)} custom-call(f32[512,128]{1,0:T(8,128)S(1)} %get-tuple-element.23.refs_0_, f32[512,128]{1,0:T(8,128)S(1)} %chunk_sums.3.refs_1_, bf16[512,128]{1,0:T(8,128)(2,1)S(1)} %collective-permute-done.11.refs_2_, bf16[512,128]{1,0:T(8,128)(2,1)S(1)} %collective-permute-done.12.refs_3_), custom_call_target="tpu_custom_call" | custom-call | tf_op jit(solution)/shard_map/accumulate/pallas_call | solution.py:283
  (2 shorter events, 0.0 us)
Async XLA Ops:
  1.4 2.7 %collective-permute-start.1 = (bf16[2,512,128]{2,1,0:T(8,128)(2,1)S(1)}, bf16[2,512,128]{2,1,0:T(8,128)(2,1)S(1)}, u32[]{:S(2)}, u32[]{:S(2)}) collective-permute-start(bf16[2,512,128]{2,1,0:T(8,128)(2,1)S(1)} %get-tuple-element.19.own_ref), channel_id=1, source_target_pairs={{2,16},{6,20},{10,17},{14,21},{3,0},{7,4},{11,9},{15,13},{1,8},{5,... | collective-permute-start | bytes 786440 | tf_op jit(solution)/shard_map/ppermute | solution.py:307
  2.1 3.4 %collective-permute-start.3 = (bf16[2,512,128]{2,1,0:T(8,128)(2,1)S(1)}, bf16[2,512,128]{2,1,0:T(8,128)(2,1)S(1)}, u32[]{:S(2)}, u32[]{:S(2)}) collective-permute-start(bf16[2,512,128]{2,1,0:T(8,128)(2,1)S(1)} %get-tuple-element.20), channel_id=1, source_target_pairs={{2,20},{6,16},{10,21},{14,17},{3,0},{7,5},{11,9},{15,12},{0,4},{1,... | collective-permute-start | bytes 786440 | tf_op jit(solution)/shard_map/ppermute | solution.py:307
  2.8 6.5 %collective-permute-start = (bf16[2,512,128]{2,1,0:T(8,128)(2,1)S(1)}, bf16[2,512,128]{2,1,0:T(8,128)(2,1)S(1)}, u32[]{:S(2)}, u32[]{:S(2)}) collective-permute-start(bf16[2,512,128]{2,1,0:T(8,128)(2,1)S(1)} %get-tuple-element.17.own_ref), channel_id=1, source_target_pairs={{2,16},{6,20},{10,17},{14,21},{3,0},{7,4},{11,9},{15,13},{1,8},{5,... | collective-permute-start | bytes 786440 | tf_op jit(solution)/shard_map/ppermute | solution.py:307
  3.4 7.1 %collective-permute-start.7 = (bf16[2,512,128]{2,1,0:T(8,128)(2,1)S(1)}, bf16[2,512,128]{2,1,0:T(8,128)(2,1)S(1)}, u32[]{:S(2)}, u32[]{:S(2)}) collective-permute-start(bf16[2,512,128]{2,1,0:T(8,128)(2,1)S(1)} %get-tuple-element.25), channel_id=1, source_target_pairs={{2,20},{6,16},{10,21},{14,17},{3,0},{7,5},{11,9},{15,12},{0,4},{1,... | collective-permute-start | bytes 786440 | tf_op jit(solution)/shard_map/ppermute | solution.py:307
  4.1 16.6 %collective-permute-start.2 = (bf16[2,512,128]{2,1,0:T(8,128)(2,1)S(1)}, bf16[2,512,128]{2,1,0:T(8,128)(2,1)S(1)}, u32[]{:S(2)}, u32[]{:S(2)}) collective-permute-start(bf16[2,512,128]{2,1,0:T(8,128)(2,1)S(1)} %collective-permute-done.1.refs_0_), channel_id=1, source_target_pairs={{0,24},{4,28},{9,25},{13,29}} | collective-permute-start | bytes 786440 | tf_op jit(solution)/shard_map/ppermute | solution.py:307
  5.4 25.6 %collective-permute-start.4 = (bf16[2,512,128]{2,1,0:T(8,128)(2,1)S(1)}, bf16[2,512,128]{2,1,0:T(8,128)(2,1)S(1)}, u32[]{:S(2)}, u32[]{:S(2)}) collective-permute-start(bf16[2,512,128]{2,1,0:T(8,128)(2,1)S(1)} %collective-permute-done.3.refs_2_), channel_id=1, source_target_pairs={{0,28},{5,24},{9,29},{12,25},{1,12}} | collective-permute-start | bytes 786440 | tf_op jit(solution)/shard_map/ppermute | solution.py:307
  9.2 23.9 %collective-permute-start.6 = (bf16[2,512,128]{2,1,0:T(8,128)(2,1)S(1)}, bf16[2,512,128]{2,1,0:T(8,128)(2,1)S(1)}, u32[]{:S(2)}, u32[]{:S(2)}) collective-permute-start(bf16[2,512,128]{2,1,0:T(8,128)(2,1)S(1)} %collective-permute-done.refs_0_), channel_id=1, source_target_pairs={{0,24},{4,28},{9,25},{13,29}} | collective-permute-start | bytes 786440 | tf_op jit(solution)/shard_map/ppermute | solution.py:307
  10.5 24.0 %collective-permute-start.8 = (bf16[2,512,128]{2,1,0:T(8,128)(2,1)S(1)}, bf16[2,512,128]{2,1,0:T(8,128)(2,1)S(1)}, u32[]{:S(2)}, u32[]{:S(2)}) collective-permute-start(bf16[2,512,128]{2,1,0:T(8,128)(2,1)S(1)} %collective-permute-done.7.refs_1_), channel_id=1, source_target_pairs={{0,28},{5,24},{9,29},{12,25},{1,12}} | collective-permute-start | bytes 786440 | tf_op jit(solution)/shard_map/ppermute | solution.py:307
  31.8 7.1 %collective-permute-start.5 = (bf16[512,128]{1,0:T(8,128)(2,1)S(1)}, bf16[512,128]{1,0:T(8,128)(2,1)S(1)}, u32[]{:S(2)}, u32[]{:S(2)}) collective-permute-start(bf16[512,128]{1,0:T(8,128)(2,1)S(1)} %get-tuple-element.22), channel_id=1, source_target_pairs={{0,3},{4,7},{8,11},{9,10},{12,15},{13,14},{16,18},{17,19},{20,22},... | collective-permute-start | bytes 393224 | tf_op jit(solution)/shard_map/ppermute | solution.py:307
  35.0 5.3 %collective-permute-start.10 = (bf16[512,128]{1,0:T(8,128)(2,1)S(1)}, bf16[512,128]{1,0:T(8,128)(2,1)S(1)}, u32[]{:S(2)}, u32[]{:S(2)}) collective-permute-start(bf16[512,128]{1,0:T(8,128)(2,1)S(1)} %get-tuple-element.27), channel_id=1, source_target_pairs={{0,2},{4,6},{8,10},{9,11},{12,14},{13,15},{16,19},{17,18},{20,23},... | collective-permute-start | bytes 393224 | tf_op jit(solution)/shard_map/ppermute | solution.py:307
  36.3 4.0 %collective-permute-start.9 = (bf16[512,128]{1,0:T(8,128)(2,1)S(1)}, bf16[512,128]{1,0:T(8,128)(2,1)S(1)}, u32[]{:S(2)}, u32[]{:S(2)}) collective-permute-start(bf16[512,128]{1,0:T(8,128)(2,1)S(1)} %get-tuple-element.27), channel_id=1, source_target_pairs={{0,3},{4,7},{8,11},{9,10},{12,15},{13,14},{16,18},{17,19},{20,22},... | collective-permute-start | bytes 393224 | tf_op jit(solution)/shard_map/ppermute | solution.py:307
  37.6 3.2 %collective-permute-start.12 = (bf16[512,128]{1,0:T(8,128)(2,1)S(1)}, bf16[512,128]{1,0:T(8,128)(2,1)S(1)}, u32[]{:S(2)}, u32[]{:S(2)}) collective-permute-start(bf16[512,128]{1,0:T(8,128)(2,1)S(1)} %get-tuple-element.27), channel_id=1, source_target_pairs={{0,1},{4,5},{8,9},{12,13},{16,17},{18,19},{20,21},{22,23},{24,25},... | collective-permute-start | bytes 393224 | tf_op jit(solution)/shard_map/ppermute | solution.py:307
  39.0 3.2 %collective-permute-start.11 = (bf16[512,128]{1,0:T(8,128)(2,1)S(1)}, bf16[512,128]{1,0:T(8,128)(2,1)S(1)}, u32[]{:S(2)}, u32[]{:S(2)}) collective-permute-start(bf16[512,128]{1,0:T(8,128)(2,1)S(1)} %get-tuple-element.28), channel_id=1, source_target_pairs={{0,1},{2,3},{4,5},{6,7},{8,9},{10,11},{12,13},{14,15},{16,17},{18,... | collective-permute-start | bytes 393224 | tf_op jit(solution)/shard_map/ppermute | solution.py:307

commit v7 on v6

--- a/solution.py
+++ b/solution.py
@@ -39,15 +39,12 @@
     relays, kept = set(), set()
     for z, y, src, dst in hops:
         choice = None
-        for g in range(half):
+        turn = (z + (y + 1) * (s % 2)) % 2
+        for g in range(half)[:: -1 if turn else 1]:
             relay = at(z, y, g)
-            if relay in relays or relay in kept:
-                continue
-            if relay not in near:
+            if relay not in relays and relay not in kept and near.get(relay) not in relays:
                 choice = relay
                 break
-            if choice is None and near[relay] not in relays:
-                choice = relay
         if choice is None:
             left.append((src, dst))
             continue

time: 43.4 us -> 43.4 us (level)
  transfers between devices with their start and end apart: 13 -> 13, of which waited for: 5 -> 6; matrix products, arithmetic and copies ran while one was open for 0% -> 0% of each run, Pallas kernels for 10% -> 10%
where the time goes in v7:
time: 43.4 us; the launch traced here: 43 us
  waiting for transfers between devices  22 us (51%)
  starting transfers between devices  14.4 us (33%)
  Pallas kernels  6.45 us (15%)
    ppermute x13, waiting for transfers between devices, send(): return lax.ppermute(x, AXES, pairs)  22 us
    ppermute x13, starting transfers between devices, send(): return lax.ppermute(x, AXES, pairs)  14.4 us
    pallas_call x1, Pallas kernels, sigmas(): pl.pallas_call(kernel, out_shape=held((ratio, rows, 2 * rows), BF16), in_...  2.46 us
    pallas_call x3, Pallas kernels, partial(): pl.pallas_call(kernel, out_shape=shapes, in_specs=[pl.BlockSpec(memory_sp...  1.69 us
    pallas_call x1, Pallas kernels, pack(): pl.pallas_call(kernel, out_shape=[held((2, r1 - r0, c1 - c0), BF16) for _...  1.38 us
  transfers between devices with their start and end apart: 13, of which 6 were waited for; matrix products, arithmetic and copies ran while one was open for 0% of the time, Pallas kernels for 10%

profile of v7, /device:TPU:25, one launch (start us, length us, event | category | flops | bytes accessed | tf_op | source)
XLA Modules:
  0.0 43.0 jit_solution(5061969604008709253)
XLA Ops:
  0.0 1.4 %pack_windows.1 = (bf16[2,512,128]{2,1,0:T(8,128)(2,1)S(1)}, bf16[2,512,128]{2,1,0:T(8,128)(2,1)S(1)}, bf16[2,512,128]{2,1,0:T(8,128)(2,1)S(1)}, bf16[2,512,128]{2,1,0:T(8,128)(2,1)S(1)}) custom-call(bf16[512,1024]{1,0:T(8,128)(2,1)} %refs_0_.1, bf16[512,1024]{1,0:T(8,128)(2,1)} %refs_1_.1), custom_call_target="tpu_custom_call" | custom-call | tf_op jit(solution)/shard_map/pack_windows/pallas_call | solution.py:134
  1.4 0.7 %collective-permute-start.1 = (bf16[2,512,128]{2,1,0:T(8,128)(2,1)S(1)}, bf16[2,512,128]{2,1,0:T(8,128)(2,1)S(1)}, u32[]{:S(2)}, u32[]{:S(2)}) collective-permute-start(bf16[2,512,128]{2,1,0:T(8,128)(2,1)S(1)} %get-tuple-element.19.own_ref), channel_id=1, source_target_pairs={{2,16},{6,20},{10,17},{14,21},{3,0},{7,4},{11,9},{15,13},{1,8},{5,... | collective-permute-start | bytes 786440 | tf_op jit(solution)/shard_map/ppermute | solution.py:304
  2.1 0.7 %collective-permute-start.3 = (bf16[2,512,128]{2,1,0:T(8,128)(2,1)S(1)}, bf16[2,512,128]{2,1,0:T(8,128)(2,1)S(1)}, u32[]{:S(2)}, u32[]{:S(2)}) collective-permute-start(bf16[2,512,128]{2,1,0:T(8,128)(2,1)S(1)} %get-tuple-element.20), channel_id=1, source_target_pairs={{2,20},{6,16},{10,21},{14,17},{3,1},{7,4},{11,8},{15,13},{0,0},{1,... | collective-permute-start | bytes 786440 | tf_op jit(solution)/shard_map/ppermute | solution.py:304
  2.8 0.7 %collective-permute-start = (bf16[2,512,128]{2,1,0:T(8,128)(2,1)S(1)}, bf16[2,512,128]{2,1,0:T(8,128)(2,1)S(1)}, u32[]{:S(2)}, u32[]{:S(2)}) collective-permute-start(bf16[2,512,128]{2,1,0:T(8,128)(2,1)S(1)} %get-tuple-element.17.own_ref), channel_id=1, source_target_pairs={{2,16},{6,20},{10,17},{14,21},{3,0},{7,4},{11,9},{15,13},{1,8},{5,... | collective-permute-start | bytes 786440 | tf_op jit(solution)/shard_map/ppermute | solution.py:304
  3.4 0.7 %collective-permute-start.7 = (bf16[2,512,128]{2,1,0:T(8,128)(2,1)S(1)}, bf16[2,512,128]{2,1,0:T(8,128)(2,1)S(1)}, u32[]{:S(2)}, u32[]{:S(2)}) collective-permute-start(bf16[2,512,128]{2,1,0:T(8,128)(2,1)S(1)} %get-tuple-element.25), channel_id=1, source_target_pairs={{2,20},{6,16},{10,21},{14,17},{3,1},{7,4},{11,8},{15,13},{0,0},{1,... | collective-permute-start | bytes 786440 | tf_op jit(solution)/shard_map/ppermute | solution.py:304
  4.1 0.0 collective-permute-done.1.refs_0_
  4.1 1.3 %collective-permute-start.2 = (bf16[2,512,128]{2,1,0:T(8,128)(2,1)S(1)}, bf16[2,512,128]{2,1,0:T(8,128)(2,1)S(1)}, u32[]{:S(2)}, u32[]{:S(2)}) collective-permute-start(bf16[2,512,128]{2,1,0:T(8,128)(2,1)S(1)} %collective-permute-done.1.refs_0_), channel_id=1, source_target_pairs={{0,24},{4,28},{9,25},{13,29}} | collective-permute-start | bytes 786440 | tf_op jit(solution)/shard_map/ppermute | solution.py:304
  5.4 0.0 collective-permute-done.3.refs_2_
  5.4 1.3 %collective-permute-start.4 = (bf16[2,512,128]{2,1,0:T(8,128)(2,1)S(1)}, bf16[2,512,128]{2,1,0:T(8,128)(2,1)S(1)}, u32[]{:S(2)}, u32[]{:S(2)}) collective-permute-start(bf16[2,512,128]{2,1,0:T(8,128)(2,1)S(1)} %collective-permute-done.3.refs_2_), channel_id=1, source_target_pairs={{1,28},{4,24},{8,29},{13,25},{0,4},{5,8},{9,13}} | collective-permute-start | bytes 786440 | tf_op jit(solution)/shard_map/ppermute | solution.py:304
  6.7 2.5 %sigma_blocks.1.both_ref = bf16[2,512,1024]{2,1,0:T(8,128)(2,1)S(1)} custom-call(bf16[512,1024]{1,0:T(8,128)(2,1)} %refs_0_.1, bf16[512,1024]{1,0:T(8,128)(2,1)} %refs_1_.1, bf16[512,1024]{1,0:T(8,128)(2,1)} %refs_2_.1, bf16[512,1024]{1,0:T(8,128)(2,1)} %refs_3_.1), custom_call_target="tpu_custom_call" | custom-call | tf_op jit(solution)/shard_map/sigma_blocks/pallas_call | solution.py:176
  9.2 0.0 collective-permute-done.refs_0_
  9.2 1.3 %collective-permute-start.6 = (bf16[2,512,128]{2,1,0:T(8,128)(2,1)S(1)}, bf16[2,512,128]{2,1,0:T(8,128)(2,1)S(1)}, u32[]{:S(2)}, u32[]{:S(2)}) collective-permute-start(bf16[2,512,128]{2,1,0:T(8,128)(2,1)S(1)} %collective-permute-done.refs_0_), channel_id=1, source_target_pairs={{0,24},{4,28},{9,25},{13,29}} | collective-permute-start | bytes 786440 | tf_op jit(solution)/shard_map/ppermute | solution.py:304
  10.5 0.0 collective-permute-done.7.refs_1_
  10.5 1.3 %collective-permute-start.8 = (bf16[2,512,128]{2,1,0:T(8,128)(2,1)S(1)}, bf16[2,512,128]{2,1,0:T(8,128)(2,1)S(1)}, u32[]{:S(2)}, u32[]{:S(2)}) collective-permute-start(bf16[2,512,128]{2,1,0:T(8,128)(2,1)S(1)} %collective-permute-done.7.refs_1_), channel_id=1, source_target_pairs={{1,28},{4,24},{8,29},{13,25},{0,4},{5,8},{9,13}} | collective-permute-start | bytes 786440 | tf_op jit(solution)/shard_map/ppermute | solution.py:304
  11.8 5.7 %collective-permute-done.2.refs_1_ = bf16[2,512,128]{2,1,0:T(8,128)(2,1)S(1)} collective-permute-done((bf16[2,512,128]{2,1,0:T(8,128)(2,1)S(1)}, bf16[2,512,128]{2,1,0:T(8,128)(2,1)S(1)}, u32[]{:S(2)}, u32[]{:S(2)}) %collective-permute-start.2) | collective-permute-done | bytes 262176 | tf_op jit(solution)/shard_map/ppermute | solution.py:304
  17.5 8.9 %collective-permute-done.4.refs_3_ = bf16[2,512,128]{2,1,0:T(8,128)(2,1)S(1)} collective-permute-done((bf16[2,512,128]{2,1,0:T(8,128)(2,1)S(1)}, bf16[2,512,128]{2,1,0:T(8,128)(2,1)S(1)}, u32[]{:S(2)}, u32[]{:S(2)}) %collective-permute-start.4) | collective-permute-done | bytes 262176 | tf_op jit(solution)/shard_map/ppermute | solution.py:304
  26.4 0.7 %partial.3 = (f32[512,128]{1,0:T(8,128)S(1)}, bf16[512,128]{1,0:T(8,128)(2,1)S(1)}) custom-call(bf16[2,512,1024]{2,1,0:T(8,128)(2,1)S(1)} %sigma_blocks.1.both_ref, bf16[2,512,128]{2,1,0:T(8,128)(2,1)S(1)} %get-tuple-element.19.own_ref, bf16[2,512,128]{2,1,0:T(8,128)(2,1)S(1)} %collective-permute-done.1.refs_0_, ...), custom_call_target="tpu_custom_call" | custom-call | tf_op jit(solution)/shard_map/partial/pallas_call | solution.py:238
  27.1 1.3 %collective-permute-start.5 = (bf16[512,128]{1,0:T(8,128)(2,1)S(1)}, bf16[512,128]{1,0:T(8,128)(2,1)S(1)}, u32[]{:S(2)}, u32[]{:S(2)}) collective-permute-start(bf16[512,128]{1,0:T(8,128)(2,1)S(1)} %get-tuple-element.22), channel_id=1, source_target_pairs={{0,3},{4,7},{8,11},{9,10},{12,15},{13,14},{16,18},{17,19},{20,22},... | collective-permute-start | bytes 393224 | tf_op jit(solution)/shard_map/ppermute | solution.py:304
  28.5 4.4 %collective-permute-done.6.refs_1_ = bf16[2,512,128]{2,1,0:T(8,128)(2,1)S(1)} collective-permute-done((bf16[2,512,128]{2,1,0:T(8,128)(2,1)S(1)}, bf16[2,512,128]{2,1,0:T(8,128)(2,1)S(1)}, u32[]{:S(2)}, u32[]{:S(2)}) %collective-permute-start.6) | collective-permute-done | bytes 262176 | tf_op jit(solution)/shard_map/ppermute | solution.py:304
  32.8 0.5 %partial.4.refs_0_ = f32[512,128]{1,0:T(8,128)S(1)} custom-call(bf16[2,512,1024]{2,1,0:T(8,128)(2,1)S(1)} %sigma_blocks.1.both_ref, bf16[2,512,128]{2,1,0:T(8,128)(2,1)S(1)} %get-tuple-element.17.own_ref, bf16[2,512,128]{2,1,0:T(8,128)(2,1)S(1)} %collective-permute-done.refs_0_, bf16[2,512,128]{2,1,0:T(8,128)(2,1)S(1)} %collective-permute-done.6.refs_1_), custom_call_target="tpu_custom_call" | custom-call | tf_op jit(solution)/shard_map/partial/pallas_call | solution.py:238
  33.3 1.2 %collective-permute-done.8.refs_2_ = bf16[2,512,128]{2,1,0:T(8,128)(2,1)S(1)} collective-permute-done((bf16[2,512,128]{2,1,0:T(8,128)(2,1)S(1)}, bf16[2,512,128]{2,1,0:T(8,128)(2,1)S(1)}, u32[]{:S(2)}, u32[]{:S(2)}) %collective-permute-start.8) | collective-permute-done | bytes 262176 | tf_op jit(solution)/shard_map/ppermute | solution.py:304
  34.5 0.5 %partial.5 = (f32[512,128]{1,0:T(8,128)S(1)}, bf16[512,128]{1,0:T(8,128)(2,1)S(1)}) custom-call(bf16[2,512,1024]{2,1,0:T(8,128)(2,1)S(1)} %sigma_blocks.1.both_ref, bf16[2,512,128]{2,1,0:T(8,128)(2,1)S(1)} %get-tuple-element.17.own_ref, f32[512,128]{1,0:T(8,128)S(1)} %partial.4.refs_0_, bf16[2,512,128]{2,1,0:T(8,128)(2,1)S(1)} %collective-permute-done.7.refs_1_, ...), custom_call_target="tpu_custom_call" | custom-call | tf_op jit(solution)/shard_map/partial/pallas_call | solution.py:238
  35.0 1.3 %collective-permute-start.10 = (bf16[512,128]{1,0:T(8,128)(2,1)S(1)}, bf16[512,128]{1,0:T(8,128)(2,1)S(1)}, u32[]{:S(2)}, u32[]{:S(2)}) collective-permute-start(bf16[512,128]{1,0:T(8,128)(2,1)S(1)} %get-tuple-element.27), channel_id=1, source_target_pairs={{0,2},{4,6},{8,10},{9,11},{12,14},{13,15},{16,19},{17,18},{20,23},... | collective-permute-start | bytes 393224 | tf_op jit(solution)/shard_map/ppermute | solution.py:304
  36.3 1.3 %collective-permute-start.9 = (bf16[512,128]{1,0:T(8,128)(2,1)S(1)}, bf16[512,128]{1,0:T(8,128)(2,1)S(1)}, u32[]{:S(2)}, u32[]{:S(2)}) collective-permute-start(bf16[512,128]{1,0:T(8,128)(2,1)S(1)} %get-tuple-element.27), channel_id=1, source_target_pairs={{0,3},{4,7},{8,11},{9,10},{12,15},{13,14},{16,18},{17,19},{20,22},... | collective-permute-start | bytes 393224 | tf_op jit(solution)/shard_map/ppermute | solution.py:304
  37.6 1.3 %collective-permute-start.12 = (bf16[512,128]{1,0:T(8,128)(2,1)S(1)}, bf16[512,128]{1,0:T(8,128)(2,1)S(1)}, u32[]{:S(2)}, u32[]{:S(2)}) collective-permute-start(bf16[512,128]{1,0:T(8,128)(2,1)S(1)} %get-tuple-element.27), channel_id=1, source_target_pairs={{0,1},{4,5},{8,9},{12,13},{16,17},{18,19},{20,21},{22,23},{24,25},... | collective-permute-start | bytes 393224 | tf_op jit(solution)/shard_map/ppermute | solution.py:304
  38.9 0.0 collective-permute-done.5.refs_0_
  38.9 0.1 chunk_sums.2
  39.0 1.3 %collective-permute-start.11 = (bf16[512,128]{1,0:T(8,128)(2,1)S(1)}, bf16[512,128]{1,0:T(8,128)(2,1)S(1)}, u32[]{:S(2)}, u32[]{:S(2)}) collective-permute-start(bf16[512,128]{1,0:T(8,128)(2,1)S(1)} %get-tuple-element.28), channel_id=1, source_target_pairs={{0,1},{2,3},{4,5},{6,7},{8,9},{10,11},{12,13},{14,15},{16,17},{18,... | collective-permute-start | bytes 393224 | tf_op jit(solution)/shard_map/ppermute | solution.py:304
  40.3 0.0 collective-permute-done.9.refs_0_
  40.3 0.5 %collective-permute-done.12.refs_3_ = bf16[512,128]{1,0:T(8,128)(2,1)S(1)} collective-permute-done((bf16[512,128]{1,0:T(8,128)(2,1)S(1)}, bf16[512,128]{1,0:T(8,128)(2,1)S(1)}, u32[]{:S(2)}, u32[]{:S(2)}) %collective-permute-start.12) | collective-permute-done | bytes 131104 | tf_op jit(solution)/shard_map/ppermute | solution.py:304
  40.8 1.4 %collective-permute-done.11.refs_2_ = bf16[512,128]{1,0:T(8,128)(2,1)S(1)} collective-permute-done((bf16[512,128]{1,0:T(8,128)(2,1)S(1)}, bf16[512,128]{1,0:T(8,128)(2,1)S(1)}, u32[]{:S(2)}, u32[]{:S(2)}) %collective-permute-start.11) | collective-permute-done | bytes 131104 | tf_op jit(solution)/shard_map/ppermute | solution.py:304
  42.2 0.8 %accumulate.1 = f32[512,256]{1,0:T(8,128)} custom-call(f32[512,128]{1,0:T(8,128)S(1)} %get-tuple-element.23.refs_0_, f32[512,128]{1,0:T(8,128)S(1)} %chunk_sums.3.refs_1_, bf16[512,128]{1,0:T(8,128)(2,1)S(1)} %collective-permute-done.11.refs_2_, bf16[512,128]{1,0:T(8,128)(2,1)S(1)} %collective-permute-done.12.refs_3_), custom_call_target="tpu_custom_call" | custom-call | tf_op jit(solution)/shard_map/accumulate/pallas_call | solution.py:280
  (2 shorter events, 0.0 us)
Async XLA Ops:
  1.4 2.7 %collective-permute-start.1 = (bf16[2,512,128]{2,1,0:T(8,128)(2,1)S(1)}, bf16[2,512,128]{2,1,0:T(8,128)(2,1)S(1)}, u32[]{:S(2)}, u32[]{:S(2)}) collective-permute-start(bf16[2,512,128]{2,1,0:T(8,128)(2,1)S(1)} %get-tuple-element.19.own_ref), channel_id=1, source_target_pairs={{2,16},{6,20},{10,17},{14,21},{3,0},{7,4},{11,9},{15,13},{1,8},{5,... | collective-permute-start | bytes 786440 | tf_op jit(solution)/shard_map/ppermute | solution.py:304
  2.1 3.4 %collective-permute-start.3 = (bf16[2,512,128]{2,1,0:T(8,128)(2,1)S(1)}, bf16[2,512,128]{2,1,0:T(8,128)(2,1)S(1)}, u32[]{:S(2)}, u32[]{:S(2)}) collective-permute-start(bf16[2,512,128]{2,1,0:T(8,128)(2,1)S(1)} %get-tuple-element.20), channel_id=1, source_target_pairs={{2,20},{6,16},{10,21},{14,17},{3,1},{7,4},{11,8},{15,13},{0,0},{1,... | collective-permute-start | bytes 786440 | tf_op jit(solution)/shard_map/ppermute | solution.py:304
  2.8 6.5 %collective-permute-start = (bf16[2,512,128]{2,1,0:T(8,128)(2,1)S(1)}, bf16[2,512,128]{2,1,0:T(8,128)(2,1)S(1)}, u32[]{:S(2)}, u32[]{:S(2)}) collective-permute-start(bf16[2,512,128]{2,1,0:T(8,128)(2,1)S(1)} %get-tuple-element.17.own_ref), channel_id=1, source_target_pairs={{2,16},{6,20},{10,17},{14,21},{3,0},{7,4},{11,9},{15,13},{1,8},{5,... | collective-permute-start | bytes 786440 | tf_op jit(solution)/shard_map/ppermute | solution.py:304
  3.4 7.1 %collective-permute-start.7 = (bf16[2,512,128]{2,1,0:T(8,128)(2,1)S(1)}, bf16[2,512,128]{2,1,0:T(8,128)(2,1)S(1)}, u32[]{:S(2)}, u32[]{:S(2)}) collective-permute-start(bf16[2,512,128]{2,1,0:T(8,128)(2,1)S(1)} %get-tuple-element.25), channel_id=1, source_target_pairs={{2,20},{6,16},{10,21},{14,17},{3,1},{7,4},{11,8},{15,13},{0,0},{1,... | collective-permute-start | bytes 786440 | tf_op jit(solution)/shard_map/ppermute | solution.py:304
  4.1 13.4 %collective-permute-start.2 = (bf16[2,512,128]{2,1,0:T(8,128)(2,1)S(1)}, bf16[2,512,128]{2,1,0:T(8,128)(2,1)S(1)}, u32[]{:S(2)}, u32[]{:S(2)}) collective-permute-start(bf16[2,512,128]{2,1,0:T(8,128)(2,1)S(1)} %collective-permute-done.1.refs_0_), channel_id=1, source_target_pairs={{0,24},{4,28},{9,25},{13,29}} | collective-permute-start | bytes 786440 | tf_op jit(solution)/shard_map/ppermute | solution.py:304
  5.4 21.0 %collective-permute-start.4 = (bf16[2,512,128]{2,1,0:T(8,128)(2,1)S(1)}, bf16[2,512,128]{2,1,0:T(8,128)(2,1)S(1)}, u32[]{:S(2)}, u32[]{:S(2)}) collective-permute-start(bf16[2,512,128]{2,1,0:T(8,128)(2,1)S(1)} %collective-permute-done.3.refs_2_), channel_id=1, source_target_pairs={{1,28},{4,24},{8,29},{13,25},{0,4},{5,8},{9,13}} | collective-permute-start | bytes 786440 | tf_op jit(solution)/shard_map/ppermute | solution.py:304
  9.2 23.6 %collective-permute-start.6 = (bf16[2,512,128]{2,1,0:T(8,128)(2,1)S(1)}, bf16[2,512,128]{2,1,0:T(8,128)(2,1)S(1)}, u32[]{:S(2)}, u32[]{:S(2)}) collective-permute-start(bf16[2,512,128]{2,1,0:T(8,128)(2,1)S(1)} %collective-permute-done.refs_0_), channel_id=1, source_target_pairs={{0,24},{4,28},{9,25},{13,29}} | collective-permute-start | bytes 786440 | tf_op jit(solution)/shard_map/ppermute | solution.py:304
  10.5 24.0 %collective-permute-start.8 = (bf16[2,512,128]{2,1,0:T(8,128)(2,1)S(1)}, bf16[2,512,128]{2,1,0:T(8,128)(2,1)S(1)}, u32[]{:S(2)}, u32[]{:S(2)}) collective-permute-start(bf16[2,512,128]{2,1,0:T(8,128)(2,1)S(1)} %collective-permute-done.7.refs_1_), channel_id=1, source_target_pairs={{1,28},{4,24},{8,29},{13,25},{0,4},{5,8},{9,13}} | collective-permute-start | bytes 786440 | tf_op jit(solution)/shard_map/ppermute | solution.py:304
  27.1 11.7 %collective-permute-start.5 = (bf16[512,128]{1,0:T(8,128)(2,1)S(1)}, bf16[512,128]{1,0:T(8,128)(2,1)S(1)}, u32[]{:S(2)}, u32[]{:S(2)}) collective-permute-start(bf16[512,128]{1,0:T(8,128)(2,1)S(1)} %get-tuple-element.22), channel_id=1, source_target_pairs={{0,3},{4,7},{8,11},{9,10},{12,15},{13,14},{16,18},{17,19},{20,22},... | collective-permute-start | bytes 393224 | tf_op jit(solution)/shard_map/ppermute | solution.py:304
  35.0 5.3 %collective-permute-start.10 = (bf16[512,128]{1,0:T(8,128)(2,1)S(1)}, bf16[512,128]{1,0:T(8,128)(2,1)S(1)}, u32[]{:S(2)}, u32[]{:S(2)}) collective-permute-start(bf16[512,128]{1,0:T(8,128)(2,1)S(1)} %get-tuple-element.27), channel_id=1, source_target_pairs={{0,2},{4,6},{8,10},{9,11},{12,14},{13,15},{16,19},{17,18},{20,23},... | collective-permute-start | bytes 393224 | tf_op jit(solution)/shard_map/ppermute | solution.py:304
  36.3 4.0 %collective-permute-start.9 = (bf16[512,128]{1,0:T(8,128)(2,1)S(1)}, bf16[512,128]{1,0:T(8,128)(2,1)S(1)}, u32[]{:S(2)}, u32[]{:S(2)}) collective-permute-start(bf16[512,128]{1,0:T(8,128)(2,1)S(1)} %get-tuple-element.27), channel_id=1, source_target_pairs={{0,3},{4,7},{8,11},{9,10},{12,15},{13,14},{16,18},{17,19},{20,22},... | collective-permute-start | bytes 393224 | tf_op jit(solution)/shard_map/ppermute | solution.py:304
  37.6 3.2 %collective-permute-start.12 = (bf16[512,128]{1,0:T(8,128)(2,1)S(1)}, bf16[512,128]{1,0:T(8,128)(2,1)S(1)}, u32[]{:S(2)}, u32[]{:S(2)}) collective-permute-start(bf16[512,128]{1,0:T(8,128)(2,1)S(1)} %get-tuple-element.27), channel_id=1, source_target_pairs={{0,1},{4,5},{8,9},{12,13},{16,17},{18,19},{20,21},{22,23},{24,25},... | collective-permute-start | bytes 393224 | tf_op jit(solution)/shard_map/ppermute | solution.py:304
  39.0 3.2 %collective-permute-start.11 = (bf16[512,128]{1,0:T(8,128)(2,1)S(1)}, bf16[512,128]{1,0:T(8,128)(2,1)S(1)}, u32[]{:S(2)}, u32[]{:S(2)}) collective-permute-start(bf16[512,128]{1,0:T(8,128)(2,1)S(1)} %get-tuple-element.28), channel_id=1, source_target_pairs={{0,1},{2,3},{4,5},{6,7},{8,9},{10,11},{12,13},{14,15},{16,17},{18,... | collective-permute-start | bytes 393224 | tf_op jit(solution)/shard_map/ppermute | solution.py:304
